TPU v7x, 32 devices: a whole 2x2x4 slice. The times are simulated.
32 devices in a mesh: rows: 8 (over z, y), cols: 4 (over x, core).
Axes of the slice: x: 2, y: 2, z: 4, core: 2. Of those that a mesh axis runs over, the one named last changes fastest.
Arguments:
- features: bfloat16 [192, 96, 2048], P('rows', 'cols'), may hold values from -216 to 216
- image_ids: int32 [192, 96], replicated, may hold values from 0 to 35, as said below
- w_point: bfloat16 [2048, 256], replicated, may hold values from -0.125 to 0.125
- w_atrous: bfloat16 [3, 9, 2048, 256], replicated, may hold values from -0.046875 to 0.046875
- w_pool: bfloat16 [2048, 256], replicated, may hold values from -0.125 to 0.125
- w_proj: bfloat16 [1280, 256], replicated, may hold values from -0.15625 to 0.15625
- norm_gain: float32 [6, 256], replicated, may hold values from 0.5 to 1.5
- norm_shift: float32 [6, 256], replicated, may hold values from -3 to 3
- cotangent: bfloat16 [192, 96, 256], P('rows', 'cols'), may hold values from -6 to 6
Outputs:
- output: bfloat16 [192, 96, 256], P('rows', 'cols')
- grad_features: bfloat16 [192, 96, 2048], P('rows', 'cols')
- grad_point: float32 [2048, 256], P('rows')
- grad_atrous: float32 [3, 9, 2048, 256], P(None, None, 'rows')
- grad_pool: float32 [2048, 256], P('rows')
- grad_proj: float32 [1280, 256], P('rows')
- grad_gain: float32 [6, 256], replicated
- grad_shift: float32 [6, 256], replicated
Inputs may be any that keep to these rules, and one draw needn't show every extreme that they name: `image_ids`: the images are rectangles that tile the grid: vertical bands, each cut across into 12 rectangles, numbered band by band from the left and top to bottom inside a band; every number occurs.
All inputs are finite; a program needn't handle non-finite values.
Results may differ from a plain program's by a relative error of at most 0.017.
Values may be sent and summed in bfloat16 or wider, within the bound.
A program may use at most 384 MiB of HBM per device.

v0:
```python
import jax
import jax.numpy as jnp
from jax import lax
from jax.sharding import PartitionSpec as P

RATE_LOW = 6
RATE_MID = 12
RATE_TOP = 18


epsilon = 1e-05


def extended(cells, sides, width):
    for axis, dim in sides:
        count = lax.axis_size(axis)
        ends = count - 1
        head = lax.slice_in_dim(cells, 0, width, axis=dim)
        tail = lax.slice_in_dim(cells, cells.shape[dim] - width, cells.shape[dim], axis=dim)
        cells = jnp.concatenate(
            [
                lax.ppermute(tail, axis, [(i, (i + 1) % count) for i in range(ends)]),
                cells,
                lax.ppermute(head, axis, [((i + 1) % count, i) for i in range(ends)]),
            ],
            axis=dim,
        )
    return cells


def image_match(window, own_ids, row_start, col_start):
    rows_here, cols_here = own_ids.shape
    section = window[row_start : row_start + rows_here, col_start : col_start + cols_here]
    return (section == own_ids).astype(jnp.float32).reshape(rows_here * cols_here, 1)


def silu_slope(preact_in):
    sigma = jax.nn.sigmoid(preact_in)
    return sigma * (1.0 + preact_in * (1.0 - sigma))


def transposed(left, right):
    return lax.dot_general(
        left, right, (((1,), (1,)), ((), ())), preferred_element_type=jnp.float32
    )


def shards(
    features, image_ids, w_point, w_atrous, w_pool, w_proj, norm_gain, norm_shift, cotangent
):
    rows_here, cols_here, channels = features.shape
    branch_width = w_point.shape[1]
    pixels = rows_here * cols_here
    grid_rows, grid_cols = image_ids.shape
    total_pixels = float(grid_rows * grid_cols)
    image_count = grid_rows // 16 * (grid_cols // 32)
    dilations = (RATE_LOW, RATE_MID, RATE_TOP)
    margin = RATE_TOP
    row_index = lax.axis_index("rows")
    col_index = lax.axis_index("cols")
    id_padded = jnp.pad(image_ids, margin, constant_values=-1)
    window = lax.dynamic_slice(
        id_padded,
        (row_index * rows_here, col_index * cols_here),
        (rows_here + 2 * margin, cols_here + 2 * margin),
    )
    own_ids = window[margin : margin + rows_here, margin : margin + cols_here]
    own_flat = own_ids.reshape(pixels)
    flattened = features.reshape(pixels, channels)
    padded = extended(features, (("rows", 0), ("cols", 1)), margin)
    one_hot = (own_flat[:, None] == jnp.arange(image_count, dtype=jnp.int32)[None, :]).astype(
        jnp.bfloat16
    )
    local_sums = jnp.einsum("pn,pc->nc", one_hot, flattened, preferred_element_type=jnp.float32)
    counts = jax.ops.segment_sum(
        jnp.ones((grid_rows * grid_cols,), jnp.float32), image_ids.reshape(-1), image_count
    )
    image_totals = lax.psum(local_sums, ("rows", "cols"))
    branch_outs = [jnp.dot(flattened, w_point, preferred_element_type=jnp.float32)]
    for branch, dilation in enumerate(dilations):
        running = jnp.zeros((pixels, branch_width), jnp.float32)
        for stencil in range(9):
            row_shift = (stencil // 3 - 1) * dilation
            col_shift = (stencil % 3 - 1) * dilation
            source = padded[
                margin + row_shift : margin + row_shift + rows_here,
                margin + col_shift : margin + col_shift + cols_here,
            ].reshape(pixels, channels)
            same_image = image_match(window, own_ids, margin + row_shift, margin + col_shift)
            running = running + same_image * jnp.dot(
                source, w_atrous[branch, stencil], preferred_element_type=jnp.float32
            )
        branch_outs.append(running)
    spatial = jnp.stack(branch_outs, axis=1)
    first_sum = jnp.sum(spatial, axis=0)
    second_sum = jnp.sum(spatial * spatial, axis=0)
    first_sum, second_sum = lax.psum((first_sum, second_sum), ("rows", "cols"))
    average = first_sum / total_pixels
    inverse_std = lax.rsqrt(second_sum / total_pixels - average * average + epsilon)
    normed = (spatial - average) * inverse_std
    preact = norm_gain[:4] * normed + norm_shift[:4]
    active = jax.nn.silu(preact).astype(jnp.bfloat16)
    pooled = (image_totals / counts[:, None]).astype(jnp.bfloat16)
    pool_z = jnp.dot(pooled, w_pool, preferred_element_type=jnp.float32)
    pool_avg = jnp.mean(pool_z, axis=0)
    pool_square = jnp.mean(pool_z * pool_z, axis=0)
    pool_inverse = lax.rsqrt(pool_square - pool_avg * pool_avg + epsilon)
    pool_normed = (pool_z - pool_avg) * pool_inverse
    pool_pre = norm_gain[4] * pool_normed + norm_shift[4]
    pool_active = jax.nn.silu(pool_pre).astype(jnp.bfloat16)
    joined = jnp.concatenate(
        [active.reshape(pixels, 4 * branch_width), jnp.take(pool_active, own_flat, axis=0)], axis=1
    )
    final_z = jnp.dot(joined, w_proj, preferred_element_type=jnp.float32)
    final_first, final_second = lax.psum(
        (jnp.sum(final_z, axis=0), jnp.sum(final_z * final_z, axis=0)), ("rows", "cols")
    )
    final_avg = final_first / total_pixels
    final_inverse = lax.rsqrt(final_second / total_pixels - final_avg * final_avg + epsilon)
    final_normed = (final_z - final_avg) * final_inverse
    final_pre = norm_gain[5] * final_normed + norm_shift[5]
    output = jax.nn.silu(final_pre).astype(jnp.bfloat16).reshape(rows_here, cols_here, branch_width)
    upstream = cotangent.reshape(pixels, branch_width).astype(jnp.float32)
    grad_final = upstream * silu_slope(final_pre)
    shift_last, gain_last = lax.psum(
        (jnp.sum(grad_final, axis=0), jnp.sum(grad_final * final_normed, axis=0)), ("rows", "cols")
    )
    grad_final_z = (
        final_inverse
        * (
            grad_final * norm_gain[5]
            - norm_gain[5] * shift_last / total_pixels
            - final_normed * (norm_gain[5] * gain_last / total_pixels)
        )
    ).astype(jnp.bfloat16)
    proj_term = jnp.einsum("pk,pc->kc", joined, grad_final_z, preferred_element_type=jnp.float32)
    grad_joined = transposed(grad_final_z, w_proj)
    grad_pre = grad_joined[:, : 4 * branch_width].reshape(pixels, 4, branch_width) * silu_slope(
        preact
    )
    grad_pixel = grad_joined[:, 4 * branch_width :]
    shift_sums = jnp.sum(grad_pre, axis=0)
    gain_sums = jnp.sum(grad_pre * normed, axis=0)
    image_grads = jax.ops.segment_sum(grad_pixel, own_flat, image_count)
    shift_sums, gain_sums, image_grads = lax.psum(
        (shift_sums, gain_sums, image_grads), ("rows", "cols")
    )
    grad_branch = (
        inverse_std
        * (
            grad_pre * norm_gain[:4]
            - norm_gain[:4] * shift_sums / total_pixels
            - normed * (norm_gain[:4] * gain_sums / total_pixels)
        )
    ).astype(jnp.bfloat16)
    grad_pool_pre = image_grads * silu_slope(pool_pre)
    pool_shift = jnp.sum(grad_pool_pre, axis=0)
    pool_gain = jnp.sum(grad_pool_pre * pool_normed, axis=0)
    grad_pool_z = (
        pool_inverse
        * (
            grad_pool_pre * norm_gain[4]
            - norm_gain[4] * pool_shift / image_count
            - pool_normed * (norm_gain[4] * pool_gain / image_count)
        )
    ).astype(jnp.bfloat16)
    row_share = channels // lax.axis_size("rows")
    pool_columns = lax.dynamic_slice_in_dim(pooled, row_index * row_share, row_share, 1)
    grad_pool = jnp.einsum(
        "nk,nc->kc", pool_columns, grad_pool_z, preferred_element_type=jnp.float32
    )
    grad_pooled = transposed(grad_pool_z, w_pool) / counts[:, None]
    grad_input = jnp.take(grad_pooled, own_flat, axis=0) + transposed(grad_branch[:, 0], w_point)
    point_term = jnp.einsum(
        "pk,pc->kc", flattened, grad_branch[:, 0], preferred_element_type=jnp.float32
    )
    stacked = grad_branch[:, 1:].reshape(rows_here, cols_here, 3 * branch_width)
    grad_padded = extended(stacked, (("rows", 0), ("cols", 1)), margin)
    rim_list = [
        grad_padded[:, :, branch * branch_width : (branch + 1) * branch_width]
        for branch in range(3)
    ]
    rim_bases = [margin, margin, margin]
    atrous_terms = []
    for branch, dilation in enumerate(dilations):
        tap_terms = []
        rim_base = rim_bases[branch]
        for stencil in range(9):
            row_shift = (stencil // 3 - 1) * dilation
            col_shift = (stencil % 3 - 1) * dilation
            source = padded[
                margin + row_shift : margin + row_shift + rows_here,
                margin + col_shift : margin + col_shift + cols_here,
            ].reshape(pixels, channels)
            same_image = image_match(window, own_ids, margin + row_shift, margin + col_shift)
            masked = same_image.astype(jnp.bfloat16) * grad_branch[:, branch + 1]
            tap_terms.append(
                jnp.einsum("pk,pc->kc", source, masked, preferred_element_type=jnp.float32)
            )
            incoming = rim_list[branch][
                rim_base - row_shift : rim_base - row_shift + rows_here,
                rim_base - col_shift : rim_base - col_shift + cols_here,
            ].reshape(pixels, branch_width)
            back_image = image_match(window, own_ids, margin - row_shift, margin - col_shift)
            grad_input = grad_input + back_image * transposed(incoming, w_atrous[branch, stencil])
        atrous_terms.append(jnp.stack(tap_terms))
    atrous_term = jnp.stack(atrous_terms)
    shared = (
        lax.psum_scatter(
            point_term.astype(jnp.bfloat16), "rows", scatter_dimension=0, tiled=True
        ).astype(jnp.float32),
        lax.psum_scatter(
            atrous_term.astype(jnp.bfloat16), "rows", scatter_dimension=2, tiled=True
        ).astype(jnp.float32),
        lax.psum_scatter(
            proj_term.astype(jnp.bfloat16), "rows", scatter_dimension=0, tiled=True
        ).astype(jnp.float32),
    )
    shared = (
        lax.psum(shared[0].astype(jnp.bfloat16), "cols").astype(jnp.float32),
        lax.psum(shared[1].astype(jnp.bfloat16), "cols").astype(jnp.float32),
        lax.psum(shared[2].astype(jnp.bfloat16), "cols").astype(jnp.float32),
    )
    grad_gain = jnp.concatenate([gain_sums, pool_gain[None], gain_last[None]], axis=0)
    grad_shift = jnp.concatenate([shift_sums, pool_shift[None], shift_last[None]], axis=0)
    grad_features = grad_input.astype(jnp.bfloat16).reshape(rows_here, cols_here, channels)
    return (
        output,
        grad_features,
        shared[0],
        shared[1],
        grad_pool,
        shared[2],
        grad_gain,
        grad_shift,
    )


def solution(mesh):
    placed = (P("rows", "cols", None), P(), P(), P(), P(), P(), P(), P(), P("rows", "cols", None))
    return jax.shard_map(
        shards,
        mesh=mesh,
        in_specs=placed,
        out_specs=(
            P("rows", "cols", None),
            P("rows", "cols", None),
            P("rows", None),
            P(None, None, "rows", None),
            P("rows", None),
            P("rows", None),
            P(),
            P(),
        ),
        check_vma=False,
    )
```

profile of v0, /device:TPU:0, one launch (start us, length us, event | category | flops | bytes accessed | tf_op | source)
XLA Modules:
  0.0 1252.5 jit_solution(10970161068335618437)
XLA Ops:
  7.2 4.4 fusion.410
  11.7 6.1 collective-permute-start
  59.2 127.7 %scatter_custom_fusion = f32[36]{0:T(128)S(1)} fusion(s32[18432]{0:T(1024)} %reshape.868, f32[18432]{0:T(1024)} %broadcast.233, f32[]{:T(128)} %constant.79.clone.1), kind=kCustom, calls=%fused_computation.597 | custom fusion | flops 18432 | bytes 656 | tf_op jit(solution)/shard_map/scatter-add | solution.py:75
  194.9 3.3 constant_dynamic-update-slice_fusion.5
  200.2 5.1 fusion.407
  205.2 4.6 copy.48
  209.8 3.8 collective-permute-start.2
  217.6 3.2 gather_fusion
  222.7 7.5 copy.50
  232.2 3.8 convolution_multiply_fusion.22
  248.7 3.0 convolution_multiply_fusion.1
  251.7 5.0 copy.49
  256.8 9.8 fusion.64
  266.6 3.6 convolution_multiply_fusion.20
  270.2 4.9 copy.51
  275.1 9.5 fusion.57
  284.7 5.2 convolution_multiply_fusion.21
  333.3 55.2 %all-reduce.4 = (f32[4,256]{1,0:T(4,128)S(1)}, f32[4,256]{1,0:T(4,128)S(1)}) all-reduce(f32[4,256]{1,0:T(4,128)S(1)} %get-tuple-element.43, f32[4,256]{1,0:T(4,128)S(1)} %get-tuple-element.42), channel_id=1, replica_groups=mesh['rows'=8,'cols'=4] {'rows','cols'}, use_global_device_ids=true, to_apply=%region_3.4 | all-reduce | flops 2048 | bytes 16384 | tf_op jit(solution)/shard_map/psum | solution.py:97
  393.8 40.3 %all-reduce.3 = (f32[256]{0:T(256)S(1)}, f32[256]{0:T(256)S(1)}) all-reduce(f32[256]{0:T(256)S(1)} %get-tuple-element.47, f32[256]{0:T(256)S(1)} %get-tuple-element.46), channel_id=1, replica_groups=mesh['rows'=8,'cols'=4] {'rows','cols'}, use_global_device_ids=true, to_apply=%region_11.12 | all-reduce | flops 512 | bytes 4096 | tf_op jit(solution)/shard_map/psum | solution.py:115
  435.6 39.7 %all-reduce.2 = (f32[256]{0:T(256)S(1)}, f32[256]{0:T(256)S(1)}) all-reduce(f32[256]{0:T(256)S(1)} %get-tuple-element.45, f32[256]{0:T(256)S(1)} %get-tuple-element.44), channel_id=1, replica_groups=mesh['rows'=8,'cols'=4] {'rows','cols'}, use_global_device_ids=true, to_apply=%region_15.16 | all-reduce | flops 512 | bytes 4096 | tf_op jit(solution)/shard_map/psum | solution.py:125
  481.7 3.2 multiply_multiply_fusion
  484.9 7.3 scatter_custom_fusion.1
  492.2 3.0 convolution_convert_fusion.28
  498.2 40.8 %all-reduce.1 = (f32[4,256]{1,0:T(4,128)S(1)}, f32[4,256]{1,0:T(4,128)S(1)}, f32[36,256]{1,0:T(8,128)S(1)}) all-reduce(f32[4,256]{1,0:T(4,128)S(1)} %reduce_sum.131, f32[4,256]{1,0:T(4,128)S(1)} %reduce_sum.129, f32[36,256]{1,0:T(8,128)S(1)} %scatter_custom_fusion.1), channel_id=1, replica_groups=mesh['rows'=8,'cols'=4] {'rows','cols'}, use_global_device_ids=true, to_apply=%region_23.24 | all-reduce | flops 11264 | bytes 90112 | tf_op jit(solution)/shard_map/psum | solution.py:145
  539.1 3.5 fusion.75
  570.4 4.0 fusion.12
  605.6 3.9 fusion.54
  609.4 19.8 %pad_maximum_fusion = bf16[3,9,2048,256]{3,2,1,0:T(8,128)(2,1)} fusion(bf16[1,9,2048,256]{3,2,1,0:T(8,128)(2,1)} %bitcast.155, bf16[1,9,2048,256]{3,2,1,0:T(8,128)(2,1)} %bitcast.135, bf16[1,9,2048,256]{3,2,1,0:T(8,128)(2,1)} %bitcast.573), kind=kLoop, calls=%fused_computation.4 | loop fusion | flops 28311552 | bytes 56623104 | tf_op jit(solution)/shard_map/stack | solution.py:207
  631.6 3.1 slice.702
  634.7 5.0 collective-permute-start.4
  646.7 3.1 slice.705
  656.6 4.1 fusion.111
  660.7 4.2 fusion.138
  665.5 4.4 gather_fusion.1
  671.6 4.3 fusion.165
  683.8 4.4 fusion.120
  688.1 4.4 fusion.147
  709.3 3.1 fusion.108
  712.4 3.3 fusion.117
  721.6 3.2 fusion.144
  724.8 3.0 fusion.153
  730.8 3.0 fusion.171
  739.7 3.0 fusion.123
  742.8 3.1 fusion.132
  760.9 397.1 %reduce-scatter.6.cloned.1.call-done = bf16[3,9,256,256]{3,2,1,0:T(8,128)(2,1)} async-done(((bf16[3,9,2048,256]{3,2,1,0:T(8,128)(2,1)}), bf16[3,9,256,256]{3,2,1,0:T(8,128)(2,1)}) %reduce-scatter.6.cloned.1.call-update) | async-done | bytes 3538960 | tf_op jit(solution)/shard_map/reduce_scatter | solution.py:212
  1158.2 44.6 %add_convert_fusion = bf16[576,2048]{1,0:T(8,128)(2,1)} fusion(f32[576,2048]{1,0:T(8,128)} %fusion.102, f32[576,2048]{1,0:T(8,128)} %fusion.105, f32[576,2048]{1,0:T(8,128)} %fusion.108, f32[576,2048]{1,0:T(8,128)} %fusion.111, f32[576,2048]{1,0:T(8,128)} %fusion.114, f32[576,2048]{1,0:T(8,128)} %fusion.117, f32[576,2048]{1,0:T(8,128)} %fusion.120, ...), kind=kOutput, calls=%fused_computation.37 | convolution fusion | flops 667680768 | bytes 135879232 | tf_op jit(solution)/shard_map/dot_general | solution.py:43
  1202.8 35.5 %all-reduce.11.cloned.1.call-done = (bf16[256,256]{0,1:T(8,128)(2,1)}, bf16[3,9,256,256]{3,2,1,0:T(8,128)(2,1)}, bf16[160,256]{1,0:T(8,128)(2,1)}) async-done(((bf16[256,256]{0,1:T(8,128)(2,1)}, bf16[3,9,256,256]{3,2,1,0:T(8,128)(2,1)}, bf16[160,256]{1,0:T(8,128)(2,1)}), (bf16[256,256]{0,1:T(8,128)(2,1)}, bf16[3,9,256,256]{3,2,1,0:T(8,128)(2,1)}, bf16[160,256]{1,0:T(8,128)(2,1)})) %all-reduce.11.cloned.1.call-update) | async-done | bytes 3751952 | tf_op jit(solution)/shard_map/psum | solution.py:220
  1238.3 5.9 convert_element_type.378
  (566 shorter events, 262.9 us)
Async XLA Ops:
  7.2 206.4 %all-reduce.9.cloned.1.call-start = ((), (), s32[]{:S(2)}) async-start(), calls=%async_computation.3 | async-start | bytes 655360 | tf_op jit(solution)/shard_map/psum | solution.py:78
  11.7 180.3 %collective-permute-start = (bf16[18,24,2048]{2,1,0:T(8,128)(2,1)}, bf16[18,24,2048]{2,1,0:T(8,128)(2,1)}, u32[]{:S(2)}, u32[]{:S(2)}) collective-permute-start(bf16[18,24,2048]{2,1,0:T(8,128)(2,1)} %get-tuple-element.118), channel_id=1, source_target_pairs={{0,4},{4,8},{8,12},{12,16},{16,20},{20,24},{24,28},{1,5},{5,9},{9,... | collective-permute-start | bytes 5308424 | tf_op jit(solution)/shard_map/ppermute | solution.py:22
  17.8 177.1 %collective-permute-start.1 = (bf16[18,24,2048]{2,1,0:T(8,128)(2,1)}, bf16[18,24,2048]{2,1,0:T(8,128)(2,1)}, u32[]{:S(2)}, u32[]{:S(2)}) collective-permute-start(bf16[18,24,2048]{2,1,0:T(8,128)(2,1)} %get-tuple-element.117), channel_id=1, source_target_pairs={{4,0},{8,4},{12,8},{16,12},{20,16},{24,20},{28,24},{5,1},{9,5},{13... | collective-permute-start | bytes 5308424 | tf_op jit(solution)/shard_map/ppermute | solution.py:24
  21.3 739.5 %reduce-scatter.8.cloned.1.call-start = ((), (), s32[]{:S(2)}) async-start(), calls=%async_computation.6 | async-start | bytes 737280 | tf_op jit(solution)/shard_map/reduce_scatter | solution.py:215
  28.6 296.1 %copy-start.80 = (f32[576]{0:T(1024)}, f32[576]{0:T(1024)S(1)}, u32[]{:S(2)}) copy-start(f32[576]{0:T(1024)S(1)} %reshape.829) | copy-start | bytes 6916
  33.4 276.2 %copy-start.114 = (f32[576]{0:T(1024)}, f32[576]{0:T(1024)S(1)}, u32[]{:S(2)}) copy-start(f32[576]{0:T(1024)S(1)} %reshape.840) | copy-start | bytes 6916
  35.0 292.0 %copy-start.84 = (f32[576]{0:T(1024)}, f32[576]{0:T(1024)S(1)}, u32[]{:S(2)}) copy-start(f32[576]{0:T(1024)S(1)} %reshape.837) | copy-start | bytes 6916
  35.8 276.0 %copy-start.118 = (f32[576]{0:T(1024)}, f32[576]{0:T(1024)S(1)}, u32[]{:S(2)}) copy-start(f32[576]{0:T(1024)S(1)} %reshape.844) | copy-start | bytes 6916
  36.6 277.4 %copy-start.120 = (f32[576]{0:T(1024)}, f32[576]{0:T(1024)S(1)}, u32[]{:S(2)}) copy-start(f32[576]{0:T(1024)S(1)} %reshape.843) | copy-start | bytes 6916
  38.2 278.0 %copy-start.86 = (f32[576]{0:T(1024)}, f32[576]{0:T(1024)S(1)}, u32[]{:S(2)}) copy-start(f32[576]{0:T(1024)S(1)} %reshape.841) | copy-start | bytes 6916
  39.0 281.4 %copy-start.124 = (f32[576]{0:T(1024)}, f32[576]{0:T(1024)S(1)}, u32[]{:S(2)}) copy-start(f32[576]{0:T(1024)S(1)} %reshape.846) | copy-start | bytes 6916
  39.8 282.8 %copy-start.126 = (f32[576]{0:T(1024)}, f32[576]{0:T(1024)S(1)}, u32[]{:S(2)}) copy-start(f32[576]{0:T(1024)S(1)} %reshape.848) | copy-start | bytes 6916
  41.4 287.9 %copy-start.88 = (f32[576]{0:T(1024)}, f32[576]{0:T(1024)S(1)}, u32[]{:S(2)}) copy-start(f32[576]{0:T(1024)S(1)} %reshape.845) | copy-start | bytes 6916
  209.8 41.9 %collective-permute-start.2 = (bf16[60,18,2048]{2,0,1:T(8,128)(2,1)}, bf16[60,18,2048]{2,0,1:T(8,128)(2,1)}, u32[]{:S(2)}, u32[]{:S(2)}) collective-permute-start(bf16[60,18,2048]{2,0,1:T(8,128)(2,1)} %copy.48), channel_id=1, source_target_pairs={{0,1},{1,2},{2,3},{4,5},{5,6},{6,7},{8,9},{9,10},{10,11},{12,13},{... | collective-permute-start | bytes 13271048 | tf_op jit(solution)/shard_map/ppermute | solution.py:22
  230.2 40.0 %collective-permute-start.3 = (bf16[60,18,2048]{2,0,1:T(8,128)(2,1)}, bf16[60,18,2048]{2,0,1:T(8,128)(2,1)}, u32[]{:S(2)}, u32[]{:S(2)}) collective-permute-start(bf16[60,18,2048]{2,0,1:T(8,128)(2,1)} %copy.50), channel_id=1, source_target_pairs={{1,0},{2,1},{3,2},{5,4},{6,5},{7,6},{9,8},{10,9},{11,10},{13,12},{... | collective-permute-start | bytes 13271048 | tf_op jit(solution)/shard_map/ppermute | solution.py:24
  570.3 190.6 %reduce-scatter.4.cloned.1.call-start = ((), (), s32[]{:S(2)}) async-start(), calls=%async_computation.4 | async-start | bytes 1179648 | tf_op jit(solution)/shard_map/reduce_scatter | solution.py:209
  605.5 552.4 %reduce-scatter.6.cloned.1.call-start = ((), (), s32[]{:S(2)}) async-start(), calls=%async_computation.5 | async-start | bytes 31850496 | tf_op jit(solution)/shard_map/reduce_scatter | solution.py:212
  629.2 609.1 %all-reduce.11.cloned.1.call-start = ((), (), s32[]{:S(2)}) async-start(), calls=%async_computation.7 | async-start | bytes 7503872 | tf_op jit(solution)/shard_map/psum | solution.py:220
  634.7 41.2 %collective-permute-start.4 = (bf16[18,24,768]{2,1,0:T(8,128)(2,1)}, bf16[18,24,768]{2,1,0:T(8,128)(2,1)}, u32[]{:S(2)}, u32[]{:S(2)}) collective-permute-start(bf16[18,24,768]{2,1,0:T(8,128)(2,1)} %slice.702), channel_id=1, source_target_pairs={{0,4},{4,8},{8,12},{12,16},{16,20},{20,24},{24,28},{1,5},{5,9},{9,... | collective-permute-start | bytes 1990664 | tf_op jit(solution)/shard_map/ppermute | solution.py:22
  649.8 27.5 %collective-permute-start.5 = (bf16[18,24,768]{2,1,0:T(8,128)(2,1)}, bf16[18,24,768]{2,1,0:T(8,128)(2,1)}, u32[]{:S(2)}, u32[]{:S(2)}) collective-permute-start(bf16[18,24,768]{2,1,0:T(8,128)(2,1)} %slice.705), channel_id=1, source_target_pairs={{4,0},{8,4},{12,8},{16,12},{20,16},{24,20},{28,24},{5,1},{9,5},{13... | collective-permute-start | bytes 1990664 | tf_op jit(solution)/shard_map/ppermute | solution.py:24
  680.2 24.3 %collective-permute-start.7 = (bf16[60,18,768]{2,0,1:T(8,128)(2,1)S(1)}, bf16[60,18,768]{2,0,1:T(8,128)(2,1)S(1)}, u32[]{:S(2)}, u32[]{:S(2)}) collective-permute-start(bf16[60,18,768]{2,0,1:T(8,128)(2,1)S(1)} %copy.59), channel_id=1, source_target_pairs={{0,1},{1,2},{2,3},{4,5},{5,6},{6,7},{8,9},{9,10},{10,11},{12,13},{... | collective-permute-start | bytes 4976648 | tf_op jit(solution)/shard_map/ppermute | solution.py:22
  681.9 23.5 %collective-permute-start.6 = (bf16[60,18,768]{2,0,1:T(8,128)(2,1)S(1)}, bf16[60,18,768]{2,0,1:T(8,128)(2,1)S(1)}, u32[]{:S(2)}, u32[]{:S(2)}) collective-permute-start(bf16[60,18,768]{2,0,1:T(8,128)(2,1)S(1)} %copy.57), channel_id=1, source_target_pairs={{1,0},{2,1},{3,2},{5,4},{6,5},{7,6},{9,8},{10,9},{11,10},{13,12},{... | collective-permute-start | bytes 4976648 | tf_op jit(solution)/shard_map/ppermute | solution.py:24
  760.6 397.4 %copy-start.70 = (bf16[24,24,256]{2,1,0:T(8,128)(2,1)S(1)}, bf16[24,24,256]{2,1,0:T(8,128)(2,1)}, u32[]{:S(2)}) copy-start(bf16[24,24,256]{2,1,0:T(8,128)(2,1)} %get-tuple-element.87) | copy-start | bytes 884740
  760.6 397.4 %copy-start.79 = (f32[576]{0:T(1024)S(1)}, f32[576]{0:T(1024)}, u32[]{:S(2)}) copy-start(f32[576]{0:T(1024)} %copy-done.78) | copy-start | bytes 6916
  760.6 397.4 %copy-start.81 = (f32[576]{0:T(1024)S(1)}, f32[576]{0:T(1024)}, u32[]{:S(2)}) copy-start(f32[576]{0:T(1024)} %copy-done.80) | copy-start | bytes 6916
  760.6 397.4 %copy-start.83 = (f32[576]{0:T(1024)S(1)}, f32[576]{0:T(1024)}, u32[]{:S(2)}) copy-start(f32[576]{0:T(1024)} %copy-done.82) | copy-start | bytes 6916
  760.6 397.4 %copy-start.85 = (f32[576]{0:T(1024)S(1)}, f32[576]{0:T(1024)}, u32[]{:S(2)}) copy-start(f32[576]{0:T(1024)} %copy-done.84) | copy-start | bytes 6916
  760.6 397.4 %copy-start.87 = (f32[576]{0:T(1024)S(1)}, f32[576]{0:T(1024)}, u32[]{:S(2)}) copy-start(f32[576]{0:T(1024)} %copy-done.86) | copy-start | bytes 6916
  760.6 397.4 %copy-start.89 = (f32[576]{0:T(1024)S(1)}, f32[576]{0:T(1024)}, u32[]{:S(2)}) copy-start(f32[576]{0:T(1024)} %copy-done.88) | copy-start | bytes 6916
  760.6 397.4 %copy-start.95 = (f32[576]{0:T(1024)S(1)}, f32[576]{0:T(1024)}, u32[]{:S(2)}) copy-start(f32[576]{0:T(1024)} %copy-done.94) | copy-start | bytes 6916
  760.6 397.4 %copy-start.97 = (f32[576]{0:T(1024)S(1)}, f32[576]{0:T(1024)}, u32[]{:S(2)}) copy-start(f32[576]{0:T(1024)} %reshape.826) | copy-start | bytes 6916
  760.6 397.4 %copy-start.99 = (f32[576]{0:T(1024)S(1)}, f32[576]{0:T(1024)}, u32[]{:S(2)}) copy-start(f32[576]{0:T(1024)} %copy-done.98) | copy-start | bytes 6916
  760.6 397.4 %copy-start.101 = (f32[576]{0:T(1024)S(1)}, f32[576]{0:T(1024)}, u32[]{:S(2)}) copy-start(f32[576]{0:T(1024)} %copy-done.100) | copy-start | bytes 6916
  760.7 397.4 %copy-start.103 = (f32[576]{0:T(1024)S(1)}, f32[576]{0:T(1024)}, u32[]{:S(2)}) copy-start(f32[576]{0:T(1024)} %copy-done.102) | copy-start | bytes 6916
  760.7 397.4 %copy-start.105 = (f32[576]{0:T(1024)S(1)}, f32[576]{0:T(1024)}, u32[]{:S(2)}) copy-start(f32[576]{0:T(1024)} %copy-done.104) | copy-start | bytes 6916
  760.7 397.4 %copy-start.107 = (f32[576]{0:T(1024)S(1)}, f32[576]{0:T(1024)}, u32[]{:S(2)}) copy-start(f32[576]{0:T(1024)} %copy-done.106) | copy-start | bytes 6916
  760.7 397.4 %copy-start.109 = (f32[576]{0:T(1024)S(1)}, f32[576]{0:T(1024)}, u32[]{:S(2)}) copy-start(f32[576]{0:T(1024)} %copy-done.108) | copy-start | bytes 6916
  760.7 397.4 %copy-start.111 = (f32[576]{0:T(1024)S(1)}, f32[576]{0:T(1024)}, u32[]{:S(2)}) copy-start(f32[576]{0:T(1024)} %copy-done.110) | copy-start | bytes 6916
  760.7 397.4 %copy-start.113 = (f32[576]{0:T(1024)S(1)}, f32[576]{0:T(1024)}, u32[]{:S(2)}) copy-start(f32[576]{0:T(1024)} %copy-done.112) | copy-start | bytes 6916
  760.7 397.4 %copy-start.115 = (f32[576]{0:T(1024)S(1)}, f32[576]{0:T(1024)}, u32[]{:S(2)}) copy-start(f32[576]{0:T(1024)} %copy-done.114) | copy-start | bytes 6916
  760.7 397.4 %copy-start.117 = (f32[576]{0:T(1024)S(1)}, f32[576]{0:T(1024)}, u32[]{:S(2)}) copy-start(f32[576]{0:T(1024)} %copy-done.116) | copy-start | bytes 6916
  760.7 397.4 %copy-start.119 = (f32[576]{0:T(1024)S(1)}, f32[576]{0:T(1024)}, u32[]{:S(2)}) copy-start(f32[576]{0:T(1024)} %copy-done.118) | copy-start | bytes 6916
  760.7 397.4 %copy-start.121 = (f32[576]{0:T(1024)S(1)}, f32[576]{0:T(1024)}, u32[]{:S(2)}) copy-start(f32[576]{0:T(1024)} %copy-done.120) | copy-start | bytes 6916
  760.8 397.4 %copy-start.123 = (f32[576]{0:T(1024)S(1)}, f32[576]{0:T(1024)}, u32[]{:S(2)}) copy-start(f32[576]{0:T(1024)} %copy-done.122) | copy-start | bytes 6916
  760.8 397.4 %copy-start.125 = (f32[576]{0:T(1024)S(1)}, f32[576]{0:T(1024)}, u32[]{:S(2)}) copy-start(f32[576]{0:T(1024)} %copy-done.124) | copy-start | bytes 6916
  760.8 397.4 %copy-start.127 = (f32[576]{0:T(1024)S(1)}, f32[576]{0:T(1024)}, u32[]{:S(2)}) copy-start(f32[576]{0:T(1024)} %copy-done.126) | copy-start | bytes 6916
  760.8 397.4 %copy-start.129 = (f32[576]{0:T(1024)S(1)}, f32[576]{0:T(1024)}, u32[]{:S(2)}) copy-start(f32[576]{0:T(1024)} %copy-done.128) | copy-start | bytes 6916
  760.8 397.4 %copy-start.141 = (pred[576]{0:T(1024)(128)(4,1)S(1)}, pred[576]{0:T(1024)(128)(4,1)}, u32[]{:S(2)}) copy-start(pred[576]{0:T(1024)(128)(4,1)} %compare_and_fusion) | copy-start | bytes 1732
  (143 other events, 4534.1 us)
Sparse Core Ops, SparseCore 0:
  21.4 152.9 all-reduce.8
  570.4 63.0 reduce-scatter.7
  636.8 67.4 reduce-scatter.3
  708.7 449.1 reduce-scatter.5
  1160.3 77.9 all-reduce.10
where the time goes:
time: 1270 us; the launch traced here: 1250 us
  waiting for transfers between devices  433 us (34%)
  matrix products  275 us (22%)
  other arithmetic  223 us (18%)
  blocking collectives  176 us (14%)
  local copies, waits for them, and re-layouts  108 us (9%)
  starting transfers between devices  22.1 us (2%)
  between operations  16.7 us (1%)
    reduce_scatter x1, waiting for transfers between devices, shards(): lax.psum_scatter(atrous_term.astype(jnp.bfloat16), 'rows', scatter_dimens...  397 us
    dot_general x30, matrix products, transposed(): lax.dot_general(left, right, (((1,), (1,)), ((), ())), preferred_element_...  135 us
    scatter-add x1, other arithmetic, shards(): jax.ops.segment_sum(jnp.ones((grid_rows * grid_cols,), jnp.float32), imag...  128 us
    dot_general x27, matrix products, shards(): jnp.dot(source, w_atrous[branch, stencil], preferred_element_type=jnp.flo...  67 us
    dot_general x27, matrix products, shards(): jnp.einsum('pk,pc->kc', source, masked, preferred_element_type=jnp.float32)  59.7 us
    psum x1, blocking collectives, shards(): first_sum, second_sum = lax.psum((first_sum, second_sum), ('rows', 'cols'))  55.2 us
    psum x1, blocking collectives, shards(): lax.psum((shift_sums, gain_sums, image_grads), ('rows', 'cols'))  40.8 us
    psum x1, blocking collectives, shards(): lax.psum((jnp.sum(final_z, axis=0), jnp.sum(final_z * final_z, axis=0)),...  40.3 us
  transfers between devices with their start and end apart: 13, of which 2 were waited for; matrix products, arithmetic and copies ran while one was open for 37% of the time, Pallas kernels for 0%

commit v1 on v0

--- a/solution.py
+++ b/solution.py
@@ -1,14 +1,488 @@
+import functools
 import jax
 import jax.numpy as jnp
 from jax import lax
+from jax.experimental import pallas as pl
+from jax.experimental.pallas import tpu as pltpu
 from jax.sharding import PartitionSpec as P
 
+MESH = pl.DeviceIdType.MESH
 RATE_LOW = 6
 RATE_MID = 12
 RATE_TOP = 18
-
-
+STEP = RATE_LOW
+REACH = RATE_TOP // STEP
+HALO = {1: 48, 2: 80, 3: 112}
+SLOTS = 4
 epsilon = 1e-05
+F32 = jnp.float32
+BF16 = jnp.bfloat16
+
+
+def wide(column, width):
+    return jnp.concatenate([column] * (width // column.shape[-1]), axis=-1)
+
+
+def silu_parts(preact):
+    sigma = jax.nn.sigmoid(preact)
+    return preact * sigma, sigma * (1.0 + preact * (1.0 - sigma))
+
+
+def contract_rows(left, right):
+    return lax.dot_general(left, right, (((0,), (0,)), ((), ())), preferred_element_type=F32)
+
+
+def contract_lanes(left, right):
+    return lax.dot_general(left, right, (((1,), (1,)), ((), ())), preferred_element_type=F32)
+
+
+def greet_all(rows, cols, r, c):
+    barrier = pltpu.get_barrier_semaphore()
+    for dr in range(rows):
+        for dc in range(cols):
+            if dr or dc:
+                other = (lax.rem(r + dr, rows), lax.rem(c + dc, cols))
+                pl.semaphore_signal(barrier, inc=1, device_id=other, device_id_type=MESH)
+    pl.semaphore_wait(barrier, rows * cols - 1)
+
+
+class Exchange:
+    def __init__(self, axis_size, place, to_device, slots, send_sems, recv_sems):
+        self.size, self.place, self.to_device = axis_size, place, to_device
+        self.slots, self.send_sems, self.recv_sems = slots, send_sems, recv_sems
+
+    def copy(self, step, source=None):
+        other = lax.rem(self.place + step, self.size)
+        mine = self.slots.at[self.place]
+        return pltpu.make_async_remote_copy(
+            src_ref=mine if source is None else source(other),
+            dst_ref=mine,
+            send_sem=self.send_sems.at[step],
+            recv_sem=self.recv_sems.at[self.place],
+            device_id=self.to_device(other),
+            device_id_type=MESH,
+        )
+
+    def start(self, source=None):
+        for step in range(1, self.size):
+            self.copy(step, source).start()
+
+    def finish(self, source=None):
+        for step in range(1, self.size):
+            other = lax.rem(self.place + step, self.size)
+            there = self.slots.at[other]
+            pltpu.make_async_remote_copy(
+                src_ref=there,
+                dst_ref=there,
+                send_sem=self.send_sems.at[step],
+                recv_sem=self.recv_sems.at[other],
+                device_id=self.to_device(other),
+                device_id_type=MESH,
+            ).wait_recv()
+        for step in range(1, self.size):
+            self.copy(step, source).wait_send()
+
+    def total(self):
+        value = self.slots[0]
+        for other in range(1, self.size):
+            value = value + self.slots[other]
+        return value
+
+
+def forward_kernel(
+    rows, cols, image_count, total_pixels,
+    x_ref, ids_ref, wat_ref, wpt_ref, wpl_ref, wpj_ref, gain_ref, shift_ref, cot_ref, counts_ref,
+    out_ref, dz_ref, pj_ref, stat_ref, pooled_ref, pooln_ref, pools_ref, dap_ref, xsub_ref,
+    idrep, wbuf, wplbuf, ubuf, zx1, zx2, zx3, zs1, zs2, zs3,
+    halo_bufs, zn, slope, joined, zf, dzf, isum, cbuf, rbuf, pr_buf, pc_buf, pz_buf,
+    wsem, wplsem, hsend, hrecv, csend, crecv, rsend, rrecv, psend, precv, pcsend, pcrecv, pzsend, pzrecv,
+    xsend, xrecv,
+):
+    r, c = lax.axis_index("rows"), lax.axis_index("cols")
+    blocks, rb, width = zn.shape[1], zn.shape[2], zn.shape[3]
+    pixels = blocks * rb
+    own = REACH * 36
+    images = isum.shape[0]
+    zx, zs = {1: zx1, 2: zx2, 3: zx3}, {1: zs1, 2: zs2, 3: zs3}
+    order = (3, 2, 1)
+    taps = 27
+
+    def weight_copy(n):
+        branch, tap = 2 - n // 9, lax.rem(n, 9)
+        slot = lax.rem(n, SLOTS)
+        return pltpu.make_async_copy(wat_ref.at[branch, tap], wbuf.at[slot], wsem.at[slot])
+
+    for n in range(SLOTS - 1):
+        weight_copy(jnp.int32(n)).start()
+    share = x_ref.shape[1] // rows
+    pool_weight = pltpu.make_async_copy(
+        wpl_ref.at[pl.ds(pl.multiple_of(r * share, share), share)], wplbuf, wplsem
+    )
+    pool_weight.start()
+    for block in range(idrep.shape[0]):
+        idrep[block] = jnp.broadcast_to(ids_ref[:, block : block + 1], idrep.shape[1:])
+    greet_all(rows, cols, r, c)
+
+    own_ids = jnp.concatenate([idrep[REACH + a, own : own + rb, :] for a in range(blocks)], axis=0)
+    lanes = lax.broadcasted_iota(jnp.int32, (pixels, 128), 1).astype(F32)
+    one_hot = jnp.concatenate(
+        [(own_ids == lanes + 128.0 * part).astype(F32).astype(BF16) for part in range(pl.cdiv(images, 128))],
+        axis=1,
+    )
+    for part in range(rows):
+        piece = slice(part * share, (part + 1) * share)
+        isum[:, piece] = contract_rows(one_hot, x_ref[:, piece])[:images]
+    pool_rows = Exchange(rows, r, lambda other: (other, c), pr_buf, psend, precv)
+
+    def share_of(other):
+        return isum.at[:, pl.ds(pl.multiple_of(other * share, share), share)]
+
+    pr_buf[r] = isum[:, pl.ds(pl.multiple_of(r * share, share), share)]
+    pool_rows.start(share_of)
+
+    def halo_copies(m):
+        height = HALO[m]
+        a_range = {-1: (0, m), 0: (m, blocks), 1: (m + blocks, m)}
+        r_range = {-1: (0, height), 0: (height, rb), 1: (height + rb, height)}
+        copies = []
+        for place, (dr, dc) in enumerate(DIRECTIONS):
+            a0, na = a_range[dc]
+            r0, nr = r_range[dr]
+            copies.append(
+                (
+                    dr,
+                    dc,
+                    pltpu.make_async_remote_copy(
+                        src_ref=zs[m].at[pl.ds(a0, na), pl.ds(r0, nr)],
+                        dst_ref=halo_bufs[(m - 1) * 8 + place],
+                        send_sem=hsend.at[m - 1, place],
+                        recv_sem=hrecv.at[m - 1, place],
+                        device_id=(lax.rem(r + dr + rows, rows), lax.rem(c + dc + cols, cols)),
+                        device_id_type=MESH,
+                    ),
+                )
+            )
+        return copies
+
+    def inside(dr, dc):
+        return (r + dr >= 0) & (r + dr < rows) & (c + dc >= 0) & (c + dc < cols)
+
+    for position, m in enumerate(order):
+        height = HALO[m]
+
+        @pl.loop(0, blocks + 2 * m)
+        def _(block):
+            zx[m][block] = jnp.zeros(zx[m].shape[1:], F32)
+
+        for i in range(3):
+            @pl.loop(0, blocks + 2 * m)
+            def _(block):
+                ubuf[block] = jnp.zeros(ubuf.shape[1:], F32)
+
+            @pl.loop(0, 3)
+            def _(j):
+                n = position * 9 + 3 * i + j
+                slot = lax.rem(n, SLOTS)
+                ahead = n + SLOTS - 1
+
+                @pl.when(ahead < taps)
+                def _():
+                    weight_copy(ahead).start()
+
+                weight_copy(n).wait()
+                product = jnp.dot(x_ref[...], wbuf[slot], preferred_element_type=F32)
+                for a in range(blocks):
+                    same = idrep[REACH + a, own : own + rb] == idrep[REACH + a - (j - 1) * m, own : own + rb]
+                    part = product[a * rb : (a + 1) * rb]
+                    ubuf[a + (2 - j) * m] += jnp.where(wide(same.astype(F32), width) > 0.0, part, 0.0)
+
+            up = (i - 1) * 36 * m
+
+            @pl.loop(0, blocks + 2 * m)
+            def _(block):
+                value = ubuf[block]
+                if i != 1:
+                    here = REACH - m + block
+                    same = idrep[here, own : own + rb] == idrep[here, own - up : own - up + rb]
+                    value = jnp.where(wide(same.astype(F32), width) > 0.0, value, 0.0)
+                zx[m][block, height - up : height - up + rb] += value
+
+        @pl.loop(0, blocks + 2 * m)
+        def _(block):
+            zs[m][block] = zx[m][block].astype(BF16)
+
+        for dr, dc, copy in halo_copies(m):
+            pl.when(inside(dr, dc))(copy.start)
+
+        @pl.loop(0, blocks)
+        def _(a):
+            zn[m, a] = zx[m][m + a, height : height + rb]
+
+    product = jnp.dot(x_ref[...], wpt_ref[...], preferred_element_type=F32)
+    for a in range(blocks):
+        zn[0, a] = product[a * rb : (a + 1) * rb]
+
+    members = [(dy, dx, dk) for dy in range(2) for dx in range(2) for dk in range(2)]
+    half = share // 2
+
+    def channel_slices(y, x, k):
+        return [pl.multiple_of((2 * (2 * k + l) + y) * share + x * half, 128) for l in range(2)]
+
+    def member_copies():
+        mine = lax.rem(r, 2) * cols + c
+        copies = []
+        for step, (dy, dx, dk) in enumerate(members):
+            y, x, k = lax.rem(r + dy, 2), lax.rem(c // 2 + dx, 2), lax.rem(c + dk, 2)
+            for l, start in enumerate(channel_slices(y, x, k)):
+                source = x_ref.at[:, pl.ds(start, half)]
+                target = xsub_ref.at[l, mine]
+                if step == 0:
+                    copies.append(pltpu.make_async_copy(source, target, xrecv.at[l, mine]))
+                else:
+                    copies.append(
+                        pltpu.make_async_remote_copy(
+                            src_ref=source,
+                            dst_ref=target,
+                            send_sem=xsend.at[l, step],
+                            recv_sem=xrecv.at[l, mine],
+                            device_id=(2 * (r // 2) + y, 2 * x + k),
+                            device_id_type=MESH,
+                        )
+                    )
+        return copies
+
+    for copy in member_copies():
+        copy.start()
+
+    pool_rows.finish(share_of)
+    pool_cols = Exchange(cols, c, lambda other: (r, other), pc_buf, pcsend, pcrecv)
+    pc_buf[c] = pool_rows.total()
+    pool_cols.start()
+    pool_cols.finish()
+    counts = counts_ref[...]
+    pooled = (pool_cols.total() / wide(counts, share)).astype(BF16)
+    pooled_ref[...] = pooled
+    pool_weight.wait()
+    pool_z = Exchange(rows, r, lambda other: (other, c), pz_buf, pzsend, pzrecv)
+    pz_buf[r] = jnp.dot(pooled, wplbuf[...], preferred_element_type=F32)
+    pool_z.start()
+    pool_z.finish()
+    zp = pool_z.total()
+    pool_avg = jnp.sum(zp, axis=0, keepdims=True) / image_count
+    pool_square = jnp.sum(zp * zp, axis=0, keepdims=True) / image_count
+    pool_inverse = lax.rsqrt(pool_square - pool_avg * pool_avg + epsilon)
+    pool_normed = (zp - pool_avg) * pool_inverse
+    pool_active, pool_slope = silu_parts(gain_ref[4:5] * pool_normed + shift_ref[4:5])
+    pooln_ref[...] = pool_normed
+    pools_ref[...] = pool_slope
+    spare = one_hot.shape[1] - images
+    pool_active = jnp.concatenate([pool_active, jnp.zeros((spare, width), F32)], axis=0).astype(BF16)
+    joined[:, 4 * width : 5 * width] = jnp.dot(one_hot, pool_active, preferred_element_type=F32).astype(BF16)
+
+    for m in order:
+        height = HALO[m]
+        a_range = {-1: (blocks - m, m), 0: (0, blocks), 1: (0, m)}
+        r_range = {-1: (rb - height, height), 0: (0, rb), 1: (0, height)}
+        for place, (dr, dc, copy) in enumerate(halo_copies(m)):
+            a0, na = a_range[dc]
+            r0, nr = r_range[dr]
+
+            @pl.when(inside(-dr, -dc))
+            def _():
+                copy.wait_recv()
+                for a in range(na):
+                    zn[m, a0 + a, r0 : r0 + nr] += halo_bufs[(m - 1) * 8 + place][a].astype(F32)
+
+    def all_sum(step, value):
+        across = Exchange(cols, c, lambda other: (r, other), cbuf.at[step], csend.at[step], crecv.at[step])
+        cbuf[step, c] = value
+        across.start()
+        across.finish()
+        down = Exchange(rows, r, lambda other: (other, c), rbuf.at[step], rsend.at[step], rrecv.at[step])
+        rbuf[step, r] = across.total()
+        down.start()
+        down.finish()
+        return down.total()
+
+    zero = jnp.zeros((1, width), F32)
+
+    def row_sum(value):
+        return jnp.sum(value, axis=0, keepdims=True)
+
+    firsts, seconds = [], []
+    for k in range(4):
+        first, second = zero, zero
+        for a in range(blocks):
+            value = zn[k, a]
+            first, second = first + row_sum(value), second + row_sum(value * value)
+        firsts.append(first)
+        seconds.append(second)
+    moments = all_sum(0, jnp.concatenate(firsts + seconds, axis=0))
+    average = moments[0:4] / total_pixels
+    inverse = lax.rsqrt(moments[4:8] / total_pixels - average * average + epsilon)
+    for k in range(4):
+        @pl.loop(0, blocks)
+        def _(a):
+            normed = (zn[k, a] - average[k : k + 1]) * inverse[k : k + 1]
+            active, slant = silu_parts(gain_ref[k : k + 1] * normed + shift_ref[k : k + 1])
+            zn[k, a] = normed
+            slope[k, a] = slant
+            joined[pl.ds(pl.multiple_of(a * rb, rb), rb), k * width : (k + 1) * width] = active.astype(BF16)
+
+    zf[...] = jnp.dot(joined[...], wpj_ref[...], preferred_element_type=F32)
+    first, second = zero, zero
+    for a in range(blocks):
+        value = zf[a * rb : (a + 1) * rb]
+        first, second = first + row_sum(value), second + row_sum(value * value)
+    moments = all_sum(1, jnp.concatenate([first, second] + [zero] * 6, axis=0))
+    final_avg = moments[0:1] / total_pixels
+    final_inverse = lax.rsqrt(moments[1:2] / total_pixels - final_avg * final_avg + epsilon)
+    shift_last, gain_last = zero, zero
+    for a in range(blocks):
+        piece = slice(a * rb, (a + 1) * rb)
+        normed = (zf[piece] - final_avg) * final_inverse
+        result, slant = silu_parts(gain_ref[5:6] * normed + shift_ref[5:6])
+        out_ref[piece] = result.astype(BF16)
+        grad = cot_ref[piece].astype(F32) * slant
+        zf[piece] = normed
+        slope_last = grad
+        dzf[piece] = slope_last
+        shift_last, gain_last = shift_last + row_sum(grad), gain_last + row_sum(grad * normed)
+    sums = all_sum(2, jnp.concatenate([shift_last, gain_last] + [zero] * 6, axis=0))
+    shift_last, gain_last = sums[0:1], sums[1:2]
+    gain = gain_ref[5:6]
+    for a in range(blocks):
+        piece = slice(a * rb, (a + 1) * rb)
+        dzf[piece] = final_inverse * (
+            dzf[piece] * gain
+            - gain * shift_last / total_pixels
+            - zf[piece] * (gain * gain_last / total_pixels)
+        )
+    grad_final = dzf[...].astype(BF16)
+
+    shifts, gains = [], []
+    for k in range(4):
+        grad = contract_lanes(grad_final, wpj_ref[k * width : (k + 1) * width])
+        shift_sum, gain_sum = zero, zero
+        for a in range(blocks):
+            part = grad[a * rb : (a + 1) * rb] * slope[k, a]
+            slope[k, a] = part
+            shift_sum, gain_sum = shift_sum + row_sum(part), gain_sum + row_sum(part * zn[k, a])
+        shifts.append(shift_sum)
+        gains.append(gain_sum)
+    grad_pixel = contract_lanes(grad_final, wpj_ref[4 * width : 5 * width])
+    upper = grad_pixel.astype(BF16)
+    lower = (grad_pixel - upper.astype(F32)).astype(BF16)
+    dap_ref[...] = (contract_rows(one_hot, upper) + contract_rows(one_hot, lower))[:images]
+    sums = all_sum(3, jnp.concatenate(shifts + gains, axis=0))
+    for k in range(4):
+        gain = gain_ref[k : k + 1]
+        from_shift = gain * sums[k : k + 1] / total_pixels
+        from_gain = gain * sums[4 + k : 5 + k] / total_pixels
+
+        @pl.loop(0, blocks)
+        def _(a):
+            dz_ref[k, a] = (
+                inverse[k : k + 1] * (slope[k, a] * gain - from_shift - zn[k, a] * from_gain)
+            ).astype(BF16)
+
+    for k in range(5):
+        piece = slice(k * width, (k + 1) * width)
+        pj_ref[piece] = contract_rows(joined[:, piece], grad_final).astype(BF16)
+    stat_ref[...] = jnp.concatenate([sums, shift_last, gain_last, pool_inverse] + [zero] * 5, axis=0)
+
+    for m in order:
+        for dr, dc, copy in halo_copies(m):
+            pl.when(inside(dr, dc))(copy.wait_send)
+    for step, copy in enumerate(member_copies()):
+        if step < 2:
+            copy.wait()
+        else:
+            copy.wait_send()
+    for l in range(2):
+        for step, (dy, dx, dk) in enumerate(members):
+            if step:
+                y, x, k = lax.rem(r + dy, 2), lax.rem(c // 2 + dx, 2), lax.rem(c + dk, 2)
+                there = xsub_ref.at[l, y * cols + 2 * x + k]
+                pltpu.make_async_remote_copy(
+                    src_ref=there,
+                    dst_ref=there,
+                    send_sem=xsend.at[l, step],
+                    recv_sem=xrecv.at[l, y * cols + 2 * x + k],
+                    device_id=(2 * (r // 2) + y, 2 * x + k),
+                    device_id_type=MESH,
+                ).wait_recv()
+
+
+DIRECTIONS = ((-1, 0), (1, 0), (-1, -1), (-1, 1), (1, -1), (1, 1), (0, -1), (0, 1))
+
+
+def forward_call(rows, cols, image_count, x, ids, wat, wpt, wpl, wpj, gain, shift, cot, counts):
+    pixels, channels = x.shape
+    width = wpt.shape[1]
+    blocks, rb = 4, pixels // 4
+    images = counts.shape[0]
+    share = channels // rows
+    total_pixels = float(pixels * rows * cols)
+    vmem = pl.BlockSpec(memory_space=pltpu.VMEM)
+    hbm = pl.BlockSpec(memory_space=pl.ANY)
+
+    def ext(m, kind):
+        return pltpu.VMEM((blocks + 2 * m, 2 * HALO[m] + rb, width), kind)
+
+    halo_bufs = []
+    for m in (1, 2, 3):
+        for dr, dc in DIRECTIONS:
+            halo_bufs.append(pltpu.VMEM((m if dc else blocks, HALO[m] if dr else rb, width), BF16))
+    dma = pltpu.SemaphoreType.DMA
+    return pl.pallas_call(
+        functools.partial(forward_kernel, rows, cols, float(image_count), total_pixels),
+        out_shape=(
+            jax.ShapeDtypeStruct((pixels, width), BF16),
+            jax.ShapeDtypeStruct((4, blocks, rb, width), BF16),
+            jax.ShapeDtypeStruct((5 * width, width), BF16),
+            jax.ShapeDtypeStruct((16, width), F32),
+            jax.ShapeDtypeStruct((images, share), BF16),
+            jax.ShapeDtypeStruct((images, width), F32),
+            jax.ShapeDtypeStruct((images, width), F32),
+            jax.ShapeDtypeStruct((images, width), F32),
+            jax.ShapeDtypeStruct((2, 8, pixels, share // 2), BF16),
+        ),
+        in_specs=[vmem, vmem, hbm, vmem, hbm, vmem, vmem, vmem, vmem, vmem],
+        out_specs=(vmem,) * 8 + (hbm,),
+        scratch_shapes=[
+            pltpu.VMEM((blocks + 2 * REACH, ids.shape[0], 128), F32),
+            pltpu.VMEM((SLOTS, channels, width), BF16),
+            pltpu.VMEM((share, width), BF16),
+            pltpu.VMEM((blocks + 2 * REACH, rb, width), F32),
+            ext(1, F32), ext(2, F32), ext(3, F32),
+            ext(1, BF16), ext(2, BF16), ext(3, BF16),
+            halo_bufs,
+            pltpu.VMEM((4, blocks, rb, width), F32),
+            pltpu.VMEM((4, blocks, rb, width), F32),
+            pltpu.VMEM((pixels, 5 * width), BF16),
+            pltpu.VMEM((pixels, width), F32),
+            pltpu.VMEM((pixels, width), F32),
+            pltpu.VMEM((images, channels), F32),
+            pltpu.VMEM((4, cols, 8, width), F32),
+            pltpu.VMEM((4, rows, 8, width), F32),
+            pltpu.VMEM((rows, images, share), F32),
+            pltpu.VMEM((cols, images, share), F32),
+            pltpu.VMEM((rows, images, width), F32),
+            dma((SLOTS,)), dma,
+            dma((3, 8)), dma((3, 8)),
+            dma((4, cols)), dma((4, cols)),
+            dma((4, rows)), dma((4, rows)),
+            dma((rows,)), dma((rows,)),
+            dma((cols,)), dma((cols,)),
+            dma((rows,)), dma((rows,)),
+            dma((2, 8)), dma((2, 8)),
+        ],
+        compiler_params=pltpu.CompilerParams(
+            collective_id=0, has_side_effects=True, vmem_limit_bytes=60 * 2**20
+        ),
+        cost_estimate=pl.CostEstimate(flops=2 * pixels * channels * width * 28, bytes_accessed=40_000_000, transcendentals=0),
+    )(x, ids, wat, wpt, wpl, wpj, gain, shift, cot, counts)
 
 
 def extended(cells, sides, width):
@@ -236,10 +710,112 @@
     )
 
 
+def to_blocks(cells):
+    height, breadth, depth = cells.shape
+    cells = cells.reshape(height, breadth // STEP, STEP, depth)
+    return cells.transpose(1, 0, 2, 3).reshape(height * breadth, depth)
+
+
+def from_blocks(cells, height, breadth):
+    depth = cells.shape[-1]
+    cells = cells.reshape(breadth // STEP, height, STEP, depth)
+    return cells.transpose(1, 0, 2, 3).reshape(height, breadth, depth)
+
+
+def id_columns(ids):
+    height, breadth = ids.shape
+    table = ids.reshape(height, breadth // STEP, STEP).transpose(0, 2, 1).reshape(height * STEP, breadth // STEP)
+    return jnp.pad(table.astype(F32), ((0, 0), (0, 128 - breadth // STEP)))
+
+
+def quick_shards(
+    features, image_ids, w_point, w_atrous, w_pool, w_proj, norm_gain, norm_shift, cotangent
+):
+    rows_here, cols_here, channels = features.shape
+    branch_width = w_point.shape[1]
+    pixels = rows_here * cols_here
+    grid_rows, grid_cols = image_ids.shape
+    image_count = grid_rows // 16 * (grid_cols // 32)
+    images = -(-image_count // 16) * 16
+    margin = RATE_TOP
+    rows, cols = lax.axis_size("rows"), lax.axis_size("cols")
+    row_index = lax.axis_index("rows")
+    col_index = lax.axis_index("cols")
+    id_padded = jnp.pad(image_ids, margin, constant_values=-1)
+    window = lax.dynamic_slice(
+        id_padded,
+        (row_index * rows_here, col_index * cols_here),
+        (rows_here + 2 * margin, cols_here + 2 * margin),
+    )
+    own_ids = window[margin : margin + rows_here, margin : margin + cols_here]
+    own_flat = own_ids.reshape(pixels)
+    counts = jnp.sum(
+        (image_ids.reshape(-1, 1) == jnp.arange(images, dtype=jnp.int32)[None, :]).astype(F32), axis=0
+    )
+    counts = jnp.maximum(counts, 1.0)
+    x = to_blocks(features)
+    cot = to_blocks(cotangent)
+    output, dz, proj_term, stats, pooled, pool_normed, pool_slope, dap, xsub = forward_call(
+        rows, cols, image_count, x, id_columns(window), w_atrous, w_point, w_pool, w_proj,
+        norm_gain, norm_shift, cot, jnp.broadcast_to(counts[:, None], (images, 128)),
+    )
+    output = from_blocks(output, rows_here, cols_here)
+    flattened = features.reshape(pixels, channels)
+    grad_branch = dz.reshape(4, cols_here // STEP, rows_here, STEP, branch_width).transpose(2, 1, 3, 0, 4).reshape(pixels, 4, branch_width)
+    image_grads = lax.psum(dap, ("rows", "cols"))
+    grad_pool_pre = image_grads * pool_slope
+    pool_shift = jnp.sum(grad_pool_pre, axis=0)
+    pool_gain = jnp.sum(grad_pool_pre * pool_normed, axis=0)
+    grad_pool_z = (
+        stats[10]
+        * (
+            grad_pool_pre * norm_gain[4]
+            - norm_gain[4] * pool_shift / image_count
+            - pool_normed * (norm_gain[4] * pool_gain / image_count)
+        )
+    ).astype(BF16)
+    grad_pool = contract_rows(pooled, grad_pool_z)
+    grad_pooled = contract_lanes(grad_pool_z, w_pool) / counts[:, None]
+    one_hot = (own_flat[:, None] == jnp.arange(images, dtype=jnp.int32)[None, :]).astype(BF16)
+    grad_input = jnp.dot(one_hot, grad_pooled.astype(BF16), preferred_element_type=F32)
+    grad_input = grad_input + contract_lanes(grad_branch[:, 0], w_point)
+    point_term = contract_rows(flattened, grad_branch[:, 0])
+    stacked = grad_branch[:, 1:].reshape(rows_here, cols_here, 3 * branch_width)
+    grad_padded = extended(stacked, (("rows", 0), ("cols", 1)), margin)
+    terms = []
+    for branch, dilation in enumerate((RATE_LOW, RATE_MID, RATE_TOP)):
+        for stencil in range(9):
+            row_shift = (stencil // 3 - 1) * dilation
+            col_shift = (stencil % 3 - 1) * dilation
+            incoming = grad_padded[
+                margin - row_shift : margin - row_shift + rows_here,
+                margin - col_shift : margin - col_shift + cols_here,
+                branch * branch_width : (branch + 1) * branch_width,
+            ].reshape(pixels, branch_width)
+            same = image_match(window, own_ids, margin - row_shift, margin - col_shift)
+            masked = jnp.where(same > 0, incoming, jnp.zeros((), BF16))
+            grad_input = grad_input + contract_lanes(masked, w_atrous[branch, stencil])
+            terms.append(contract_rows(flattened, masked))
+    atrous_term = jnp.stack(terms).reshape(3, 9, channels, branch_width)
+
+    def shared(term, dim):
+        part = lax.psum_scatter(term.astype(BF16), "rows", scatter_dimension=dim, tiled=True)
+        return lax.psum(part, "cols").astype(F32)
+
+    grad_gain = jnp.concatenate([stats[4:8], pool_gain[None], stats[9:10]], axis=0)
+    grad_shift = jnp.concatenate([stats[0:4], pool_shift[None], stats[8:9]], axis=0)
+    grad_features = grad_input.astype(BF16).reshape(rows_here, cols_here, channels)
+    return (
+        output, grad_features, shared(point_term, 0), shared(atrous_term, 2), grad_pool,
+        shared(proj_term, 0), grad_gain, grad_shift,
+    )
+
+
 def solution(mesh):
     placed = (P("rows", "cols", None), P(), P(), P(), P(), P(), P(), P(), P("rows", "cols", None))
+    quick = mesh.shape["rows"] == 8 and mesh.shape["cols"] == 4
     return jax.shard_map(
-        shards,
+        quick_shards if quick else shards,
         mesh=mesh,
         in_specs=placed,
         out_specs=(

time: 1270 us -> 861 us (0.68)
  other arithmetic: 223 us -> 24 us
  Pallas kernels: 0 us -> 126 us
  blocking collectives: 176 us -> 55.3 us
  matrix products: 275 us -> 166 us
  waiting for transfers between devices: 433 us -> 370 us
  local copies, waits for them, and re-layouts: 108 us -> 86.6 us
    scatter-add x2 -> x0, other arithmetic: 135 us -> none  [the longest x1 128 us: shards(): jax.ops.segment_sum(jnp.ones((grid_rows * grid_cols,), jnp.float32), imag...]
    pallas_call x0 -> x1, Pallas kernels: none -> 126 us  [forward_call(): pl.pallas_call(functools.partial(forward_kernel, rows, cols, float(image_...]
    psum x4 -> x1, blocking collectives: 176 us -> 55.3 us  [quick_shards(): image_grads = lax.psum(dap, ('rows', 'cols'))]
    dot_general x91 -> x58, matrix products: 275 us -> 166 us  [the longest x28 131 us: contract_lanes(): lax.dot_general(left, right, (((1,), (1,)), ((), ())), preferred_element_...]
    reduce_scatter x3, waiting for transfers between devices: 397 us -> 309 us  [shared(): lax.psum_scatter(term.astype(BF16), 'rows', scatter_dimension=dim, tiled=...]
    convert_element_type x0 -> x5, local copies, waits for them, and re-layouts: none -> 37 us  [the longest x1 36.7 us: shared(): term.astype(BF16)]
    ppermute x4 -> x2, waiting for transfers between devices: 0.01 us -> 24.4 us  [extended(): lax.ppermute(tail, axis, [(i, (i + 1) % count) for i in range(ends)])]
    convert_element_type x32 -> x4, other arithmetic: 29.6 us -> 7.43 us  [the longest x2 6.56 us: shared(): return lax.psum(part, 'cols').astype(F32)]
  transfers between devices with their start and end apart: 13 -> 8, of which waited for: 2 -> 3; matrix products, arithmetic and copies ran while one was open for 37% -> 28% of each run, Pallas kernels for 0% -> 0%
where the time goes in v1:
time: 861 us; the launch traced here: 856 us
  waiting for transfers between devices  370 us (43%)
  matrix products  166 us (19%)
  Pallas kernels  126 us (15%)
  local copies, waits for them, and re-layouts  86.6 us (10%)
  blocking collectives  55.3 us (6%)
  other arithmetic  24 us (3%)
  between operations  15.1 us (2%)
  starting transfers between devices  11.7 us (1%)
    reduce_scatter x3, waiting for transfers between devices, shared(): lax.psum_scatter(term.astype(BF16), 'rows', scatter_dimension=dim, tiled=...  309 us
    dot_general x28, matrix products, contract_lanes(): lax.dot_general(left, right, (((1,), (1,)), ((), ())), preferred_element_...  131 us
    pallas_call x1, Pallas kernels, forward_call(): pl.pallas_call(functools.partial(forward_kernel, rows, cols, float(image_...  126 us
    psum x1, blocking collectives, quick_shards(): image_grads = lax.psum(dap, ('rows', 'cols'))  55.3 us
    psum x1, waiting for transfers between devices, shared(): return lax.psum(part, 'cols').astype(F32)  37.1 us
    convert_element_type x1, local copies, waits for them, and re-layouts, shared(): term.astype(BF16)  36.7 us
    dot_general x29, matrix products, contract_rows(): lax.dot_general(left, right, (((0,), (0,)), ((), ())), preferred_element_...  30.3 us
    ppermute x2, waiting for transfers between devices, extended(): lax.ppermute(tail, axis, [(i, (i + 1) % count) for i in range(ends)])  24.4 us
  transfers between devices with their start and end apart: 8, of which 3 were waited for; matrix products, arithmetic and copies ran while one was open for 28% of the time, Pallas kernels for 0%

profile of v1, /device:TPU:0, one launch (start us, length us, event | category | flops | bytes accessed | tf_op | source)
XLA Modules:
  0.0 855.7 jit_solution(16072670721241039933)
XLA Ops:
  9.9 3.0 copy.53
  14.2 2.4 reshape.578.x_ref
  20.0 126.3 %shard_map.152 = (bf16[576,256]{1,0:T(8,128)(2,1)}, bf16[4,4,144,256]{3,2,1,0:T(8,128)(2,1)}, bf16[1280,256]{1,0:T(8,128)(2,1)}, f32[16,256]{1,0:T(8,128)}, bf16...) custom-call(bf16[576,2048]{1,0:T(8,128)(2,1)} %reshape.578.x_ref, ...), custom_call_target="tpu_custom_call" | custom-call | flops 16911433728 | bytes 40000000 | tf_op jit(solution)/shard_map/pallas_call | solution.py:438
  151.5 4.2 collective-permute-start
  160.3 24.4 %collective-permute-done = bf16[18,24,768]{2,1,0:T(8,128)(2,1)} collective-permute-done((bf16[18,24,768]{2,1,0:T(8,128)(2,1)}, bf16[18,24,768]{2,1,0:T(8,128)(2,1)}, u32[]{:S(2)}, u32[]{:S(2)}) %collective-permute-start) | collective-permute-done | bytes 663584 | tf_op jit(solution)/shard_map/ppermute | solution.py:496
  189.1 2.6 fusion.201
  195.9 2.0 fusion.81
  204.9 4.4 collective-permute-start.3
  210.0 2.7 copy.64
  212.7 3.4 maximum_select_fusion.15
  218.2 2.4 copy.66
  220.6 3.3 maximum_select_fusion.14
  225.0 3.0 maximum_select_fusion.13
  252.9 9.5 %copy-done.3 = bf16[27,2048,256]{1,2,0:T(8,128)(2,1)} copy-done((bf16[27,2048,256]{1,2,0:T(8,128)(2,1)}, bf16[27,2048,256]{1,2,0:T(8,128)(2,1)S(1)}, u32[]{:S(2)}) %copy-start.3) | copy-done | bytes 28311576
  262.4 36.7 %copy.67 = bf16[3,9,2048,256]{3,2,1,0:T(8,128)(2,1)} copy(bf16[3,9,2048,256]{2,3,1,0:T(8,128)(2,1)} %bitcast.605) | data formatting | bytes 56623104 | tf_op jit(solution)/shard_map/convert_element_type | solution.py:802
  301.0 55.3 %psum.28 = f32[48,256]{1,0:T(8,128)S(1)} all-reduce(f32[48,256]{1,0:T(8,128)S(1)} %copy-done.66), channel_id=1, replica_groups=mesh['rows'=8,'cols'=4] {'rows','cols'}, use_global_device_ids=true, to_apply=%region_1.2 | all-reduce | flops 12288 | bytes 98304 | tf_op jit(solution)/shard_map/psum | solution.py:765
  359.6 4.6 fusion.83
  364.2 4.6 fusion.167
  368.8 4.6 fusion.109
  373.3 4.7 fusion.127
  378.0 4.3 fusion.92
  382.3 4.3 fusion.115
  386.7 2.9 fusion.133
  389.6 2.9 fusion.103
  392.5 3.0 fusion.121
  395.5 3.0 fusion.86
  398.5 3.1 fusion.105
  401.6 3.0 fusion.111
  404.6 3.0 fusion.117
  407.6 2.9 fusion.135
  410.5 3.0 fusion.94
  413.5 3.1 fusion.99
  416.6 3.0 fusion.101
  419.6 3.0 fusion.107
  422.6 2.9 fusion.113
  425.5 2.9 fusion.131
  428.5 2.9 fusion.90
  431.4 2.9 fusion.96
  434.3 2.9 fusion.119
  437.3 3.0 fusion.123
  440.2 3.0 fusion.125
  443.3 2.9 fusion.129
  446.2 3.0 fusion.84
  449.2 3.0 fusion.88
  452.2 308.8 %reduce-scatter.6.cloned.1.call-done = bf16[3,9,256,256]{3,2,1,0:T(8,128)(2,1)} async-done(((bf16[3,9,2048,256]{3,2,1,0:T(8,128)(2,1)}), bf16[3,9,256,256]{3,2,1,0:T(8,128)(2,1)}) %reduce-scatter.6.cloned.1.call-update) | async-done | bytes 3538960 | tf_op jit(solution)/shard_map/reduce_scatter | solution.py:802
  761.0 43.4 %add_convert_fusion = bf16[576,2048]{1,0:T(8,128)(2,1)} fusion(f32[576,2048]{1,0:T(8,128)} %fusion.84, f32[576,2048]{1,0:T(8,128)} %fusion.86, f32[576,2048]{1,0:T(8,128)} %fusion.88, f32[576,2048]{1,0:T(8,128)} %fusion.90, f32[576,2048]{1,0:T(8,128)} %fusion.92, f32[576,2048]{1,0:T(8,128)} %fusion.94, f32[576,2048]{1,0:T(8,128)} %fusion.96, ...), kind=kOutput, calls=%fused_computation | convolution fusion | flops 638189568 | bytes 135823360 | tf_op jit(solution)/shard_map/dot_general | solution.py:36
  804.5 37.1 %all-reduce.5.cloned.1.call-done = (bf16[256,256]{0,1:T(8,128)(2,1)}, bf16[3,9,256,256]{3,2,1,0:T(8,128)(2,1)}, bf16[160,256]{1,0:T(8,128)(2,1)}) async-done(((bf16[256,256]{0,1:T(8,128)(2,1)}, bf16[3,9,256,256]{3,2,1,0:T(8,128)(2,1)}, bf16[160,256]{1,0:T(8,128)(2,1)}), (bf16[256,256]{0,1:T(8,128)(2,1)}, bf16[3,9,256,256]{3,2,1,0:T(8,128)(2,1)}, bf16[160,256]{1,0:T(8,128)(2,1)})) %all-reduce.5.cloned.1.call-update) | async-done | bytes 3751952 | tf_op jit(solution)/shard_map/psum | solution.py:803
  841.6 5.9 convert_element_type.160
  (243 shorter events, 67.3 us)
Async XLA Ops:
  7.2 445.0 %reduce-scatter.8.cloned.1.call-start = ((), (), s32[]{:S(2)}) async-start(), calls=%async_computation.5 | async-start | bytes 737280 | tf_op jit(solution)/shard_map/reduce_scatter | solution.py:802
  9.9 9.4 %copy-start.69 = (f32[48]{0:T(128)}, f32[48]{0:T(128)S(1)}, u32[]{:S(2)}) copy-start(f32[48]{0:T(128)S(1)} %broadcast_maximum_fusion) | copy-start | bytes 580
  151.5 33.2 %collective-permute-start = (bf16[18,24,768]{2,1,0:T(8,128)(2,1)}, bf16[18,24,768]{2,1,0:T(8,128)(2,1)}, u32[]{:S(2)}, u32[]{:S(2)}) collective-permute-start(bf16[18,24,768]{2,1,0:T(8,128)(2,1)} %slice.317), channel_id=1, source_target_pairs={{0,4},{4,8},{8,12},{12,16},{16,20},{20,24},{24,28},{1,5},{5,9},{9,... | collective-permute-start | bytes 1990664 | tf_op jit(solution)/shard_map/ppermute | solution.py:496
  157.3 28.9 %collective-permute-start.1 = (bf16[18,24,768]{2,1,0:T(8,128)(2,1)}, bf16[18,24,768]{2,1,0:T(8,128)(2,1)}, u32[]{:S(2)}, u32[]{:S(2)}) collective-permute-start(bf16[18,24,768]{2,1,0:T(8,128)(2,1)} %slice.320), channel_id=1, source_target_pairs={{4,0},{8,4},{12,8},{16,12},{20,16},{24,20},{28,24},{5,1},{9,5},{13... | collective-permute-start | bytes 1990664 | tf_op jit(solution)/shard_map/ppermute | solution.py:498
  158.6 293.6 %reduce-scatter.4.cloned.1.call-start = ((), (), s32[]{:S(2)}) async-start(), calls=%async_computation.3 | async-start | bytes 1179648 | tf_op jit(solution)/shard_map/reduce_scatter | solution.py:802
  160.3 28.8 %copy-start.4 = (bf16[24,24,768]{2,1,0:T(8,128)(2,1)}, bf16[24,24,768]{2,1,0:T(8,128)(2,1)S(1)}, u32[]{:S(2)}) copy-start(bf16[24,24,768]{2,1,0:T(8,128)(2,1)S(1)} %reshape.585) | copy-start | bytes 2654212
  193.4 16.6 %collective-permute-start.2 = (bf16[60,18,768]{2,0,1:T(8,128)(2,1)}, bf16[60,18,768]{2,0,1:T(8,128)(2,1)}, u32[]{:S(2)}, u32[]{:S(2)}) collective-permute-start(bf16[60,18,768]{2,0,1:T(8,128)(2,1)} %copy.63), channel_id=1, source_target_pairs={{1,0},{2,1},{3,2},{5,4},{6,5},{7,6},{9,8},{10,9},{11,10},{13,12},{... | collective-permute-start | bytes 4976648 | tf_op jit(solution)/shard_map/ppermute | solution.py:498
  197.9 563.1 %reduce-scatter.6.cloned.1.call-start = ((), (), s32[]{:S(2)}) async-start(), calls=%async_computation.4 | async-start | bytes 31850496 | tf_op jit(solution)/shard_map/reduce_scatter | solution.py:802
  198.4 10.9 %copy-start.57 = (bf16[42,24,768]{2,1,0:T(8,128)(2,1)S(1)}, bf16[42,24,768]{2,1,0:T(8,128)(2,1)}, u32[]{:S(2)}) copy-start(bf16[42,24,768]{2,1,0:T(8,128)(2,1)} %copy-done.56) | copy-start | bytes 4644868
  198.4 11.2 %copy-start.59 = (bf16[42,24,768]{2,1,0:T(8,128)(2,1)S(1)}, bf16[42,24,768]{2,1,0:T(8,128)(2,1)}, u32[]{:S(2)}) copy-start(bf16[42,24,768]{2,1,0:T(8,128)(2,1)} %copy-done.58) | copy-start | bytes 4644868
  204.9 7.8 copy-start.2
  204.9 13.3 %collective-permute-start.3 = (bf16[60,18,768]{2,0,1:T(8,128)(2,1)S(1)}, bf16[60,18,768]{2,0,1:T(8,128)(2,1)}, u32[]{:S(2)}, u32[]{:S(2)}) collective-permute-start(bf16[60,18,768]{2,0,1:T(8,128)(2,1)S(1)} %copy.65), channel_id=1, source_target_pairs={{0,1},{1,2},{2,3},{4,5},{5,6},{6,7},{8,9},{9,10},{10,11},{12,13},{... | collective-permute-start | bytes 4976648 | tf_op jit(solution)/shard_map/ppermute | solution.py:496
  209.6 7.6 copy-start.40
  209.6 25.6 %copy-start.42 = (bf16[24,24,256]{2,1,0:T(8,128)(2,1)}, bf16[24,24,256]{2,1,0:T(8,128)(2,1)S(1)}, u32[]{:S(2)}) copy-start(bf16[24,24,256]{2,1,0:T(8,128)(2,1)S(1)} %get-tuple-element.87) | copy-start | bytes 884740
  209.6 34.8 %copy-start.51 = (bf16[24,24,256]{2,1,0:T(8,128)(2,1)}, bf16[24,24,256]{2,1,0:T(8,128)(2,1)S(1)}, u32[]{:S(2)}) copy-start(bf16[24,24,256]{2,1,0:T(8,128)(2,1)S(1)} %get-tuple-element.86) | copy-start | bytes 884740
  209.9 22.3 %copy-start.46 = (bf16[24,24,256]{2,1,0:T(8,128)(2,1)}, bf16[24,24,256]{2,1,0:T(8,128)(2,1)S(1)}, u32[]{:S(2)}) copy-start(bf16[24,24,256]{2,1,0:T(8,128)(2,1)S(1)} %get-tuple-element.89) | copy-start | bytes 884740
  209.9 31.4 %copy-start.48 = (bf16[24,24,256]{2,1,0:T(8,128)(2,1)}, bf16[24,24,256]{2,1,0:T(8,128)(2,1)S(1)}, u32[]{:S(2)}) copy-start(bf16[24,24,256]{2,1,0:T(8,128)(2,1)S(1)} %get-tuple-element.91) | copy-start | bytes 884740
  209.9 40.9 %copy-start.44 = (bf16[24,24,256]{2,1,0:T(8,128)(2,1)}, bf16[24,24,256]{2,1,0:T(8,128)(2,1)S(1)}, u32[]{:S(2)}) copy-start(bf16[24,24,256]{2,1,0:T(8,128)(2,1)S(1)} %get-tuple-element.90) | copy-start | bytes 884740
  216.1 18.1 %copy-start.10 = (bf16[24,24,256]{2,1,0:T(8,128)(2,1)}, bf16[24,24,256]{2,1,0:T(8,128)(2,1)S(1)}, u32[]{:S(2)}) copy-start(bf16[24,24,256]{2,1,0:T(8,128)(2,1)S(1)} %get-tuple-element.68) | copy-start | bytes 884740
  216.1 21.1 %copy-start.12 = (bf16[24,24,256]{2,1,0:T(8,128)(2,1)}, bf16[24,24,256]{2,1,0:T(8,128)(2,1)S(1)}, u32[]{:S(2)}) copy-start(bf16[24,24,256]{2,1,0:T(8,128)(2,1)S(1)} %get-tuple-element.67) | copy-start | bytes 884740
  216.1 24.2 %copy-start.14 = (bf16[24,24,256]{2,1,0:T(8,128)(2,1)}, bf16[24,24,256]{2,1,0:T(8,128)(2,1)S(1)}, u32[]{:S(2)}) copy-start(bf16[24,24,256]{2,1,0:T(8,128)(2,1)S(1)} %get-tuple-element.66) | copy-start | bytes 884740
  216.1 30.7 %copy-start.6 = (bf16[24,24,256]{2,1,0:T(8,128)(2,1)}, bf16[24,24,256]{2,1,0:T(8,128)(2,1)S(1)}, u32[]{:S(2)}) copy-start(bf16[24,24,256]{2,1,0:T(8,128)(2,1)S(1)} %get-tuple-element.64) | copy-start | bytes 884740
  223.9 12.3 %copy-start.22 = (bf16[24,24,256]{2,1,0:T(8,128)(2,1)}, bf16[24,24,256]{2,1,0:T(8,128)(2,1)S(1)}, u32[]{:S(2)}) copy-start(bf16[24,24,256]{2,1,0:T(8,128)(2,1)S(1)} %get-tuple-element.74) | copy-start | bytes 884740
  223.9 15.3 %copy-start.24 = (bf16[24,24,256]{2,1,0:T(8,128)(2,1)}, bf16[24,24,256]{2,1,0:T(8,128)(2,1)S(1)}, u32[]{:S(2)}) copy-start(bf16[24,24,256]{2,1,0:T(8,128)(2,1)S(1)} %get-tuple-element.73) | copy-start | bytes 884740
  224.0 18.4 %copy-start.26 = (bf16[24,24,256]{2,1,0:T(8,128)(2,1)}, bf16[24,24,256]{2,1,0:T(8,128)(2,1)S(1)}, u32[]{:S(2)}) copy-start(bf16[24,24,256]{2,1,0:T(8,128)(2,1)S(1)} %get-tuple-element.72) | copy-start | bytes 884740
  224.0 21.4 %copy-start.16 = (bf16[24,24,256]{2,1,0:T(8,128)(2,1)}, bf16[24,24,256]{2,1,0:T(8,128)(2,1)S(1)}, u32[]{:S(2)}) copy-start(bf16[24,24,256]{2,1,0:T(8,128)(2,1)S(1)} %get-tuple-element.71) | copy-start | bytes 884740
  224.0 24.9 %copy-start.18 = (bf16[24,24,256]{2,1,0:T(8,128)(2,1)}, bf16[24,24,256]{2,1,0:T(8,128)(2,1)S(1)}, u32[]{:S(2)}) copy-start(bf16[24,24,256]{2,1,0:T(8,128)(2,1)S(1)} %get-tuple-element.70) | copy-start | bytes 884740
  228.1 5.1 copy-start.38
  228.1 21.8 %copy-start.28 = (bf16[24,24,256]{2,1,0:T(8,128)(2,1)}, bf16[24,24,256]{2,1,0:T(8,128)(2,1)S(1)}, u32[]{:S(2)}) copy-start(bf16[24,24,256]{2,1,0:T(8,128)(2,1)S(1)} %get-tuple-element.77) | copy-start | bytes 884740
  228.1 23.8 %copy-start.30 = (bf16[24,24,256]{2,1,0:T(8,128)(2,1)}, bf16[24,24,256]{2,1,0:T(8,128)(2,1)S(1)}, u32[]{:S(2)}) copy-start(bf16[24,24,256]{2,1,0:T(8,128)(2,1)S(1)} %get-tuple-element.81) | copy-start | bytes 884740
  252.9 9.5 %copy-start.3 = (bf16[27,2048,256]{1,2,0:T(8,128)(2,1)}, bf16[27,2048,256]{1,2,0:T(8,128)(2,1)S(1)}, u32[]{:S(2)}) copy-start(bf16[27,2048,256]{1,2,0:T(8,128)(2,1)S(1)} %fusion.28) | copy-start | bytes 84934656
  299.1 57.2 %copy-start.62 = (f32[48,256]{1,0:T(8,128)S(1)}, f32[48,256]{1,0:T(8,128)}, u32[]{:S(2)}) copy-start(f32[48,256]{1,0:T(8,128)} %get-tuple-element.20) | copy-start | bytes 147460
  299.1 57.2 %copy-start.63 = (f32[48,256]{1,0:T(8,128)S(1)}, f32[48,256]{1,0:T(8,128)}, u32[]{:S(2)}) copy-start(f32[48,256]{1,0:T(8,128)} %get-tuple-element.19) | copy-start | bytes 147460
  299.1 57.2 %copy-start.68 = (f32[16,256]{1,0:T(8,128)S(1)}, f32[16,256]{1,0:T(8,128)}, u32[]{:S(2)}) copy-start(f32[16,256]{1,0:T(8,128)} %get-tuple-element.17) | copy-start | bytes 49156
  299.1 58.6 %copy-start.67 = (bf16[48,256]{1,0:T(8,128)(2,1)S(1)}, bf16[48,256]{1,0:T(8,128)(2,1)}, u32[]{:S(2)}) copy-start(bf16[48,256]{1,0:T(8,128)(2,1)} %get-tuple-element.22) | copy-start | bytes 73732
  299.1 542.5 %all-reduce.5.cloned.1.call-start = ((), (), s32[]{:S(2)}) async-start(), calls=%async_computation.6 | async-start | bytes 7503872 | tf_op jit(solution)/shard_map/psum | solution.py:803
  359.6 27.0 %slice-start = ((s8[28311552]{0:T(1024)(128)(4,1)}), s8[3145728]{0:T(1024)(128)(4,1)S(1)}, s32[]{:S(2)}) async-start(s8[28311552]{0:T(1024)(128)(4,1)} %bitcast.606), calls=%async_computation.7 | async-start | bytes 6291456
  364.2 4.6 copy-start.55
  364.2 22.4 %slice-start.1 = ((s8[28311552]{0:T(1024)(128)(4,1)}), s8[4194304]{0:T(1024)(128)(4,1)S(1)}, s32[]{:S(2)}) async-start(s8[28311552]{0:T(1024)(128)(4,1)} %bitcast.606), calls=%async_computation.8 | async-start | bytes 8388608
  368.7 4.6 copy-start.54
  368.7 17.9 %slice-start.2 = ((s8[28311552]{0:T(1024)(128)(4,1)}), s8[4194304]{0:T(1024)(128)(4,1)S(1)}, s32[]{:S(2)}) async-start(s8[28311552]{0:T(1024)(128)(4,1)} %bitcast.606), calls=%async_computation.9 | async-start | bytes 8388608
  368.7 17.9 %slice-start.3 = ((s8[28311552]{0:T(1024)(128)(4,1)}), s8[4194304]{0:T(1024)(128)(4,1)S(1)}, s32[]{:S(2)}) async-start(s8[28311552]{0:T(1024)(128)(4,1)} %bitcast.606), calls=%async_computation.10 | async-start | bytes 8388608
  373.3 4.7 copy-start.53
  373.3 13.3 %slice-start.4 = ((s8[28311552]{0:T(1024)(128)(4,1)}), s8[4194304]{0:T(1024)(128)(4,1)S(1)}, s32[]{:S(2)}) async-start(s8[28311552]{0:T(1024)(128)(4,1)} %bitcast.606), calls=%async_computation.11 | async-start | bytes 8388608
  378.0 8.6 %slice-start.5 = ((s8[28311552]{0:T(1024)(128)(4,1)}), s8[4194304]{0:T(1024)(128)(4,1)S(1)}, s32[]{:S(2)}) async-start(s8[28311552]{0:T(1024)(128)(4,1)} %bitcast.606), calls=%async_computation.12 | async-start | bytes 8388608
  449.2 311.8 %copy-start.52 = (bf16[24,24,256]{2,1,0:T(8,128)(2,1)S(1)}, bf16[24,24,256]{2,1,0:T(8,128)(2,1)}, u32[]{:S(2)}) copy-start(bf16[24,24,256]{2,1,0:T(8,128)(2,1)} %copy-done.51) | copy-start | bytes 884740
  841.6 5.9 copy-start.64
  841.6 6.7 copy-start.65
  (37 other events, 107.5 us)
Sparse Core Ops, SparseCore 0:
  158.7 65.5 reduce-scatter.7
  228.1 62.8 reduce-scatter.3
  299.2 461.7 reduce-scatter.5
  763.6 77.9 all-reduce.4

commit v2 on v1

--- a/solution.py
+++ b/solution.py
@@ -485,6 +485,512 @@
     )(x, ids, wat, wpt, wpl, wpj, gain, shift, cot, counts)
 
 
+def backward_kernel(
+    rows, cols, image_count, height,
+    dz_ref, xsub_ref, ids_ref, wat_ref, wpt_ref, wpl_ref, gain_ref, counts_ref,
+    pooled_ref, pooln_ref, pools_ref, dap_ref, stat_ref,
+    gx_ref, dw_ref, gpool_ref, gstat_ref,
+    ext0, ext1, ext2, ext3, shifted, colmask, idrep, gmat, gown, xall, xt, acc, wbuf, wpt,
+    send1, recv1, keep, relay, dw, pcbuf, prbuf,
+    xsem, wsem, wptsem, zsend, zrecv, agsend, agrecv, s1send, s1recv, s2send, s2recv, s3send, s3recv,
+    pcsend, pcrecv, prsend, prrecv, outsem,
+):
+    r, c = lax.axis_index("rows"), lax.axis_index("cols")
+    z, y = r // 2, lax.rem(r, 2)
+    x, k = c // 2, lax.rem(c, 2)
+    levels = rows // 2
+    z_lo, z_hi = lax.rem(z, 2), z // 2
+    blocks, rb, width = dz_ref.shape[1:]
+    pair = 2 * rb
+    across = cols * blocks
+    pixels = blocks * rb
+    own = REACH * 36
+    half = xt.shape[0] // 2
+    images = dap_ref.shape[0]
+    ext = {0: ext0, 1: ext1, 2: ext2, 3: ext3}
+    tall = {0: 0, **HALO}
+    directs = ((0, 1), (1, 0), (1, 1))
+
+    def x_copy(l, dev, a):
+        dev_y, dev_c = dev // cols, lax.rem(dev, cols)
+        start = pl.multiple_of((dev_c * blocks + a) * pair + dev_y * rb, 16)
+        return pltpu.make_async_copy(
+            xsub_ref.at[l, dev, a], xall.at[l, pl.ds(start, rb)], xsem.at[l, dev, a]
+        )
+
+    for l in range(2):
+        for a in range(blocks):
+            @pl.loop(0, 2 * cols)
+            def _(dev):
+                x_copy(l, dev, a).start()
+
+    def weight_copy(n, j):
+        branch, i = n // 3, lax.rem(n, 3)
+        slot = lax.rem(n, 2)
+        return pltpu.make_async_copy(
+            wat_ref.at[branch, 3 * i + j],
+            wbuf.at[slot, :, pl.ds(j * width, width)],
+            wsem.at[slot, j],
+        )
+
+    point_copy = pltpu.make_async_copy(wpt_ref, wpt, wptsem)
+    point_copy.start()
+    for n in range(2):
+        for j in range(3):
+            weight_copy(jnp.int32(n), j).start()
+
+    greet_all(rows, cols, r, c)
+
+    def has_rim(dev_y):
+        return (dev_y == 1) & (z >= 1) | (dev_y == 0) & (z <= levels - 2)
+
+    def rim_copy(m, sending):
+        high = tall[m]
+        start = pl.multiple_of(y * (rb - high), 16)
+        target = pl.multiple_of((1 - y) * (high + pair), 16)
+        return pltpu.make_async_remote_copy(
+            src_ref=dz_ref.at[m, :, pl.ds(start, high)],
+            dst_ref=ext[m].at[pl.ds(c * blocks, blocks), pl.ds(target, high)],
+            send_sem=zsend.at[m],
+            recv_sem=zrecv.at[m],
+            device_id=(lax.rem(r + 4 * y - 2 + rows, rows), c),
+            device_id_type=MESH,
+        )
+
+    sends_rim = (y == 1) & (z <= levels - 2) | (y == 0) & (z >= 1)
+
+    def item(m, kind, dev_y, dev_c):
+        high = tall[m]
+        if kind == 0:
+            return ext[m].at[pl.ds(dev_c * blocks, blocks), pl.ds(pl.multiple_of(high + rb * dev_y, 16), rb)]
+        return ext[m].at[
+            pl.ds(dev_c * blocks, blocks), pl.ds(pl.multiple_of((1 - dev_y) * (high + pair), 16), high)
+        ]
+
+    def gather_copy(m, kind, dev_y, dev_c, slot, target):
+        piece = item(m, kind, dev_y, dev_c)
+        return pltpu.make_async_remote_copy(
+            src_ref=piece,
+            dst_ref=piece,
+            send_sem=agsend.at[m, kind, slot],
+            recv_sem=agrecv.at[m, kind, dev_y * cols + dev_c],
+            device_id=target,
+            device_id_type=MESH,
+        )
+
+    sibling = (r, 2 * x + 1 - k)
+
+    def place(dy, dx):
+        return lax.rem(y + dy, 2), 2 * lax.rem(x + dx, 2) + k
+
+    def if_there(kind, dev_y, action):
+        if kind == 0:
+            action()
+        else:
+            pl.when(has_rim(dev_y))(action)
+
+    def kinds(m):
+        return (0,) if m == 0 else (0, 1)
+
+    def first_copies(m, kind):
+        copies = []
+        for slot, (dy, dx) in enumerate(directs):
+            dev_y, dev_c = place(dy, dx)
+            copies.append(gather_copy(m, kind, y, c, slot, (2 * z + dev_y, dev_c)))
+        copies.append(gather_copy(m, kind, y, c, 3, sibling))
+        return copies
+
+    def start_first(m, kind):
+        def action():
+            for copy in first_copies(m, kind):
+                copy.start()
+
+        if_there(kind, y, action)
+
+    def forward(m):
+        for kind in kinds(m):
+            for slot, (dy, dx) in enumerate(directs):
+                dev_y, dev_c = place(dy, dx)
+
+                def action():
+                    copy = gather_copy(m, kind, dev_y, dev_c, 4 + slot, sibling)
+                    copy.wait_recv()
+                    copy.start()
+
+                if_there(kind, dev_y, action)
+
+    def finish_gather(m):
+        for kind in kinds(m):
+            for dy, dx in ((0, 0),) + directs:
+                dev_y, dev_c = place(dy, dx)
+                dev_c = dev_c + 1 - 2 * k
+                if_there(kind, dev_y, lambda: gather_copy(m, kind, dev_y, dev_c, 0, sibling).wait_recv())
+
+    def finish_sends(m):
+        for kind in kinds(m):
+            def action():
+                for copy in first_copies(m, kind):
+                    copy.wait_send()
+
+            if_there(kind, y, action)
+            for slot, (dy, dx) in enumerate(directs):
+                dev_y, dev_c = place(dy, dx)
+                if_there(
+                    kind, dev_y, lambda: gather_copy(m, kind, dev_y, dev_c, 4 + slot, sibling).wait_send()
+                )
+
+    def start_branch(m):
+        high = tall[m]
+        for a in range(blocks):
+            ext[m][c * blocks + a, pl.ds(pl.multiple_of(high + rb * y, 16), rb)] = dz_ref[m, a]
+        start_first(m, 0)
+
+    def start_rims(m):
+        def action():
+            rim_copy(m, False).wait_recv()
+            for copy in first_copies(m, 1):
+                copy.start()
+
+        pl.when(has_rim(y))(action)
+
+    for m in (1, 2, 3):
+        pl.when(sends_rim)(rim_copy(m, True).start)
+    start_branch(1)
+    start_rims(1)
+    start_branch(2)
+    start_rims(2)
+
+    pool_cols = Exchange(cols, c, lambda other: (r, other), pcbuf, pcsend, pcrecv)
+    pcbuf[c] = dap_ref[...]
+    pool_cols.start()
+
+    for block in range(across):
+        idrep[block] = jnp.broadcast_to(ids_ref[:, block : block + 1], idrep.shape[1:])
+    for m in (1, 2, 3):
+        high = tall[m]
+
+        @pl.when(z == 0)
+        def _():
+            @pl.loop(0, across)
+            def _(block):
+                ext[m][block, 0:high] = jnp.zeros((high, width), BF16)
+
+        @pl.when(z == levels - 1)
+        def _():
+            @pl.loop(0, across)
+            def _(block):
+                ext[m][block, high + pair : 2 * high + pair] = jnp.zeros((high, width), BF16)
+
+    for shift in range(-REACH, REACH + 1):
+        for block in range(across):
+            if 0 <= block - shift < across:
+                same = idrep[block, own : own + 48] == idrep[block - shift, own : own + 48]
+                colmask[REACH + shift, block] = wide(same.astype(F32), width).astype(BF16)
+            else:
+                colmask[REACH + shift, block] = jnp.zeros((48, width), BF16)
+
+    for l in range(2):
+        for a in range(blocks):
+            @pl.loop(0, 2 * cols)
+            def _(dev):
+                x_copy(l, dev, a).wait()
+
+        spot = pl.multiple_of(lax.rem(l + z_lo, 2) * half, half)
+        for chunk in range(xall.shape[1] // 128):
+            piece = slice(chunk * 128, (chunk + 1) * 128)
+            xt[pl.ds(spot, half), piece] = xall[l, piece, :].astype(F32).T.astype(BF16)
+
+    point_copy.wait()
+
+    @pl.loop(0, wpt.shape[0] // 256)
+    def _(n):
+        piece = pl.ds(pl.multiple_of(n * 256, 256), 256)
+        left = jnp.concatenate([dz_ref[0, a] for a in range(blocks)], axis=0)
+        acc[:, piece] = contract_lanes(left, wpt[piece, :])
+
+    def build_shifted(m):
+        high = tall[m]
+
+        @pl.loop(0, across)
+        def _(block):
+            whole = ext[m][block].astype(F32)
+            for i in range(3):
+                down = (i - 1) * 36 * m
+                value = whole[high - down : high - down + pair]
+                if i != 1:
+                    same = idrep[block, own : own + pair] == idrep[block, own - down : own - down + pair]
+                    value = jnp.where(wide(same.astype(F32), width) > 0.0, value, 0.0)
+                shifted[i, block] = value.astype(BF16)
+
+    def masked(values, mask):
+        count = values.shape[0] // 48
+        return jnp.concatenate([values[48 * n : 48 * (n + 1)] * mask for n in range(count)], axis=0)
+
+    def scatter_first(n, part):
+        keep[n] = part[:half]
+        send1[n] = part[half:].astype(BF16)
+        stage1(n).start()
+
+    def stage1(n):
+        return pltpu.make_async_remote_copy(
+            src_ref=send1.at[n], dst_ref=recv1.at[n], send_sem=s1send.at[n], recv_sem=s1recv.at[n],
+            device_id=(r + 2 - 4 * z_lo, c), device_id_type=MESH,
+        )
+
+    def stage2(n):
+        return pltpu.make_async_remote_copy(
+            src_ref=relay.at[n], dst_ref=relay.at[n], send_sem=s2send.at[n], recv_sem=s2recv.at[n],
+            device_id=(lax.rem(r + rows // 2, rows), c), device_id_type=MESH,
+        )
+
+    def stage3(n, from_x, slot, target):
+        piece = dw.at[n, pl.ds(pl.multiple_of(from_x * half, half), half)]
+        return pltpu.make_async_remote_copy(
+            src_ref=piece, dst_ref=piece, send_sem=s3send.at[slot, n], recv_sem=s3recv.at[from_x, n],
+            device_id=target, device_id_type=MESH,
+        )
+
+    last = z_hi == k
+    beside = (r, 2 * (1 - x) + k)
+
+    def drain2(start, count):
+        @pl.loop(start, start + count)
+        def _(n):
+            stage1(n).wait_recv()
+            total = keep[n] + recv1[n].astype(F32)
+
+            @pl.when(last)
+            def _():
+                keep[n] = total
+
+            @pl.when(jnp.logical_not(last))
+            def _():
+                relay[n] = total.astype(BF16)
+                stage2(n).start()
+
+    def drain3(start, count):
+        @pl.when(last)
+        def _():
+            @pl.loop(start, start + count)
+            def _(n):
+                stage2(n).wait_recv()
+                dw[n, pl.ds(pl.multiple_of(x * half, half), half)] = (keep[n] + relay[n].astype(F32)).astype(BF16)
+                stage3(n, x, 0, beside).start()
+                stage3(n, x, 1, sibling).start()
+
+    def drain4(start, count):
+        @pl.when(last)
+        def _():
+            @pl.loop(start, start + count)
+            def _(n):
+                copy = stage3(n, 1 - x, 2, sibling)
+                copy.wait_recv()
+                copy.start()
+
+        @pl.when(jnp.logical_not(last))
+        def _():
+            @pl.loop(start, start + count)
+            def _(n):
+                stage3(n, 0, 0, sibling).wait_recv()
+                stage3(n, 1, 0, sibling).wait_recv()
+
+    def weight_grad(m):
+        @pl.loop(0, 9)
+        def _(tap):
+            i, j = tap // 3, lax.rem(tap, 3)
+            shift = (j - 1) * m
+
+            @pl.loop(0, across)
+            def _(block):
+                source = lax.rem(block - shift + across, across)
+                gmat[pl.ds(pl.multiple_of(block * pair, 16), pair)] = masked(
+                    shifted[i, source], colmask[REACH + shift, block]
+                )
+
+            scatter_first((m - 1) * 9 + tap, jnp.dot(xt[...], gmat[...], preferred_element_type=F32))
+
+    def feature_grad(m):
+        for i in range(3):
+            n = (m - 1) * 3 + i
+            slot = n % 2
+            for j in range(3):
+                shift = (j - 1) * m
+                for a in range(blocks):
+                    block = c * blocks + a
+                    source = lax.rem(block - shift + across, across)
+                    gown[a * rb : (a + 1) * rb, j * width : (j + 1) * width] = masked(
+                        shifted[i, source, pl.ds(pl.multiple_of(y * rb, 16), rb)], colmask[REACH + shift, block]
+                    )
+            for j in range(3):
+                weight_copy(jnp.int32(n), j).wait()
+
+            @pl.loop(0, wbuf.shape[1] // 256)
+            def _(chunk):
+                piece = pl.ds(pl.multiple_of(chunk * 256, 256), 256)
+                acc[:, piece] += contract_lanes(gown[...], wbuf[slot, piece, :])
+
+            if n + 2 < 9:
+                for j in range(3):
+                    weight_copy(jnp.int32(n + 2), j).start()
+
+    forward(1)
+    start_branch(3)
+    start_rims(3)
+    finish_gather(1)
+    build_shifted(1)
+    weight_grad(1)
+    forward(2)
+    start_branch(0)
+    feature_grad(1)
+    drain2(0, 9)
+    finish_gather(2)
+    build_shifted(2)
+    weight_grad(2)
+    forward(3)
+    forward(0)
+    feature_grad(2)
+    drain3(0, 9)
+    drain2(9, 9)
+    finish_gather(3)
+    build_shifted(3)
+    weight_grad(3)
+    finish_gather(0)
+
+    @pl.loop(0, across)
+    def _(block):
+        gmat[pl.ds(pl.multiple_of(block * pair, 16), pair)] = ext0[block]
+
+    scatter_first(27, jnp.dot(xt[...], gmat[...], preferred_element_type=F32))
+    drain4(0, 9)
+    drain3(9, 9)
+
+    pool_cols.finish()
+    pool_rows = Exchange(rows, r, lambda other: (other, c), prbuf, prsend, prrecv)
+    prbuf[r] = pool_cols.total()
+    pool_rows.start()
+    feature_grad(3)
+    drain2(18, 10)
+    drain4(9, 9)
+    pool_rows.finish()
+    normed = pooln_ref[...]
+    grad = pool_rows.total() * pools_ref[...]
+    shift_sum = jnp.sum(grad, axis=0, keepdims=True)
+    gain_sum = jnp.sum(grad * normed, axis=0, keepdims=True)
+    gain = gain_ref[4:5]
+    grad_z = (
+        stat_ref[10:11]
+        * (grad * gain - gain * shift_sum / image_count - normed * (gain * gain_sum / image_count))
+    ).astype(BF16)
+    gpool_ref[...] = contract_rows(pooled_ref[...], grad_z)
+    gstat_ref[...] = jnp.concatenate([shift_sum, gain_sum] + [jnp.zeros((1, width), F32)] * 6, axis=0)
+    own_ids = jnp.concatenate([idrep[c * blocks + a, own : own + pair] for a in range(blocks)], axis=0)
+    upper_row = jnp.broadcast_to((y == 0).astype(F32), (pixels, 128))
+    own_ids = jnp.where(
+        upper_row > 0.0,
+        jnp.concatenate([own_ids[a * pair : a * pair + rb] for a in range(blocks)], axis=0),
+        jnp.concatenate([own_ids[a * pair + rb : (a + 1) * pair] for a in range(blocks)], axis=0),
+    )
+    lanes = lax.broadcasted_iota(jnp.int32, (pixels, 128), 1).astype(F32)
+    one_hot = (own_ids == lanes).astype(F32).astype(BF16)
+    counts = wide(counts_ref[...], 256)
+
+    @pl.loop(0, wpl_ref.shape[0] // 256)
+    def _(n):
+        piece = pl.ds(pl.multiple_of(n * 256, 256), 256)
+        back = contract_lanes(grad_z, wpl_ref[piece, :]) / counts
+        back = jnp.concatenate([back, jnp.zeros((128 - images, 256), F32)], axis=0).astype(BF16)
+        gx_ref[:, piece] = (acc[:, piece] + jnp.dot(one_hot, back, preferred_element_type=F32)).astype(BF16)
+
+    drain3(18, 10)
+    drain4(18, 10)
+    result = pltpu.make_async_copy(dw, dw_ref, outsem)
+    result.start()
+
+    for m in (1, 2, 3):
+        pl.when(sends_rim)(rim_copy(m, True).wait_send)
+    for m in (1, 2, 3, 0):
+        finish_sends(m)
+
+    @pl.loop(0, 28)
+    def _(n):
+        stage1(n).wait_send()
+
+        @pl.when(last)
+        def _():
+            stage3(n, x, 0, beside).wait_send()
+            stage3(n, x, 1, sibling).wait_send()
+            stage3(n, 1 - x, 2, sibling).wait_send()
+
+        @pl.when(jnp.logical_not(last))
+        def _():
+            stage2(n).wait_send()
+
+    result.wait()
+
+
+def backward_call(
+    rows, cols, image_count, dz, xsub, ids, wat, wpt, wpl, gain, counts, pooled, pooln, pools, dap, stat
+):
+    _, blocks, rb, width = dz.shape
+    channels = wpt.shape[0]
+    share = channels // rows
+    pair, across, pixels = 2 * rb, cols * blocks, blocks * rb
+    images = dap.shape[0]
+    group = pair * across
+    vmem = pl.BlockSpec(memory_space=pltpu.VMEM)
+    hbm = pl.BlockSpec(memory_space=pl.ANY)
+    dma = pltpu.SemaphoreType.DMA
+    taps = 28
+
+    def ext(high):
+        return pltpu.VMEM((across, 2 * high + pair, width), BF16)
+
+    return pl.pallas_call(
+        functools.partial(backward_kernel, rows, cols, float(image_count), rb),
+        out_shape=(
+            jax.ShapeDtypeStruct((pixels, channels), BF16),
+            jax.ShapeDtypeStruct((taps, share, width), BF16),
+            jax.ShapeDtypeStruct((share, width), F32),
+            jax.ShapeDtypeStruct((8, width), F32),
+        ),
+        in_specs=[vmem, hbm, vmem, hbm, hbm] + [vmem] * 8,
+        out_specs=(vmem, hbm, vmem, vmem),
+        scratch_shapes=[
+            ext(0), ext(HALO[1]), ext(HALO[2]), ext(HALO[3]),
+            pltpu.VMEM((3, across, pair, width), BF16),
+            pltpu.VMEM((2 * REACH + 1, across, 48, width), BF16),
+            pltpu.VMEM((across, ids.shape[0], 128), F32),
+            pltpu.VMEM((group, width), BF16),
+            pltpu.VMEM((pixels, 3 * width), BF16),
+            pltpu.VMEM((2, group, share // 2), BF16),
+            pltpu.VMEM((share, group), BF16),
+            pltpu.VMEM((pixels, channels), F32),
+            pltpu.VMEM((2, channels, 3 * width), BF16),
+            pltpu.VMEM((channels, width), BF16),
+            pltpu.VMEM((taps, share // 2, width), BF16),
+            pltpu.VMEM((taps, share // 2, width), BF16),
+            pltpu.VMEM((taps, share // 2, width), F32),
+            pltpu.VMEM((taps, share // 2, width), BF16),
+            pltpu.VMEM((taps, share, width), BF16),
+            pltpu.VMEM((cols, images, width), F32),
+            pltpu.VMEM((rows, images, width), F32),
+            dma((2, 2 * cols, blocks)), dma((2, 3)), dma,
+            dma((4,)), dma((4,)),
+            dma((4, 2, 7)), dma((4, 2, 2 * cols)),
+            dma((taps,)), dma((taps,)),
+            dma((taps,)), dma((taps,)),
+            dma((3, taps)), dma((2, taps)),
+            dma((cols,)), dma((cols,)),
+            dma((rows,)), dma((rows,)),
+            dma,
+        ],
+        compiler_params=pltpu.CompilerParams(
+            collective_id=1, has_side_effects=True, vmem_limit_bytes=64 * 2**20
+        ),
+        cost_estimate=pl.CostEstimate(flops=4 * pixels * channels * width * 28, bytes_accessed=50_000_000, transcendentals=0),
+    )(dz, xsub, ids, wat, wpt, wpl, gain, counts, pooled, pooln, pools, dap, stat)
+
+
 def extended(cells, sides, width):
     for axis, dim in sides:
         count = lax.axis_size(axis)
@@ -753,60 +1259,35 @@
         (image_ids.reshape(-1, 1) == jnp.arange(images, dtype=jnp.int32)[None, :]).astype(F32), axis=0
     )
     counts = jnp.maximum(counts, 1.0)
+    count_table = jnp.broadcast_to(counts[:, None], (images, 128))
     x = to_blocks(features)
     cot = to_blocks(cotangent)
     output, dz, proj_term, stats, pooled, pool_normed, pool_slope, dap, xsub = forward_call(
         rows, cols, image_count, x, id_columns(window), w_atrous, w_point, w_pool, w_proj,
-        norm_gain, norm_shift, cot, jnp.broadcast_to(counts[:, None], (images, 128)),
+        norm_gain, norm_shift, cot, count_table,
     )
     output = from_blocks(output, rows_here, cols_here)
-    flattened = features.reshape(pixels, channels)
-    grad_branch = dz.reshape(4, cols_here // STEP, rows_here, STEP, branch_width).transpose(2, 1, 3, 0, 4).reshape(pixels, 4, branch_width)
-    image_grads = lax.psum(dap, ("rows", "cols"))
-    grad_pool_pre = image_grads * pool_slope
-    pool_shift = jnp.sum(grad_pool_pre, axis=0)
-    pool_gain = jnp.sum(grad_pool_pre * pool_normed, axis=0)
-    grad_pool_z = (
-        stats[10]
-        * (
-            grad_pool_pre * norm_gain[4]
-            - norm_gain[4] * pool_shift / image_count
-            - pool_normed * (norm_gain[4] * pool_gain / image_count)
-        )
-    ).astype(BF16)
-    grad_pool = contract_rows(pooled, grad_pool_z)
-    grad_pooled = contract_lanes(grad_pool_z, w_pool) / counts[:, None]
-    one_hot = (own_flat[:, None] == jnp.arange(images, dtype=jnp.int32)[None, :]).astype(BF16)
-    grad_input = jnp.dot(one_hot, grad_pooled.astype(BF16), preferred_element_type=F32)
-    grad_input = grad_input + contract_lanes(grad_branch[:, 0], w_point)
-    point_term = contract_rows(flattened, grad_branch[:, 0])
-    stacked = grad_branch[:, 1:].reshape(rows_here, cols_here, 3 * branch_width)
-    grad_padded = extended(stacked, (("rows", 0), ("cols", 1)), margin)
-    terms = []
-    for branch, dilation in enumerate((RATE_LOW, RATE_MID, RATE_TOP)):
-        for stencil in range(9):
-            row_shift = (stencil // 3 - 1) * dilation
-            col_shift = (stencil % 3 - 1) * dilation
-            incoming = grad_padded[
-                margin - row_shift : margin - row_shift + rows_here,
-                margin - col_shift : margin - col_shift + cols_here,
-                branch * branch_width : (branch + 1) * branch_width,
-            ].reshape(pixels, branch_width)
-            same = image_match(window, own_ids, margin - row_shift, margin - col_shift)
-            masked = jnp.where(same > 0, incoming, jnp.zeros((), BF16))
-            grad_input = grad_input + contract_lanes(masked, w_atrous[branch, stencil])
-            terms.append(contract_rows(flattened, masked))
-    atrous_term = jnp.stack(terms).reshape(3, 9, channels, branch_width)
+    pair_window = lax.dynamic_slice(
+        id_padded,
+        (row_index // 2 * (2 * rows_here), jnp.int32(margin)),
+        (2 * rows_here + 2 * margin, grid_cols),
+    )
+    grad_input, weights, grad_pool, pool_sums = backward_call(
+        rows, cols, image_count, dz, xsub.reshape(2, 8, 4, pixels // 4, -1), id_columns(pair_window), w_atrous, w_point, w_pool,
+        norm_gain, count_table, pooled, pool_normed, pool_slope, dap, stats,
+    )
+    weights = weights.astype(F32)
+    grad_atrous = weights[:27].reshape(3, 9, channels // rows, branch_width)
 
     def shared(term, dim):
         part = lax.psum_scatter(term.astype(BF16), "rows", scatter_dimension=dim, tiled=True)
         return lax.psum(part, "cols").astype(F32)
 
-    grad_gain = jnp.concatenate([stats[4:8], pool_gain[None], stats[9:10]], axis=0)
-    grad_shift = jnp.concatenate([stats[0:4], pool_shift[None], stats[8:9]], axis=0)
-    grad_features = grad_input.astype(BF16).reshape(rows_here, cols_here, channels)
+    grad_gain = jnp.concatenate([stats[4:8], pool_sums[1:2], stats[9:10]], axis=0)
+    grad_shift = jnp.concatenate([stats[0:4], pool_sums[0:1], stats[8:9]], axis=0)
+    grad_features = from_blocks(grad_input, rows_here, cols_here)
     return (
-        output, grad_features, shared(point_term, 0), shared(atrous_term, 2), grad_pool,
+        output, grad_features, weights[27], grad_atrous, grad_pool,
         shared(proj_term, 0), grad_gain, grad_shift,
     )
 

time: 861 us -> 338 us (0.39)
  waiting for transfers between devices: 370 us -> 12.9 us
  matrix products: 166 us -> 0 us
  Pallas kernels: 126 us -> 275 us
  local copies, waits for them, and re-layouts: 86.6 us -> 28.9 us
  blocking collectives: 55.3 us -> 0 us
  other arithmetic: 24 us -> 6.46 us
  starting transfers between devices: 11.7 us -> 0.08 us
    reduce_scatter x3 -> x1, waiting for transfers between devices: 309 us -> 0.01 us  [shared(): lax.psum_scatter(term.astype(BF16), 'rows', scatter_dimension=dim, tiled=...]
    dot_general x58 -> x0, matrix products: 166 us -> none  [the longest x28 131 us: contract_lanes(): lax.dot_general(left, right, (((1,), (1,)), ((), ())), preferred_element_...]
    pallas_call x0 -> x1, Pallas kernels: none -> 148 us  [backward_call(): pl.pallas_call(functools.partial(backward_kernel, rows, cols, float(image...]
    psum x1 -> x0, blocking collectives: 55.3 us -> none  [quick_shards(): image_grads = lax.psum(dap, ('rows', 'cols'))]
    convert_element_type x1 -> x0, local copies, waits for them, and re-layouts: 36.7 us -> none  [shared(): term.astype(BF16)]
    ppermute x4 -> x0, waiting for transfers between devices: 24.4 us -> none  [the longest x2 24.4 us: extended(): lax.ppermute(tail, axis, [(i, (i + 1) % count) for i in range(ends)])]
    psum x1, waiting for transfers between devices: 37.1 us -> 12.8 us  [shared(): return lax.psum(part, 'cols').astype(F32)]
    unnamed x160 -> x13, local copies, waits for them, and re-layouts: 19.5 us -> 8.17 us
  transfers between devices with their start and end apart: 8 -> 2, of which waited for: 3 -> 1; matrix products, arithmetic and copies ran while one was open for 28% -> 6% of each run, Pallas kernels for 0% -> 44%
where the time goes in v2:
time: 338 us; the launch traced here: 337 us
  Pallas kernels  275 us (81%)
  local copies, waits for them, and re-layouts  28.9 us (9%)
  between operations  14.2 us (4%)
  waiting for transfers between devices  12.9 us (4%)
  other arithmetic  6.46 us (2%)
    pallas_call x1, Pallas kernels, backward_call(): pl.pallas_call(functools.partial(backward_kernel, rows, cols, float(image...  148 us
    pallas_call x1, Pallas kernels, forward_call(): pl.pallas_call(functools.partial(forward_kernel, rows, cols, float(image_...  126 us
    psum x1, waiting for transfers between devices, shared(): return lax.psum(part, 'cols').astype(F32)  12.8 us
    unnamed x13, local copies, waits for them, and re-layouts  8.17 us
  transfers between devices with their start and end apart: 2, of which 1 were waited for; matrix products, arithmetic and copies ran while one was open for 6% of the time, Pallas kernels for 44%

profile of v2, /device:TPU:0, one launch (start us, length us, event | category | flops | bytes accessed | tf_op | source)
XLA Modules:
  0.0 337.1 jit_solution(3295678955286365967)
XLA Ops:
  7.2 0.0 reduce-scatter.2.cloned.1.call-start
  7.2 1.0 eq.15
  8.2 0.9 fusion.1
  9.1 0.1 copy.38
  9.2 0.2 copy.49
  9.4 0.4 convert_reduce_fusion
  9.9 3.0 copy.36
  12.8 1.3 copy.37
  14.2 2.4 reshape.60.x_ref
  16.6 1.0 copy.41
  17.6 0.1 copy.42
  17.7 0.8 reshape.62.cot_ref
  18.5 0.7 pad.13.ids_ref
  19.2 0.7 broadcast_in_dim.2.counts_ref
  19.9 0.0 copy-start
  19.9 126.4 %shard_map.152 = (bf16[576,256]{1,0:T(8,128)(2,1)}, bf16[4,4,144,256]{3,2,1,0:T(8,128)(2,1)}, bf16[1280,256]{1,0:T(8,128)(2,1)}, f32[16,256]{1,0:T(8,128)}, bf16...) custom-call(bf16[576,2048]{1,0:T(8,128)(2,1)} %reshape.60.x_ref, ...), custom_call_target="tpu_custom_call" | custom-call | flops 16911433728 | bytes 40000000 | tf_op jit(solution)/shard_map/pallas_call | solution.py:438
  146.2 0.0 reduce-scatter.2.cloned.1.call-update
  146.3 0.0 all-reduce.5.cloned.1.call-start
  146.3 0.0 copy-done
  146.4 0.1 copy.44
  146.5 0.2 copy.45
  146.7 0.7 pad.14.ids_ref
  147.5 148.2 %shard_map.153 = (bf16[576,2048]{1,0:T(8,128)(2,1)}, bf16[28,256,256]{2,1,0:T(8,128)(2,1)}, f32[256,256]{1,0:T(8,128)}, f32[8,256]{1,0:T(8,128)}) custom-call(bf16[4,4,144,256]{3,2,1,0:T(8,128)(2,1)} %get-tuple-element.22.dz_ref, bf16[2,8,4,144,128]{4,3,2,1,0:T(8,128)(2,1)} %bitcast.29, f32[504,128]{1,0:T(8,128)} %pad.14.ids_ref, ...), custom_call_target="tpu_custom_call" | custom-call | flops 33822867456 | bytes 50000000 | tf_op jit(solution)/shard_map/pallas_call | solution.py:948
  295.7 0.0 copy-start.3
  295.7 3.0 convert_element_type.46
  298.6 0.0 copy-done.3
  298.6 0.8 fusion.4
  299.4 0.7 slice_bitcast_fusion
  300.1 0.0 reduce-scatter.2.cloned.1.call-done
  300.1 0.0 all-reduce.5.cloned.1.call-update
  300.2 0.6 pad_maximum_fusion
  300.8 5.8 %slice.33 = f32[27,256,256]{2,1,0:T(8,128)} slice(bf16[28,256,256]{2,1,0:T(8,128)(2,1)} %get-tuple-element.30), slice={[0:27], [0:256], [0:256]} | slice | bytes 14155776 | tf_op jit(solution)/shard_map/slice | solution.py:1280
  306.6 3.6 %reshape.66 = bf16[4,24,6,2048]{3,2,1,0:T(8,128)(2,1)S(1)} reshape(bf16[576,2048]{1,0:T(8,128)(2,1)} %get-tuple-element.29) | data formatting | bytes 4718592 | tf_op jit(solution)/shard_map/reshape | solution.py:1227
  310.2 1.3 copy.46
  311.5 0.0 copy-start.1
  311.5 0.0 copy-start.2
  311.5 2.7 copy.48
  314.2 0.0 copy-done.1
  314.2 0.1 reshape.63
  314.3 0.1 copy.43
  314.4 0.8 copy.47
  315.2 12.8 %all-reduce.5.cloned.1.call-done = bf16[160,256]{1,0:T(8,128)(2,1)} async-done(((bf16[160,256]{1,0:T(8,128)(2,1)}), bf16[160,256]{1,0:T(8,128)(2,1)}) %all-reduce.5.cloned.1.call-update) | async-done | bytes 81936 | tf_op jit(solution)/shard_map/psum | solution.py:1284
  328.0 1.6 convert_element_type.47
  329.6 0.0 copy-done.2
  329.6 0.7 copy.53
  (8 shorter events, 0.1 us)
Async XLA Ops:
  7.2 293.0 %reduce-scatter.2.cloned.1.call-start = ((), (), s32[]{:S(2)}) async-start(), calls=%async_computation.1 | async-start | bytes 737280 | tf_op jit(solution)/shard_map/reduce_scatter | solution.py:1283
  19.9 126.5 %copy-start = (s32[192,96]{1,0:T(8,128)S(1)}, s32[192,96]{1,0:T(8,128)}, u32[]{:S(2)}) copy-start(s32[192,96]{1,0:T(8,128)} %param.10) | copy-start | bytes 221188
  146.3 181.7 %all-reduce.5.cloned.1.call-start = ((), (), s32[]{:S(2)}) async-start(), calls=%async_computation.2 | async-start | bytes 163840 | tf_op jit(solution)/shard_map/psum | solution.py:1284
  295.7 3.0 copy-start.3
  311.5 2.7 copy-start.1
  311.5 18.0 %copy-start.2 = (f32[256,256]{1,0:T(8,128)S(1)}, f32[256,256]{1,0:T(8,128)}, u32[]{:S(2)}) copy-start(f32[256,256]{1,0:T(8,128)} %get-tuple-element.70) | copy-start | bytes 786436
Sparse Core Ops, SparseCore 0:
  146.4 73.6 reduce-scatter.1
  300.3 27.6 all-reduce.4

commit v3 on v2

--- a/solution.py
+++ b/solution.py
@@ -1,6 +1,7 @@
 import functools
 import jax
 import jax.numpy as jnp
+import numpy as np
 from jax import lax
 from jax.experimental import pallas as pl
 from jax.experimental.pallas import tpu as pltpu
@@ -67,7 +68,7 @@
         for step in range(1, self.size):
             self.copy(step, source).start()
 
-    def finish(self, source=None):
+    def arrive(self):
         for step in range(1, self.size):
             other = lax.rem(self.place + step, self.size)
             there = self.slots.at[other]
@@ -79,6 +80,8 @@
                 device_id=self.to_device(other),
                 device_id_type=MESH,
             ).wait_recv()
+
+    def leave(self, source=None):
         for step in range(1, self.size):
             self.copy(step, source).wait_send()
 
@@ -91,10 +94,10 @@
 
 def forward_kernel(
     rows, cols, image_count, total_pixels,
-    x_ref, ids_ref, wat_ref, wpt_ref, wpl_ref, wpj_ref, gain_ref, shift_ref, cot_ref, counts_ref,
-    out_ref, dz_ref, pj_ref, stat_ref, pooled_ref, pooln_ref, pools_ref, dap_ref, xsub_ref,
-    idrep, wbuf, wplbuf, ubuf, zx1, zx2, zx3, zs1, zs2, zs3,
-    halo_bufs, zn, slope, joined, zf, dzf, isum, cbuf, rbuf, pr_buf, pc_buf, pz_buf,
+    raw_ref, order_ref, back_ref, ids_ref, wat_ref, wpt_ref, wpl_ref, wpj_ref, gain_ref, shift_ref, cot_ref,
+    counts_ref, out_ref, dz_ref, pj_ref, stat_ref, pooled_ref, pooln_ref, pools_ref, dap_ref, xsub_ref,
+    x_ref, idrep, wbuf, wplbuf, ubuf, zx1, zx2, zx3, zs1, zs2, zs3,
+    halo_bufs, zn, slope, joined, zf, dzf, active, isum, cbuf, rbuf, pr_buf, pc_buf, pz_buf,
     wsem, wplsem, hsend, hrecv, csend, crecv, rsend, rrecv, psend, precv, pcsend, pcrecv, pzsend, pzrecv,
     xsend, xrecv,
 ):
@@ -122,6 +125,11 @@
     for block in range(idrep.shape[0]):
         idrep[block] = jnp.broadcast_to(ids_ref[:, block : block + 1], idrep.shape[1:])
     greet_all(rows, cols, r, c)
+
+    @pl.loop(0, x_ref.shape[1] // 256)
+    def _(n):
+        piece = pl.ds(pl.multiple_of(n * 256, 256), 256)
+        x_ref[:, piece] = jnp.dot(order_ref[...], raw_ref[:, piece], preferred_element_type=F32).astype(BF16)
 
     own_ids = jnp.concatenate([idrep[REACH + a, own : own + rb, :] for a in range(blocks)], axis=0)
     lanes = lax.broadcasted_iota(jnp.int32, (pixels, 128), 1).astype(F32)
@@ -167,7 +175,7 @@
     def inside(dr, dc):
         return (r + dr >= 0) & (r + dr < rows) & (c + dc >= 0) & (c + dc < cols)
 
-    for position, m in enumerate(order):
+    def conv(position, m):
         height = HALO[m]
 
         @pl.loop(0, blocks + 2 * m)
@@ -218,9 +226,6 @@
         def _(a):
             zn[m, a] = zx[m][m + a, height : height + rb]
 
-    product = jnp.dot(x_ref[...], wpt_ref[...], preferred_element_type=F32)
-    for a in range(blocks):
-        zn[0, a] = product[a * rb : (a + 1) * rb]
 
     members = [(dy, dx, dk) for dy in range(2) for dx in range(2) for dk in range(2)]
     half = share // 2
@@ -251,22 +256,27 @@
                     )
         return copies
 
-    for copy in member_copies():
-        copy.start()
-
-    pool_rows.finish(share_of)
     pool_cols = Exchange(cols, c, lambda other: (r, other), pc_buf, pcsend, pcrecv)
+    pool_z = Exchange(rows, r, lambda other: (other, c), pz_buf, pzsend, pzrecv)
+    conv(0, 3)
+    pool_rows.arrive()
     pc_buf[c] = pool_rows.total()
     pool_cols.start()
-    pool_cols.finish()
+    conv(1, 2)
+    pool_cols.arrive()
     counts = counts_ref[...]
     pooled = (pool_cols.total() / wide(counts, share)).astype(BF16)
     pooled_ref[...] = pooled
     pool_weight.wait()
-    pool_z = Exchange(rows, r, lambda other: (other, c), pz_buf, pzsend, pzrecv)
     pz_buf[r] = jnp.dot(pooled, wplbuf[...], preferred_element_type=F32)
     pool_z.start()
-    pool_z.finish()
+    conv(2, 1)
+    product = jnp.dot(x_ref[...], wpt_ref[...], preferred_element_type=F32)
+    for a in range(blocks):
+        zn[0, a] = product[a * rb : (a + 1) * rb]
+    for copy in member_copies():
+        copy.start()
+    pool_z.arrive()
     zp = pool_z.total()
     pool_avg = jnp.sum(zp, axis=0, keepdims=True) / image_count
     pool_square = jnp.sum(zp * zp, axis=0, keepdims=True) / image_count
@@ -293,15 +303,18 @@
                 for a in range(na):
                     zn[m, a0 + a, r0 : r0 + nr] += halo_bufs[(m - 1) * 8 + place][a].astype(F32)
 
+    started = []
+
     def all_sum(step, value):
         across = Exchange(cols, c, lambda other: (r, other), cbuf.at[step], csend.at[step], crecv.at[step])
         cbuf[step, c] = value
         across.start()
-        across.finish()
+        across.arrive()
         down = Exchange(rows, r, lambda other: (other, c), rbuf.at[step], rsend.at[step], rrecv.at[step])
         rbuf[step, r] = across.total()
         down.start()
-        down.finish()
+        down.arrive()
+        started.extend((across, down))
         return down.total()
 
     zero = jnp.zeros((1, width), F32)
@@ -324,10 +337,10 @@
         @pl.loop(0, blocks)
         def _(a):
             normed = (zn[k, a] - average[k : k + 1]) * inverse[k : k + 1]
-            active, slant = silu_parts(gain_ref[k : k + 1] * normed + shift_ref[k : k + 1])
+            value, slant = silu_parts(gain_ref[k : k + 1] * normed + shift_ref[k : k + 1])
             zn[k, a] = normed
             slope[k, a] = slant
-            joined[pl.ds(pl.multiple_of(a * rb, rb), rb), k * width : (k + 1) * width] = active.astype(BF16)
+            joined[pl.ds(pl.multiple_of(a * rb, rb), rb), k * width : (k + 1) * width] = value.astype(BF16)
 
     zf[...] = jnp.dot(joined[...], wpj_ref[...], preferred_element_type=F32)
     first, second = zero, zero
@@ -338,16 +351,17 @@
     final_avg = moments[0:1] / total_pixels
     final_inverse = lax.rsqrt(moments[1:2] / total_pixels - final_avg * final_avg + epsilon)
     shift_last, gain_last = zero, zero
+    upstream = jnp.dot(order_ref[...], cot_ref[...], preferred_element_type=F32)
     for a in range(blocks):
         piece = slice(a * rb, (a + 1) * rb)
         normed = (zf[piece] - final_avg) * final_inverse
         result, slant = silu_parts(gain_ref[5:6] * normed + shift_ref[5:6])
-        out_ref[piece] = result.astype(BF16)
-        grad = cot_ref[piece].astype(F32) * slant
+        active[piece] = result.astype(BF16)
+        grad = upstream[piece] * slant
         zf[piece] = normed
-        slope_last = grad
-        dzf[piece] = slope_last
+        dzf[piece] = grad
         shift_last, gain_last = shift_last + row_sum(grad), gain_last + row_sum(grad * normed)
+    out_ref[...] = jnp.dot(back_ref[...], active[...], preferred_element_type=F32).astype(BF16)
     sums = all_sum(2, jnp.concatenate([shift_last, gain_last] + [zero] * 6, axis=0))
     shift_last, gain_last = sums[0:1], sums[1:2]
     gain = gain_ref[5:6]
@@ -391,6 +405,9 @@
         pj_ref[piece] = contract_rows(joined[:, piece], grad_final).astype(BF16)
     stat_ref[...] = jnp.concatenate([sums, shift_last, gain_last, pool_inverse] + [zero] * 5, axis=0)
 
+    pool_rows.leave(share_of)
+    for exchange in (pool_cols, pool_z, *started):
+        exchange.leave()
     for m in order:
         for dr, dc, copy in halo_copies(m):
             pl.when(inside(dr, dc))(copy.wait_send)
@@ -417,7 +434,7 @@
 DIRECTIONS = ((-1, 0), (1, 0), (-1, -1), (-1, 1), (1, -1), (1, 1), (0, -1), (0, 1))
 
 
-def forward_call(rows, cols, image_count, x, ids, wat, wpt, wpl, wpj, gain, shift, cot, counts):
+def forward_call(rows, cols, image_count, x, order, back, ids, wat, wpt, wpl, wpj, gain, shift, cot, counts):
     pixels, channels = x.shape
     width = wpt.shape[1]
     blocks, rb = 4, pixels // 4
@@ -448,9 +465,10 @@
             jax.ShapeDtypeStruct((images, width), F32),
             jax.ShapeDtypeStruct((2, 8, pixels, share // 2), BF16),
         ),
-        in_specs=[vmem, vmem, hbm, vmem, hbm, vmem, vmem, vmem, vmem, vmem],
+        in_specs=[vmem, vmem, vmem, vmem, hbm, vmem, hbm, vmem, vmem, vmem, vmem, vmem],
         out_specs=(vmem,) * 8 + (hbm,),
         scratch_shapes=[
+            pltpu.VMEM((pixels, channels), BF16),
             pltpu.VMEM((blocks + 2 * REACH, ids.shape[0], 128), F32),
             pltpu.VMEM((SLOTS, channels, width), BF16),
             pltpu.VMEM((share, width), BF16),
@@ -463,6 +481,7 @@
             pltpu.VMEM((pixels, 5 * width), BF16),
             pltpu.VMEM((pixels, width), F32),
             pltpu.VMEM((pixels, width), F32),
+            pltpu.VMEM((pixels, width), BF16),
             pltpu.VMEM((images, channels), F32),
             pltpu.VMEM((4, cols, 8, width), F32),
             pltpu.VMEM((4, rows, 8, width), F32),
@@ -482,14 +501,14 @@
             collective_id=0, has_side_effects=True, vmem_limit_bytes=60 * 2**20
         ),
         cost_estimate=pl.CostEstimate(flops=2 * pixels * channels * width * 28, bytes_accessed=40_000_000, transcendentals=0),
-    )(x, ids, wat, wpt, wpl, wpj, gain, shift, cot, counts)
+    )(x, order, back, ids, wat, wpt, wpl, wpj, gain, shift, cot, counts)
 
 
 def backward_kernel(
     rows, cols, image_count, height,
     dz_ref, xsub_ref, ids_ref, wat_ref, wpt_ref, wpl_ref, gain_ref, counts_ref,
-    pooled_ref, pooln_ref, pools_ref, dap_ref, stat_ref,
-    gx_ref, dw_ref, gpool_ref, gstat_ref,
+    pooled_ref, pooln_ref, pools_ref, dap_ref, stat_ref, back_ref,
+    gx_ref, dw_ref, dpoint_ref, gpool_ref, gstat_ref,
     ext0, ext1, ext2, ext3, shifted, colmask, idrep, gmat, gown, xall, xt, acc, wbuf, wpt,
     send1, recv1, keep, relay, dw, pcbuf, prbuf,
     xsem, wsem, wptsem, zsend, zrecv, agsend, agrecv, s1send, s1recv, s2send, s2recv, s3send, s3recv,
@@ -509,7 +528,6 @@
     images = dap_ref.shape[0]
     ext = {0: ext0, 1: ext1, 2: ext2, 3: ext3}
     tall = {0: 0, **HALO}
-    directs = ((0, 1), (1, 0), (1, 1))
 
     def x_copy(l, dev, a):
         dev_y, dev_c = dev // cols, lax.rem(dev, cols)
@@ -559,29 +577,27 @@
 
     sends_rim = (y == 1) & (z <= levels - 2) | (y == 0) & (z >= 1)
 
-    def item(m, kind, dev_y, dev_c):
+    def item(m, kind, dev_y, dev_c, first=0, count=None):
         high = tall[m]
-        if kind == 0:
-            return ext[m].at[pl.ds(dev_c * blocks, blocks), pl.ds(pl.multiple_of(high + rb * dev_y, 16), rb)]
-        return ext[m].at[
-            pl.ds(dev_c * blocks, blocks), pl.ds(pl.multiple_of((1 - dev_y) * (high + pair), 16), high)
-        ]
-
-    def gather_copy(m, kind, dev_y, dev_c, slot, target):
-        piece = item(m, kind, dev_y, dev_c)
+        count = blocks if count is None else count
+        start = high + rb * dev_y if kind == 0 else (1 - dev_y) * (high + pair)
+        height = rb if kind == 0 else high
+        return ext[m].at[pl.ds(dev_c * blocks + first, count), pl.ds(pl.multiple_of(start, 16), height)]
+
+    def gather_copy(m, kind, dev_y, dev_c, slot, target, first=0, count=None):
+        piece = item(m, kind, dev_y, dev_c, first, count)
         return pltpu.make_async_remote_copy(
             src_ref=piece,
             dst_ref=piece,
             send_sem=agsend.at[m, kind, slot],
-            recv_sem=agrecv.at[m, kind, dev_y * cols + dev_c],
+            recv_sem=agrecv.at[m, kind, 2 * cols if first else dev_y * cols + dev_c],
             device_id=target,
             device_id_type=MESH,
         )
 
-    sibling = (r, 2 * x + 1 - k)
-
-    def place(dy, dx):
-        return lax.rem(y + dy, 2), 2 * lax.rem(x + dx, 2) + k
+    most = blocks - 1
+    side = 2 * (1 - x) + k
+    sibling, beside, below = (r, 2 * x + 1 - k), (r, side), (2 * z + 1 - y, c)
 
     def if_there(kind, dev_y, action):
         if kind == 0:
@@ -592,73 +608,83 @@
     def kinds(m):
         return (0,) if m == 0 else (0, 1)
 
-    def first_copies(m, kind):
-        copies = []
-        for slot, (dy, dx) in enumerate(directs):
-            dev_y, dev_c = place(dy, dx)
-            copies.append(gather_copy(m, kind, y, c, slot, (2 * z + dev_y, dev_c)))
-        copies.append(gather_copy(m, kind, y, c, 3, sibling))
-        return copies
-
-    def start_first(m, kind):
+    def own_copies(m, kind):
+        return [gather_copy(m, kind, y, c, slot, to) for slot, to in enumerate((beside, below, sibling))]
+
+    def side_copies(m, kind):
+        return [gather_copy(m, kind, y, side, 3, below, 0, most), gather_copy(m, kind, y, side, 5, sibling)]
+
+    def below_copies(m, kind):
+        return [
+            gather_copy(m, kind, 1 - y, c, 4, beside, most, blocks - most),
+            gather_copy(m, kind, 1 - y, c, 6, sibling),
+        ]
+
+    def diagonal_copies(m, kind):
+        return [gather_copy(m, kind, 1 - y, side, 7, sibling)]
+
+    def start_own(m, kind):
+        if kind == 0:
+            high = tall[m]
+            for a in range(blocks):
+                ext[m][c * blocks + a, pl.ds(pl.multiple_of(high + rb * y, 16), rb)] = dz_ref[m, a]
+
         def action():
-            for copy in first_copies(m, kind):
+            if kind == 1:
+                rim_copy(m, False).wait_recv()
+            for copy in own_copies(m, kind):
                 copy.start()
 
         if_there(kind, y, action)
 
-    def forward(m):
+    def pass_on(m):
         for kind in kinds(m):
-            for slot, (dy, dx) in enumerate(directs):
-                dev_y, dev_c = place(dy, dx)
-
-                def action():
-                    copy = gather_copy(m, kind, dev_y, dev_c, 4 + slot, sibling)
-                    copy.wait_recv()
+            def from_side():
+                gather_copy(m, kind, y, side, 0, beside).wait_recv()
+                for copy in side_copies(m, kind):
                     copy.start()
 
-                if_there(kind, dev_y, action)
+            def from_below():
+                gather_copy(m, kind, 1 - y, c, 0, below).wait_recv()
+                for copy in below_copies(m, kind):
+                    copy.start()
+
+            if_there(kind, y, from_side)
+            if_there(kind, 1 - y, from_below)
+
+    def pass_last(m):
+        for kind in kinds(m):
+            def action():
+                gather_copy(m, kind, 1 - y, side, 0, below, 0, most).wait_recv()
+                gather_copy(m, kind, 1 - y, side, 0, beside, most, blocks - most).wait_recv()
+                for copy in diagonal_copies(m, kind):
+                    copy.start()
+
+            if_there(kind, 1 - y, action)
 
     def finish_gather(m):
         for kind in kinds(m):
-            for dy, dx in ((0, 0),) + directs:
-                dev_y, dev_c = place(dy, dx)
-                dev_c = dev_c + 1 - 2 * k
-                if_there(kind, dev_y, lambda: gather_copy(m, kind, dev_y, dev_c, 0, sibling).wait_recv())
+            for dev_y in (y, 1 - y):
+                for dev_c in (c, side):
+                    piece = gather_copy(m, kind, dev_y, dev_c + 1 - 2 * k, 0, sibling)
+                    if_there(kind, dev_y, piece.wait_recv)
 
     def finish_sends(m):
         for kind in kinds(m):
             def action():
-                for copy in first_copies(m, kind):
+                for copy in own_copies(m, kind) + side_copies(m, kind):
                     copy.wait_send()
 
+            def below_action():
+                for copy in below_copies(m, kind) + diagonal_copies(m, kind):
+                    copy.wait_send()
+
             if_there(kind, y, action)
-            for slot, (dy, dx) in enumerate(directs):
-                dev_y, dev_c = place(dy, dx)
-                if_there(
-                    kind, dev_y, lambda: gather_copy(m, kind, dev_y, dev_c, 4 + slot, sibling).wait_send()
-                )
-
-    def start_branch(m):
-        high = tall[m]
-        for a in range(blocks):
-            ext[m][c * blocks + a, pl.ds(pl.multiple_of(high + rb * y, 16), rb)] = dz_ref[m, a]
-        start_first(m, 0)
-
-    def start_rims(m):
-        def action():
-            rim_copy(m, False).wait_recv()
-            for copy in first_copies(m, 1):
-                copy.start()
-
-        pl.when(has_rim(y))(action)
+            if_there(kind, 1 - y, below_action)
 
     for m in (1, 2, 3):
         pl.when(sends_rim)(rim_copy(m, True).start)
-    start_branch(1)
-    start_rims(1)
-    start_branch(2)
-    start_rims(2)
+    start_own(1, 0)
 
     pool_cols = Exchange(cols, c, lambda other: (r, other), pcbuf, pcsend, pcrecv)
     pcbuf[c] = dap_ref[...]
@@ -689,6 +715,8 @@
             else:
                 colmask[REACH + shift, block] = jnp.zeros((48, width), BF16)
 
+    start_own(1, 1)
+    start_own(2, 0)
     for l in range(2):
         for a in range(blocks):
             @pl.loop(0, 2 * cols)
@@ -700,6 +728,8 @@
             piece = slice(chunk * 128, (chunk + 1) * 128)
             xt[pl.ds(spot, half), piece] = xall[l, piece, :].astype(F32).T.astype(BF16)
 
+    pass_on(1)
+
     point_copy.wait()
 
     @pl.loop(0, wpt.shape[0] // 256)
@@ -707,6 +737,9 @@
         piece = pl.ds(pl.multiple_of(n * 256, 256), 256)
         left = jnp.concatenate([dz_ref[0, a] for a in range(blocks)], axis=0)
         acc[:, piece] = contract_lanes(left, wpt[piece, :])
+
+    pool_copy = pltpu.make_async_copy(wpl_ref, wpt, wptsem)
+    pool_copy.start()
 
     def build_shifted(m):
         high = tall[m]
@@ -751,7 +784,6 @@
         )
 
     last = z_hi == k
-    beside = (r, 2 * (1 - x) + k)
 
     def drain2(start, count):
         @pl.loop(start, start + count)
@@ -809,8 +841,8 @@
 
             scatter_first((m - 1) * 9 + tap, jnp.dot(xt[...], gmat[...], preferred_element_type=F32))
 
-    def feature_grad(m):
-        for i in range(3):
+    def feature_grad(m, lines):
+        for i in lines:
             n = (m - 1) * 3 + i
             slot = n % 2
             for j in range(3):
@@ -833,24 +865,30 @@
                 for j in range(3):
                     weight_copy(jnp.int32(n + 2), j).start()
 
-    forward(1)
-    start_branch(3)
-    start_rims(3)
+    pass_last(1)
+    start_own(2, 1)
+    start_own(3, 0)
     finish_gather(1)
     build_shifted(1)
     weight_grad(1)
-    forward(2)
-    start_branch(0)
-    feature_grad(1)
+    pass_on(2)
+    feature_grad(1, (0, 1))
+    pass_last(2)
+    start_own(3, 1)
+    start_own(0, 0)
+    feature_grad(1, (2,))
     drain2(0, 9)
     finish_gather(2)
     build_shifted(2)
     weight_grad(2)
-    forward(3)
-    forward(0)
-    feature_grad(2)
+    pass_on(3)
+    feature_grad(2, (0, 1))
+    pass_last(3)
+    pass_on(0)
+    feature_grad(2, (2,))
     drain3(0, 9)
     drain2(9, 9)
+    pass_last(0)
     finish_gather(3)
     build_shifted(3)
     weight_grad(3)
@@ -864,14 +902,14 @@
     drain4(0, 9)
     drain3(9, 9)
 
-    pool_cols.finish()
+    pool_cols.arrive()
     pool_rows = Exchange(rows, r, lambda other: (other, c), prbuf, prsend, prrecv)
     prbuf[r] = pool_cols.total()
     pool_rows.start()
-    feature_grad(3)
+    feature_grad(3, (0, 1, 2))
     drain2(18, 10)
     drain4(9, 9)
-    pool_rows.finish()
+    pool_rows.arrive()
     normed = pooln_ref[...]
     grad = pool_rows.total() * pools_ref[...]
     shift_sum = jnp.sum(grad, axis=0, keepdims=True)
@@ -893,19 +931,27 @@
     lanes = lax.broadcasted_iota(jnp.int32, (pixels, 128), 1).astype(F32)
     one_hot = (own_ids == lanes).astype(F32).astype(BF16)
     counts = wide(counts_ref[...], 256)
-
-    @pl.loop(0, wpl_ref.shape[0] // 256)
+    pool_copy.wait()
+
+    @pl.loop(0, wpt.shape[0] // 256)
     def _(n):
         piece = pl.ds(pl.multiple_of(n * 256, 256), 256)
-        back = contract_lanes(grad_z, wpl_ref[piece, :]) / counts
+        back = contract_lanes(grad_z, wpt[piece, :]) / counts
         back = jnp.concatenate([back, jnp.zeros((128 - images, 256), F32)], axis=0).astype(BF16)
-        gx_ref[:, piece] = (acc[:, piece] + jnp.dot(one_hot, back, preferred_element_type=F32)).astype(BF16)
+        value = (acc[:, piece] + jnp.dot(one_hot, back, preferred_element_type=F32)).astype(BF16)
+        gx_ref[:, piece] = jnp.dot(back_ref[...], value, preferred_element_type=F32).astype(BF16)
 
     drain3(18, 10)
     drain4(18, 10)
-    result = pltpu.make_async_copy(dw, dw_ref, outsem)
-    result.start()
-
+    results = (
+        pltpu.make_async_copy(dw.at[pl.ds(0, 27)], dw_ref, outsem.at[0]),
+        pltpu.make_async_copy(dw.at[27], dpoint_ref, outsem.at[1]),
+    )
+    for result in results:
+        result.start()
+
+    pool_cols.leave()
+    pool_rows.leave()
     for m in (1, 2, 3):
         pl.when(sends_rim)(rim_copy(m, True).wait_send)
     for m in (1, 2, 3, 0):
@@ -925,11 +971,12 @@
         def _():
             stage2(n).wait_send()
 
-    result.wait()
+    for result in results:
+        result.wait()
 
 
 def backward_call(
-    rows, cols, image_count, dz, xsub, ids, wat, wpt, wpl, gain, counts, pooled, pooln, pools, dap, stat
+    rows, cols, image_count, dz, xsub, ids, wat, wpt, wpl, gain, counts, pooled, pooln, pools, dap, stat, back
 ):
     _, blocks, rb, width = dz.shape
     channels = wpt.shape[0]
@@ -949,12 +996,13 @@
         functools.partial(backward_kernel, rows, cols, float(image_count), rb),
         out_shape=(
             jax.ShapeDtypeStruct((pixels, channels), BF16),
-            jax.ShapeDtypeStruct((taps, share, width), BF16),
+            jax.ShapeDtypeStruct((taps - 1, share, width), BF16),
+            jax.ShapeDtypeStruct((share, width), BF16),
             jax.ShapeDtypeStruct((share, width), F32),
             jax.ShapeDtypeStruct((8, width), F32),
         ),
-        in_specs=[vmem, hbm, vmem, hbm, hbm] + [vmem] * 8,
-        out_specs=(vmem, hbm, vmem, vmem),
+        in_specs=[vmem, hbm, vmem, hbm, hbm, hbm] + [vmem] * 8,
+        out_specs=(vmem, hbm, hbm, vmem, vmem),
         scratch_shapes=[
             ext(0), ext(HALO[1]), ext(HALO[2]), ext(HALO[3]),
             pltpu.VMEM((3, across, pair, width), BF16),
@@ -976,19 +1024,19 @@
             pltpu.VMEM((rows, images, width), F32),
             dma((2, 2 * cols, blocks)), dma((2, 3)), dma,
             dma((4,)), dma((4,)),
-            dma((4, 2, 7)), dma((4, 2, 2 * cols)),
+            dma((4, 2, 8)), dma((4, 2, 2 * cols + 1)),
             dma((taps,)), dma((taps,)),
             dma((taps,)), dma((taps,)),
             dma((3, taps)), dma((2, taps)),
             dma((cols,)), dma((cols,)),
             dma((rows,)), dma((rows,)),
-            dma,
+            dma((2,)),
         ],
         compiler_params=pltpu.CompilerParams(
             collective_id=1, has_side_effects=True, vmem_limit_bytes=64 * 2**20
         ),
         cost_estimate=pl.CostEstimate(flops=4 * pixels * channels * width * 28, bytes_accessed=50_000_000, transcendentals=0),
-    )(dz, xsub, ids, wat, wpt, wpl, gain, counts, pooled, pooln, pools, dap, stat)
+    )(dz, xsub, ids, wat, wpt, wpl, gain, counts, pooled, pooln, pools, dap, stat, back)
 
 
 def extended(cells, sides, width):
@@ -1216,16 +1264,9 @@
     )
 
 
-def to_blocks(cells):
-    height, breadth, depth = cells.shape
-    cells = cells.reshape(height, breadth // STEP, STEP, depth)
-    return cells.transpose(1, 0, 2, 3).reshape(height * breadth, depth)
-
-
-def from_blocks(cells, height, breadth):
-    depth = cells.shape[-1]
-    cells = cells.reshape(breadth // STEP, height, STEP, depth)
-    return cells.transpose(1, 0, 2, 3).reshape(height, breadth, depth)
+def block_order(height, breadth):
+    pixel = np.arange(height * breadth).reshape(height, breadth // STEP, STEP).transpose(1, 0, 2).reshape(-1)
+    return np.eye(height * breadth, dtype=np.float32)[pixel]
 
 
 def id_columns(ids):
@@ -1260,35 +1301,33 @@
     )
     counts = jnp.maximum(counts, 1.0)
     count_table = jnp.broadcast_to(counts[:, None], (images, 128))
-    x = to_blocks(features)
-    cot = to_blocks(cotangent)
+    order = block_order(rows_here, cols_here)
+    order, back = jnp.asarray(order, BF16), jnp.asarray(order.T, BF16)
     output, dz, proj_term, stats, pooled, pool_normed, pool_slope, dap, xsub = forward_call(
-        rows, cols, image_count, x, id_columns(window), w_atrous, w_point, w_pool, w_proj,
-        norm_gain, norm_shift, cot, count_table,
-    )
-    output = from_blocks(output, rows_here, cols_here)
+        rows, cols, image_count, features.reshape(pixels, channels), order, back, id_columns(window), w_atrous, w_point, w_pool, w_proj,
+        norm_gain, norm_shift, cotangent.reshape(pixels, branch_width), count_table,
+    )
+    output = output.reshape(rows_here, cols_here, branch_width)
     pair_window = lax.dynamic_slice(
         id_padded,
         (row_index // 2 * (2 * rows_here), jnp.int32(margin)),
         (2 * rows_here + 2 * margin, grid_cols),
     )
-    grad_input, weights, grad_pool, pool_sums = backward_call(
+    grad_input, atrous, point, grad_pool, pool_sums = backward_call(
         rows, cols, image_count, dz, xsub.reshape(2, 8, 4, pixels // 4, -1), id_columns(pair_window), w_atrous, w_point, w_pool,
-        norm_gain, count_table, pooled, pool_normed, pool_slope, dap, stats,
-    )
-    weights = weights.astype(F32)
-    grad_atrous = weights[:27].reshape(3, 9, channels // rows, branch_width)
-
-    def shared(term, dim):
-        part = lax.psum_scatter(term.astype(BF16), "rows", scatter_dimension=dim, tiled=True)
-        return lax.psum(part, "cols").astype(F32)
-
+        norm_gain, count_table, pooled, pool_normed, pool_slope, dap, stats, back,
+    )
+    grad_atrous = atrous.astype(F32).reshape(3, 9, channels // rows, branch_width)
+
+    proj_share = proj_term.shape[0] // rows
+    grad_proj = lax.psum(proj_term, ("rows", "cols"))
+    grad_proj = lax.dynamic_slice_in_dim(grad_proj, row_index * proj_share, proj_share, 0).astype(F32)
     grad_gain = jnp.concatenate([stats[4:8], pool_sums[1:2], stats[9:10]], axis=0)
     grad_shift = jnp.concatenate([stats[0:4], pool_sums[0:1], stats[8:9]], axis=0)
-    grad_features = from_blocks(grad_input, rows_here, cols_here)
+    grad_features = grad_input.reshape(rows_here, cols_here, channels)
     return (
-        output, grad_features, weights[27], grad_atrous, grad_pool,
-        shared(proj_term, 0), grad_gain, grad_shift,
+        output, grad_features, point.astype(F32), grad_atrous, grad_pool,
+        grad_proj, grad_gain, grad_shift,
     )
 
 

time: 338 us -> 297 us (0.88)
  local copies, waits for them, and re-layouts: 28.9 us -> 10.1 us
  Pallas kernels: 275 us -> 260 us
  waiting for transfers between devices: 12.9 us -> 0.02 us
  other arithmetic: 6.46 us -> 11.1 us
    psum x1, waiting for transfers between devices: 12.8 us -> 0.01 us  [quick_shards(): grad_proj = lax.psum(proj_term, ('rows', 'cols'))]
    pallas_call x1, Pallas kernels: 148 us -> 138 us  [backward_call(): pl.pallas_call(functools.partial(backward_kernel, rows, cols, float(image...]
    reshape x4 -> x0, local copies, waits for them, and re-layouts: 6.92 us -> none  [the longest x2 3.68 us: from_blocks(): cells = cells.reshape(breadth // STEP, height, STEP, depth)]
    reshape x0 -> x1, other arithmetic: none -> 5.99 us  [quick_shards(): atrous.astype(F32).reshape(3, 9, channels // rows, branch_width)]
    slice x1 -> x0, local copies, waits for them, and re-layouts: 5.84 us -> none  [quick_shards(): grad_atrous = weights[:27].reshape(3, 9, channels // rows, branch_width)]
    unnamed x13 -> x19, local copies, waits for them, and re-layouts: 8.17 us -> 2.85 us
    pallas_call x1, Pallas kernels: 126 us -> 122 us  [forward_call(): pl.pallas_call(functools.partial(forward_kernel, rows, cols, float(image_...]
  transfers between devices with their start and end apart: 2 -> 1, of which waited for: 1 -> 0; matrix products, arithmetic and copies ran while one was open for 6% -> 4% of each run, Pallas kernels for 44% -> 47%
where the time goes in v3:
time: 297 us; the launch traced here: 296 us
  Pallas kernels  260 us (88%)
  between operations  14.2 us (5%)
  other arithmetic  11.1 us (4%)
  local copies, waits for them, and re-layouts  10.1 us (3%)
    pallas_call x1, Pallas kernels, backward_call(): pl.pallas_call(functools.partial(backward_kernel, rows, cols, float(image...  138 us
    pallas_call x1, Pallas kernels, forward_call(): pl.pallas_call(functools.partial(forward_kernel, rows, cols, float(image_...  122 us
    reshape x1, other arithmetic, quick_shards(): atrous.astype(F32).reshape(3, 9, channels // rows, branch_width)  5.99 us
  transfers between devices with their start and end apart: 1, of which 0 were waited for; matrix products, arithmetic and copies ran while one was open for 4% of the time, Pallas kernels for 47%

profile of v3, /device:TPU:0, one launch (start us, length us, event | category | flops | bytes accessed | tf_op | source)
XLA Modules:
  0.0 295.6 jit_solution(1696932797649719517)
XLA Ops:
  7.2 0.0 all-reduce.5.cloned.1.call-start
  7.2 1.0 eq.15
  8.2 0.9 fusion.1
  9.1 0.1 copy.26
  9.2 0.4 convert_reduce_fusion
  9.6 0.2 copy.31
  9.9 0.7 pad.13.ids_ref
  10.6 0.7 broadcast_in_dim.2.counts_ref
  11.2 0.0 copy-start.1
  11.2 122.3 %shard_map.170 = (bf16[576,256]{1,0:T(8,128)(2,1)}, bf16[4,4,144,256]{3,2,1,0:T(8,128)(2,1)}, bf16[1280,256]{1,0:T(8,128)(2,1)}, f32[16,256]{1,0:T(8,128)}, bf16...) custom-call(bf16[576,2048]{1,0:T(8,128)(2,1)} %bitcast.18, ...), custom_call_target="tpu_custom_call" | custom-call | flops 16911433728 | bytes 40000000 | tf_op jit(solution)/shard_map/pallas_call | solution.py:455
  133.5 0.0 all-reduce.5.cloned.1.call-update
  133.6 1.3 fusion.3
  134.9 1.4 fusion.2
  136.3 0.0 copy-done.1
  136.3 0.1 copy.29
  136.4 0.2 copy.30
  136.7 0.7 pad.14.ids_ref
  137.4 137.9 %shard_map.171 = (bf16[576,2048]{1,0:T(8,128)(2,1)}, bf16[27,256,256]{2,1,0:T(8,128)(2,1)}, bf16[256,256]{1,0:T(8,128)(2,1)}, f32[256,256]{1,0:T(8,128)}, f32[8,256]{1,0:T(8,128)}) custom-call(bf16[4,4,144,256]{3,2,1,0:T(8,128)(2,1)} %get-tuple-element.23.dz_ref, bf16[2,8,4,144,128]{4,3,2,1,0:T(8,128)(2,1)} %bitcast.20, f32[504,128]{1,0:T(8,128)} %pad.14.ids_ref, ...), custom_call_target="tpu_custom_call" | custom-call | flops 33822867456 | bytes 50000000 | tf_op jit(solution)/shard_map/pallas_call | solution.py:995
  275.3 1.6 convert_element_type.47
  276.9 0.0 copy-start.4
  276.9 0.0 copy-start.5
  276.9 0.0 copy-start.6
  276.9 0.0 copy-start.7
  276.9 0.0 copy-start.2
  277.0 0.0 copy-start
  277.0 6.0 %convert.1 = f32[3,9,256,256]{3,2,1,0:T(8,128)} convert(bf16[3,9,256,256]{3,2,1,0:T(8,128)(2,1)} %bitcast.13) | non-fusion elementwise | flops 1769472 | bytes 10616832 | tf_op jit(solution)/shard_map/reshape | solution.py:1320
  283.0 0.0 copy-start.3
  283.0 0.8 fusion.4
  283.7 0.0 copy-done.4
  283.7 0.0 copy-done.5
  283.7 0.0 copy-done.6
  283.8 0.0 copy-done.7
  283.8 0.6 pad_maximum_fusion
  284.4 0.0 all-reduce.5.cloned.1.call-done
  284.4 1.6 dynamic-slice_convert_fusion
  285.9 0.0 copy-done.2
  285.9 0.7 copy.37
  286.7 0.0 copy-done
  286.7 1.4 copy.38
  288.1 0.0 copy-done.3
  288.1 0.7 copy.39
  (6 shorter events, 0.1 us)
Async XLA Ops:
  7.2 277.2 %all-reduce.5.cloned.1.call-start = ((), (), s32[]{:S(2)}) async-start(), calls=%async_computation | async-start | bytes 1310720 | tf_op jit(solution)/shard_map/psum | solution.py:1323
  11.2 125.1 %copy-start.1 = (s32[192,96]{1,0:T(8,128)S(1)}, s32[192,96]{1,0:T(8,128)}, u32[]{:S(2)}) copy-start(s32[192,96]{1,0:T(8,128)} %param.12) | copy-start | bytes 221188
  276.9 6.8 %copy-start.4 = (f32[4,256]{1,0:T(4,128)S(1)}, f32[4,256]{1,0:T(4,128)}, u32[]{:S(2)}) copy-start(f32[4,256]{1,0:T(4,128)} %get-tuple-element.36) | copy-start | bytes 12292
  276.9 6.8 %copy-start.5 = (f32[4,256]{1,0:T(4,128)S(1)}, f32[4,256]{1,0:T(4,128)}, u32[]{:S(2)}) copy-start(f32[4,256]{1,0:T(4,128)} %get-tuple-element.37) | copy-start | bytes 12292
  276.9 6.8 %copy-start.6 = (f32[1,256]{1,0:T(1,128)S(1)}, f32[1,256]{1,0:T(1,128)}, u32[]{:S(2)}) copy-start(f32[1,256]{1,0:T(1,128)} %get-tuple-element.38) | copy-start | bytes 3076
  276.9 6.8 %copy-start.7 = (f32[1,256]{1,0:T(1,128)S(1)}, f32[1,256]{1,0:T(1,128)}, u32[]{:S(2)}) copy-start(f32[1,256]{1,0:T(1,128)} %get-tuple-element.39) | copy-start | bytes 3076
  276.9 9.0 %copy-start.2 = (bf16[576,256]{1,0:T(8,128)(2,1)S(1)}, bf16[576,256]{1,0:T(8,128)(2,1)}, u32[]{:S(2)}) copy-start(bf16[576,256]{1,0:T(8,128)(2,1)} %get-tuple-element.22) | copy-start | bytes 884740
  277.0 9.7 %copy-start = (bf16[576,2048]{1,0:T(8,128)(2,1)S(1)}, bf16[576,2048]{1,0:T(8,128)(2,1)}, u32[]{:S(2)}) copy-start(bf16[576,2048]{1,0:T(8,128)(2,1)} %get-tuple-element.30) | copy-start | bytes 7077892
  283.0 5.1 %copy-start.3 = (f32[256,256]{1,0:T(8,128)S(1)}, f32[256,256]{1,0:T(8,128)}, u32[]{:S(2)}) copy-start(f32[256,256]{1,0:T(8,128)} %get-tuple-element.56) | copy-start | bytes 786436
Sparse Core Ops, SparseCore 0:
  133.7 134.2 all-reduce.4

commit v4 on v3

--- a/solution.py
+++ b/solution.py
@@ -96,9 +96,8 @@
     rows, cols, image_count, total_pixels,
     raw_ref, order_ref, back_ref, ids_ref, wat_ref, wpt_ref, wpl_ref, wpj_ref, gain_ref, shift_ref, cot_ref,
     counts_ref, out_ref, dz_ref, pj_ref, stat_ref, pooled_ref, pooln_ref, pools_ref, dap_ref, xsub_ref,
-    x_ref, idrep, wbuf, wplbuf, ubuf, zx1, zx2, zx3, zs1, zs2, zs3,
-    halo_bufs, zn, slope, joined, zf, dzf, active, isum, cbuf, rbuf, pr_buf, pc_buf, pz_buf,
-    wsem, wplsem, hsend, hrecv, csend, crecv, rsend, rrecv, psend, precv, pcsend, pcrecv, pzsend, pzrecv,
+    x_ref, idrep, wbuf, wplbuf, parts, sums_by_row, edge_out, edge_in, rim_out, rim_in, zn, slope, joined, zf, dzf, active, isum, cbuf, rbuf, pr_buf, pc_buf, pz_buf,
+    wsem, wplsem, esend, erecv, hsend, hrecv, csend, crecv, rsend, rrecv, psend, precv, pcsend, pcrecv, pzsend, pzrecv,
     xsend, xrecv,
 ):
     r, c = lax.axis_index("rows"), lax.axis_index("cols")
@@ -106,8 +105,6 @@
     pixels = blocks * rb
     own = REACH * 36
     images = isum.shape[0]
-    zx, zs = {1: zx1, 2: zx2, 3: zx3}, {1: zs1, 2: zs2, 3: zs3}
-    order = (3, 2, 1)
     taps = 27
 
     def weight_copy(n):
@@ -148,44 +145,46 @@
     pr_buf[r] = isum[:, pl.ds(pl.multiple_of(r * share, share), share)]
     pool_rows.start(share_of)
 
-    def halo_copies(m):
-        height = HALO[m]
-        a_range = {-1: (0, m), 0: (m, blocks), 1: (m + blocks, m)}
-        r_range = {-1: (0, height), 0: (height, rb), 1: (height + rb, height)}
-        copies = []
-        for place, (dr, dc) in enumerate(DIRECTIONS):
-            a0, na = a_range[dc]
-            r0, nr = r_range[dr]
-            copies.append(
-                (
-                    dr,
-                    dc,
-                    pltpu.make_async_remote_copy(
-                        src_ref=zs[m].at[pl.ds(a0, na), pl.ds(r0, nr)],
-                        dst_ref=halo_bufs[(m - 1) * 8 + place],
-                        send_sem=hsend.at[m - 1, place],
-                        recv_sem=hrecv.at[m - 1, place],
-                        device_id=(lax.rem(r + dr + rows, rows), lax.rem(c + dc + cols, cols)),
-                        device_id_type=MESH,
-                    ),
-                )
+    def side_copies(m):
+        return [
+            (
+                (c > 0, c < cols - 1)[way],
+                (c < cols - 1, c > 0)[way],
+                pltpu.make_async_remote_copy(
+                    src_ref=edge_out[m - 1].at[way],
+                    dst_ref=edge_in[m - 1].at[way],
+                    send_sem=esend.at[m - 1, way],
+                    recv_sem=erecv.at[m - 1, way],
+                    device_id=(r, lax.rem(c + (cols - 1, 1)[way], cols)),
+                    device_id_type=MESH,
+                ),
             )
-        return copies
-
-    def inside(dr, dc):
-        return (r + dr >= 0) & (r + dr < rows) & (c + dc >= 0) & (c + dc < cols)
+            for way in range(2)
+        ]
+
+    def rim_copies(m):
+        return [
+            (
+                (r > 0, r < rows - 1)[way],
+                (r < rows - 1, r > 0)[way],
+                pltpu.make_async_remote_copy(
+                    src_ref=rim_out[m - 1].at[way],
+                    dst_ref=rim_in[m - 1].at[way],
+                    send_sem=hsend.at[m - 1, way],
+                    recv_sem=hrecv.at[m - 1, way],
+                    device_id=(lax.rem(r + (rows - 1, 1)[way], rows), c),
+                    device_id_type=MESH,
+                ),
+            )
+            for way in range(2)
+        ]
 
     def conv(position, m):
-        height = HALO[m]
-
-        @pl.loop(0, blocks + 2 * m)
-        def _(block):
-            zx[m][block] = jnp.zeros(zx[m].shape[1:], F32)
-
+        lines = parts[m - 1]
         for i in range(3):
             @pl.loop(0, blocks + 2 * m)
             def _(block):
-                ubuf[block] = jnp.zeros(ubuf.shape[1:], F32)
+                lines[i, block] = jnp.zeros(lines.shape[2:], F32)
 
             @pl.loop(0, 3)
             def _(j):
@@ -202,30 +201,55 @@
                 for a in range(blocks):
                     same = idrep[REACH + a, own : own + rb] == idrep[REACH + a - (j - 1) * m, own : own + rb]
                     part = product[a * rb : (a + 1) * rb]
-                    ubuf[a + (2 - j) * m] += jnp.where(wide(same.astype(F32), width) > 0.0, part, 0.0)
-
-            up = (i - 1) * 36 * m
-
-            @pl.loop(0, blocks + 2 * m)
-            def _(block):
-                value = ubuf[block]
-                if i != 1:
-                    here = REACH - m + block
-                    same = idrep[here, own : own + rb] == idrep[here, own - up : own - up + rb]
-                    value = jnp.where(wide(same.astype(F32), width) > 0.0, value, 0.0)
-                zx[m][block, height - up : height - up + rb] += value
-
-        @pl.loop(0, blocks + 2 * m)
-        def _(block):
-            zs[m][block] = zx[m][block].astype(BF16)
-
-        for dr, dc, copy in halo_copies(m):
-            pl.when(inside(dr, dc))(copy.start)
+                    lines[i, a + (2 - j) * m] += jnp.where(wide(same.astype(F32), width) > 0.0, part, 0.0)
+
+            for a in range(m):
+                edge_out[m - 1][0, i, a] = lines[i, a].astype(BF16)
+                edge_out[m - 1][1, i, a] = lines[i, m + blocks + a].astype(BF16)
+        for sends, _, copy in side_copies(m):
+            pl.when(sends)(copy.start)
+
+    def absorb(m):
+        height, lines, whole = HALO[m], parts[m - 1], sums_by_row[m - 1]
+        for way, (_, receives, copy) in enumerate(side_copies(m)):
+            @pl.when(receives)
+            def _():
+                copy.wait_recv()
+                for i in range(3):
+                    for a in range(m):
+                        lines[i, (blocks, m)[way] + a] += edge_in[m - 1][way, i, a].astype(F32)
 
         @pl.loop(0, blocks)
         def _(a):
-            zn[m, a] = zx[m][m + a, height : height + rb]
-
+            whole[a, 0:height] = jnp.zeros((height, width), F32)
+            whole[a, height : height + rb] = lines[1, m + a]
+            whole[a, height + rb : 2 * height + rb] = jnp.zeros((height, width), F32)
+            for i in (0, 2):
+                up = (i - 1) * 36 * m
+                same = idrep[REACH + a, own : own + rb] == idrep[REACH + a, own - up : own - up + rb]
+                whole[a, height - up : height - up + rb] += jnp.where(
+                    wide(same.astype(F32), width) > 0.0, lines[i, m + a], 0.0
+                )
+            rim_out[m - 1][0, a] = whole[a, 0:height].astype(BF16)
+            rim_out[m - 1][1, a] = whole[a, height + rb : 2 * height + rb].astype(BF16)
+
+        for sends, _, copy in rim_copies(m):
+            pl.when(sends)(copy.start)
+
+    def finish(m):
+        height, whole = HALO[m], sums_by_row[m - 1]
+
+        @pl.loop(0, blocks)
+        def _(a):
+            zn[m, a] = whole[a, height : height + rb]
+
+        for way, (_, receives, copy) in enumerate(rim_copies(m)):
+            @pl.when(receives)
+            def _():
+                copy.wait_recv()
+                start = (rb - height, 0)[way]
+                for a in range(blocks):
+                    zn[m, a, start : start + height] += rim_in[m - 1][way, a].astype(F32)
 
     members = [(dy, dx, dk) for dy in range(2) for dx in range(2) for dk in range(2)]
     half = share // 2
@@ -233,13 +257,15 @@
     def channel_slices(y, x, k):
         return [pl.multiple_of((2 * (2 * k + l) + y) * share + x * half, 128) for l in range(2)]
 
-    def member_copies():
+    def member_copies(steps, slices):
         mine = lax.rem(r, 2) * cols + c
         copies = []
-        for step, (dy, dx, dk) in enumerate(members):
+        for step in steps:
+            dy, dx, dk = members[step]
             y, x, k = lax.rem(r + dy, 2), lax.rem(c // 2 + dx, 2), lax.rem(c + dk, 2)
-            for l, start in enumerate(channel_slices(y, x, k)):
-                source = x_ref.at[:, pl.ds(start, half)]
+            starts = channel_slices(y, x, k)
+            for l in slices:
+                source = x_ref.at[:, pl.ds(starts[l], half)]
                 target = xsub_ref.at[l, mine]
                 if step == 0:
                     copies.append(pltpu.make_async_copy(source, target, xrecv.at[l, mine]))
@@ -256,13 +282,20 @@
                     )
         return copies
 
+    def send_members(steps, slices):
+        for copy in member_copies(steps, slices):
+            copy.start()
+
     pool_cols = Exchange(cols, c, lambda other: (r, other), pc_buf, pcsend, pcrecv)
     pool_z = Exchange(rows, r, lambda other: (other, c), pz_buf, pzsend, pzrecv)
+    send_members(range(8), (0,))
+    send_members((0, 1), (1,))
     conv(0, 3)
     pool_rows.arrive()
     pc_buf[c] = pool_rows.total()
     pool_cols.start()
     conv(1, 2)
+    absorb(3)
     pool_cols.arrive()
     counts = counts_ref[...]
     pooled = (pool_cols.total() / wide(counts, share)).astype(BF16)
@@ -271,11 +304,11 @@
     pz_buf[r] = jnp.dot(pooled, wplbuf[...], preferred_element_type=F32)
     pool_z.start()
     conv(2, 1)
+    absorb(2)
     product = jnp.dot(x_ref[...], wpt_ref[...], preferred_element_type=F32)
     for a in range(blocks):
         zn[0, a] = product[a * rb : (a + 1) * rb]
-    for copy in member_copies():
-        copy.start()
+    absorb(1)
     pool_z.arrive()
     zp = pool_z.total()
     pool_avg = jnp.sum(zp, axis=0, keepdims=True) / image_count
@@ -289,19 +322,8 @@
     pool_active = jnp.concatenate([pool_active, jnp.zeros((spare, width), F32)], axis=0).astype(BF16)
     joined[:, 4 * width : 5 * width] = jnp.dot(one_hot, pool_active, preferred_element_type=F32).astype(BF16)
 
-    for m in order:
-        height = HALO[m]
-        a_range = {-1: (blocks - m, m), 0: (0, blocks), 1: (0, m)}
-        r_range = {-1: (rb - height, height), 0: (0, rb), 1: (0, height)}
-        for place, (dr, dc, copy) in enumerate(halo_copies(m)):
-            a0, na = a_range[dc]
-            r0, nr = r_range[dr]
-
-            @pl.when(inside(-dr, -dc))
-            def _():
-                copy.wait_recv()
-                for a in range(na):
-                    zn[m, a0 + a, r0 : r0 + nr] += halo_bufs[(m - 1) * 8 + place][a].astype(F32)
+    for m in (3, 2, 1):
+        finish(m)
 
     started = []
 
@@ -331,6 +353,7 @@
         firsts.append(first)
         seconds.append(second)
     moments = all_sum(0, jnp.concatenate(firsts + seconds, axis=0))
+    send_members((2, 4), (1,))
     average = moments[0:4] / total_pixels
     inverse = lax.rsqrt(moments[4:8] / total_pixels - average * average + epsilon)
     for k in range(4):
@@ -348,6 +371,7 @@
         value = zf[a * rb : (a + 1) * rb]
         first, second = first + row_sum(value), second + row_sum(value * value)
     moments = all_sum(1, jnp.concatenate([first, second] + [zero] * 6, axis=0))
+    send_members((3, 5), (1,))
     final_avg = moments[0:1] / total_pixels
     final_inverse = lax.rsqrt(moments[1:2] / total_pixels - final_avg * final_avg + epsilon)
     shift_last, gain_last = zero, zero
@@ -363,6 +387,7 @@
         shift_last, gain_last = shift_last + row_sum(grad), gain_last + row_sum(grad * normed)
     out_ref[...] = jnp.dot(back_ref[...], active[...], preferred_element_type=F32).astype(BF16)
     sums = all_sum(2, jnp.concatenate([shift_last, gain_last] + [zero] * 6, axis=0))
+    send_members((6, 7), (1,))
     shift_last, gain_last = sums[0:1], sums[1:2]
     gain = gain_ref[5:6]
     for a in range(blocks):
@@ -408,14 +433,13 @@
     pool_rows.leave(share_of)
     for exchange in (pool_cols, pool_z, *started):
         exchange.leave()
-    for m in order:
-        for dr, dc, copy in halo_copies(m):
-            pl.when(inside(dr, dc))(copy.wait_send)
-    for step, copy in enumerate(member_copies()):
-        if step < 2:
-            copy.wait()
-        else:
-            copy.wait_send()
+    for m in (3, 2, 1):
+        for sends, _, copy in side_copies(m) + rim_copies(m):
+            pl.when(sends)(copy.wait_send)
+    for copy in member_copies((0,), (0, 1)):
+        copy.wait()
+    for copy in member_copies(range(1, 8), (0, 1)):
+        copy.wait_send()
     for l in range(2):
         for step, (dy, dx, dk) in enumerate(members):
             if step:
@@ -431,9 +455,6 @@
                 ).wait_recv()
 
 
-DIRECTIONS = ((-1, 0), (1, 0), (-1, -1), (-1, 1), (1, -1), (1, 1), (0, -1), (0, 1))
-
-
 def forward_call(rows, cols, image_count, x, order, back, ids, wat, wpt, wpl, wpj, gain, shift, cot, counts):
     pixels, channels = x.shape
     width = wpt.shape[1]
@@ -444,13 +465,9 @@
     vmem = pl.BlockSpec(memory_space=pltpu.VMEM)
     hbm = pl.BlockSpec(memory_space=pl.ANY)
 
-    def ext(m, kind):
-        return pltpu.VMEM((blocks + 2 * m, 2 * HALO[m] + rb, width), kind)
-
-    halo_bufs = []
-    for m in (1, 2, 3):
-        for dr, dc in DIRECTIONS:
-            halo_bufs.append(pltpu.VMEM((m if dc else blocks, HALO[m] if dr else rb, width), BF16))
+    def each(shape, kind):
+        return [pltpu.VMEM(shape(m) + (width,), kind) for m in (1, 2, 3)]
+
     dma = pltpu.SemaphoreType.DMA
     return pl.pallas_call(
         functools.partial(forward_kernel, rows, cols, float(image_count), total_pixels),
@@ -472,10 +489,10 @@
             pltpu.VMEM((blocks + 2 * REACH, ids.shape[0], 128), F32),
             pltpu.VMEM((SLOTS, channels, width), BF16),
             pltpu.VMEM((share, width), BF16),
-            pltpu.VMEM((blocks + 2 * REACH, rb, width), F32),
-            ext(1, F32), ext(2, F32), ext(3, F32),
-            ext(1, BF16), ext(2, BF16), ext(3, BF16),
-            halo_bufs,
+            each(lambda m: (3, blocks + 2 * m, rb), F32),
+            each(lambda m: (blocks, 2 * HALO[m] + rb), F32),
+            each(lambda m: (2, 3, m, rb), BF16), each(lambda m: (2, 3, m, rb), BF16),
+            each(lambda m: (2, blocks, HALO[m]), BF16), each(lambda m: (2, blocks, HALO[m]), BF16),
             pltpu.VMEM((4, blocks, rb, width), F32),
             pltpu.VMEM((4, blocks, rb, width), F32),
             pltpu.VMEM((pixels, 5 * width), BF16),
@@ -489,7 +506,7 @@
             pltpu.VMEM((cols, images, share), F32),
             pltpu.VMEM((rows, images, width), F32),
             dma((SLOTS,)), dma,
-            dma((3, 8)), dma((3, 8)),
+            dma((3, 2)), dma((3, 2)), dma((3, 2)), dma((3, 2)),
             dma((4, cols)), dma((4, cols)),
             dma((4, rows)), dma((4, rows)),
             dma((rows,)), dma((rows,)),
@@ -507,12 +524,12 @@
 def backward_kernel(
     rows, cols, image_count, height,
     dz_ref, xsub_ref, ids_ref, wat_ref, wpt_ref, wpl_ref, gain_ref, counts_ref,
-    pooled_ref, pooln_ref, pools_ref, dap_ref, stat_ref, back_ref,
-    gx_ref, dw_ref, dpoint_ref, gpool_ref, gstat_ref,
-    ext0, ext1, ext2, ext3, shifted, colmask, idrep, gmat, gown, xall, xt, acc, wbuf, wpt,
-    send1, recv1, keep, relay, dw, pcbuf, prbuf,
+    pooled_ref, pooln_ref, pools_ref, dap_ref, stat_ref, back_ref, pj_ref,
+    gx_ref, dw_ref, dpoint_ref, gpool_ref, gstat_ref, gproj_ref,
+    ext0, ext1, ext2, ext3, shifted, colmask, idrep, gmat, gown, xt, acc, wbuf, wpt,
+    send1, recv1, keep, relay, dw, pcbuf, prbuf, quarters, quarter_sums, row_parts, final_parts,
     xsem, wsem, wptsem, zsend, zrecv, agsend, agrecv, s1send, s1recv, s2send, s2recv, s3send, s3recv,
-    pcsend, pcrecv, prsend, prrecv, outsem,
+    pcsend, pcrecv, prsend, prrecv, qsend, qrecv, rqsend, rqrecv, fqsend, fqrecv, outsem,
 ):
     r, c = lax.axis_index("rows"), lax.axis_index("cols")
     z, y = r // 2, lax.rem(r, 2)
@@ -533,7 +550,7 @@
         dev_y, dev_c = dev // cols, lax.rem(dev, cols)
         start = pl.multiple_of((dev_c * blocks + a) * pair + dev_y * rb, 16)
         return pltpu.make_async_copy(
-            xsub_ref.at[l, dev, a], xall.at[l, pl.ds(start, rb)], xsem.at[l, dev, a]
+            xsub_ref.at[l, dev, a], gmat.at[pl.ds(start, rb), pl.ds(l * half, half)], xsem.at[l, dev, a]
         )
 
     for l in range(2):
@@ -542,20 +559,23 @@
             def _(dev):
                 x_copy(l, dev, a).start()
 
-    def weight_copy(n, j):
-        branch, i = n // 3, lax.rem(n, 3)
-        slot = lax.rem(n, 2)
-        return pltpu.make_async_copy(
-            wat_ref.at[branch, 3 * i + j],
-            wbuf.at[slot, :, pl.ds(j * width, width)],
-            wsem.at[slot, j],
-        )
+    groups = [[(0, 4), (1, 4), (2, 4)]]
+    for m in (1, 2, 3):
+        groups += [[(m - 1, 0), (m - 1, 1), (m - 1, 2)], [(m - 1, 6), (m - 1, 7), (m - 1, 8)], [(m - 1, 3), (m - 1, 5)]]
+
+    def weight_copies(n):
+        return [
+            pltpu.make_async_copy(
+                wat_ref.at[branch, tap], wbuf.at[n % 2, :, pl.ds(place * width, width)], wsem.at[n % 2, place]
+            )
+            for place, (branch, tap) in enumerate(groups[n])
+        ]
 
     point_copy = pltpu.make_async_copy(wpt_ref, wpt, wptsem)
     point_copy.start()
     for n in range(2):
-        for j in range(3):
-            weight_copy(jnp.int32(n), j).start()
+        for copy in weight_copies(n):
+            copy.start()
 
     greet_all(rows, cols, r, c)
 
@@ -595,7 +615,7 @@
             device_id_type=MESH,
         )
 
-    most = blocks - 1
+    most = blocks // 2
     side = 2 * (1 - x) + k
     sibling, beside, below = (r, 2 * x + 1 - k), (r, side), (2 * z + 1 - y, c)
 
@@ -690,6 +710,36 @@
     pcbuf[c] = dap_ref[...]
     pool_cols.start()
 
+    tall_piece, wide_piece = quarters.shape[2], quarters.shape[3]
+
+    def quarter(other):
+        rows_of = pl.ds(pl.multiple_of(lax.rem(other, 2) * tall_piece, 16), tall_piece)
+        return pj_ref.at[:, rows_of, pl.ds(pl.multiple_of(other // 2 * wide_piece, 128), wide_piece)]
+
+    proj_cols = Exchange(cols, c, lambda other: (r, other), quarters, qsend, qrecv)
+    proj_rows = Exchange(rows, r, lambda other: (other, c), row_parts, rqsend, rqrecv)
+    proj_last = Exchange(cols, c, lambda other: (r, other), final_parts, fqsend, fqrecv)
+    own_rows = pl.ds(pl.multiple_of(k * tall_piece, 16), tall_piece)
+    quarters[c] = pj_ref[:, own_rows, pl.ds(pl.multiple_of(x * wide_piece, 128), wide_piece)]
+    proj_cols.start(quarter)
+
+    def whole_sum(slots, count):
+        value = slots[0].astype(F32)
+        for other in range(1, count):
+            value = value + slots[other].astype(F32)
+        return value
+
+    def proj_down():
+        proj_cols.arrive()
+        quarter_sums[...] = whole_sum(quarters, cols).astype(BF16)
+        row_parts[r] = quarter_sums[r]
+        proj_rows.start(lambda other: quarter_sums.at[other])
+
+    def proj_spread():
+        proj_rows.arrive()
+        final_parts[c] = whole_sum(row_parts, rows).astype(BF16)
+        proj_last.start()
+
     for block in range(across):
         idrep[block] = jnp.broadcast_to(ids_ref[:, block : block + 1], idrep.shape[1:])
     for m in (1, 2, 3):
@@ -717,6 +767,7 @@
 
     start_own(1, 1)
     start_own(2, 0)
+    start_own(2, 1)
     for l in range(2):
         for a in range(blocks):
             @pl.loop(0, 2 * cols)
@@ -724,11 +775,13 @@
                 x_copy(l, dev, a).wait()
 
         spot = pl.multiple_of(lax.rem(l + z_lo, 2) * half, half)
-        for chunk in range(xall.shape[1] // 128):
+        for chunk in range(gmat.shape[0] // 128):
             piece = slice(chunk * 128, (chunk + 1) * 128)
-            xt[pl.ds(spot, half), piece] = xall[l, piece, :].astype(F32).T.astype(BF16)
+            xt[pl.ds(spot, half), piece] = gmat[piece, l * half : (l + 1) * half].astype(F32).T.astype(BF16)
 
     pass_on(1)
+    start_own(3, 0)
+    start_own(3, 1)
 
     point_copy.wait()
 
@@ -826,9 +879,11 @@
                 stage3(n, 0, 0, sibling).wait_recv()
                 stage3(n, 1, 0, sibling).wait_recv()
 
-    def weight_grad(m):
+    def weight_grad(m, between):
         @pl.loop(0, 9)
         def _(tap):
+            for when, action in between.items():
+                pl.when(tap == when)(action)
             i, j = tap // 3, lax.rem(tap, 3)
             shift = (j - 1) * m
 
@@ -841,57 +896,67 @@
 
             scatter_first((m - 1) * 9 + tap, jnp.dot(xt[...], gmat[...], preferred_element_type=F32))
 
+    def add_products(n, depth):
+        for copy in weight_copies(n):
+            copy.wait()
+
+        @pl.loop(0, wbuf.shape[1] // 256)
+        def _(chunk):
+            piece = pl.ds(pl.multiple_of(chunk * 256, 256), 256)
+            acc[:, piece] += contract_lanes(gown[:, :depth], wbuf[n % 2, piece, :depth])
+
+        if n + 2 < len(groups):
+            for copy in weight_copies(n + 2):
+                copy.start()
+
     def feature_grad(m, lines):
-        for i in lines:
-            n = (m - 1) * 3 + i
-            slot = n % 2
-            for j in range(3):
+        for line in lines:
+            n = 1 + (m - 1) * 3 + line
+            for place, (_, tap) in enumerate(groups[n]):
+                i, j = tap // 3, tap % 3
                 shift = (j - 1) * m
                 for a in range(blocks):
                     block = c * blocks + a
                     source = lax.rem(block - shift + across, across)
-                    gown[a * rb : (a + 1) * rb, j * width : (j + 1) * width] = masked(
+                    gown[a * rb : (a + 1) * rb, place * width : (place + 1) * width] = masked(
                         shifted[i, source, pl.ds(pl.multiple_of(y * rb, 16), rb)], colmask[REACH + shift, block]
                     )
-            for j in range(3):
-                weight_copy(jnp.int32(n), j).wait()
-
-            @pl.loop(0, wbuf.shape[1] // 256)
-            def _(chunk):
-                piece = pl.ds(pl.multiple_of(chunk * 256, 256), 256)
-                acc[:, piece] += contract_lanes(gown[...], wbuf[slot, piece, :])
-
-            if n + 2 < 9:
-                for j in range(3):
-                    weight_copy(jnp.int32(n + 2), j).start()
-
+            add_products(n, len(groups[n]) * width)
+
+    for m in (1, 2, 3):
+        for a in range(blocks):
+            gown[a * rb : (a + 1) * rb, (m - 1) * width : m * width] = dz_ref[m, a]
+    add_products(0, 3 * width)
     pass_last(1)
-    start_own(2, 1)
-    start_own(3, 0)
     finish_gather(1)
     build_shifted(1)
-    weight_grad(1)
-    pass_on(2)
-    feature_grad(1, (0, 1))
+
+    def second_on():
+        pass_on(2)
+        start_own(0, 0)
+
+    weight_grad(1, {4: second_on, 7: proj_down})
     pass_last(2)
-    start_own(3, 1)
-    start_own(0, 0)
-    feature_grad(1, (2,))
+    feature_grad(1, (0,))
+    pass_on(3)
     drain2(0, 9)
+    feature_grad(1, (1, 2))
     finish_gather(2)
     build_shifted(2)
-    weight_grad(2)
-    pass_on(3)
-    feature_grad(2, (0, 1))
-    pass_last(3)
-    pass_on(0)
-    feature_grad(2, (2,))
+
+    def third_last():
+        pass_on(0)
+        pass_last(3)
+
+    weight_grad(2, {2: proj_spread, 5: third_last})
+    pass_last(0)
     drain3(0, 9)
+    feature_grad(2, (0,))
     drain2(9, 9)
-    pass_last(0)
+    feature_grad(2, (1, 2))
     finish_gather(3)
     build_shifted(3)
-    weight_grad(3)
+    weight_grad(3, {})
     finish_gather(0)
 
     @pl.loop(0, across)
@@ -906,8 +971,9 @@
     pool_rows = Exchange(rows, r, lambda other: (other, c), prbuf, prsend, prrecv)
     prbuf[r] = pool_cols.total()
     pool_rows.start()
-    feature_grad(3, (0, 1, 2))
+    feature_grad(3, (0, 1))
     drain2(18, 10)
+    feature_grad(3, (2,))
     drain4(9, 9)
     pool_rows.arrive()
     normed = pooln_ref[...]
@@ -952,6 +1018,13 @@
 
     pool_cols.leave()
     pool_rows.leave()
+    proj_last.arrive()
+    for other in range(cols):
+        piece_rows = slice(other % 2 * tall_piece, (other % 2 + 1) * tall_piece)
+        gproj_ref[piece_rows, other // 2 * wide_piece : (other // 2 + 1) * wide_piece] = final_parts[other].astype(F32)
+    proj_cols.leave(quarter)
+    proj_rows.leave(lambda other: quarter_sums.at[other])
+    proj_last.leave()
     for m in (1, 2, 3):
         pl.when(sends_rim)(rim_copy(m, True).wait_send)
     for m in (1, 2, 3, 0):
@@ -976,7 +1049,7 @@
 
 
 def backward_call(
-    rows, cols, image_count, dz, xsub, ids, wat, wpt, wpl, gain, counts, pooled, pooln, pools, dap, stat, back
+    rows, cols, image_count, dz, xsub, ids, wat, wpt, wpl, gain, counts, pooled, pooln, pools, dap, stat, back, proj
 ):
     _, blocks, rb, width = dz.shape
     channels = wpt.shape[0]
@@ -1000,9 +1073,10 @@
             jax.ShapeDtypeStruct((share, width), BF16),
             jax.ShapeDtypeStruct((share, width), F32),
             jax.ShapeDtypeStruct((8, width), F32),
+            jax.ShapeDtypeStruct(proj.shape[1:], F32),
         ),
-        in_specs=[vmem, hbm, vmem, hbm, hbm, hbm] + [vmem] * 8,
-        out_specs=(vmem, hbm, hbm, vmem, vmem),
+        in_specs=[vmem, hbm, vmem, hbm, hbm, hbm] + [vmem] * 9,
+        out_specs=(vmem, hbm, hbm, vmem, vmem, vmem),
         scratch_shapes=[
             ext(0), ext(HALO[1]), ext(HALO[2]), ext(HALO[3]),
             pltpu.VMEM((3, across, pair, width), BF16),
@@ -1010,7 +1084,6 @@
             pltpu.VMEM((across, ids.shape[0], 128), F32),
             pltpu.VMEM((group, width), BF16),
             pltpu.VMEM((pixels, 3 * width), BF16),
-            pltpu.VMEM((2, group, share // 2), BF16),
             pltpu.VMEM((share, group), BF16),
             pltpu.VMEM((pixels, channels), F32),
             pltpu.VMEM((2, channels, 3 * width), BF16),
@@ -1022,6 +1095,10 @@
             pltpu.VMEM((taps, share, width), BF16),
             pltpu.VMEM((cols, images, width), F32),
             pltpu.VMEM((rows, images, width), F32),
+            pltpu.VMEM((cols, rows, proj.shape[1] // 2, width // 2), BF16),
+            pltpu.VMEM((rows, proj.shape[1] // 2, width // 2), BF16),
+            pltpu.VMEM((rows, proj.shape[1] // 2, width // 2), BF16),
+            pltpu.VMEM((cols, proj.shape[1] // 2, width // 2), BF16),
             dma((2, 2 * cols, blocks)), dma((2, 3)), dma,
             dma((4,)), dma((4,)),
             dma((4, 2, 8)), dma((4, 2, 2 * cols + 1)),
@@ -1030,13 +1107,16 @@
             dma((3, taps)), dma((2, taps)),
             dma((cols,)), dma((cols,)),
             dma((rows,)), dma((rows,)),
+            dma((cols,)), dma((cols,)),
+            dma((rows,)), dma((rows,)),
+            dma((cols,)), dma((cols,)),
             dma((2,)),
         ],
         compiler_params=pltpu.CompilerParams(
             collective_id=1, has_side_effects=True, vmem_limit_bytes=64 * 2**20
         ),
         cost_estimate=pl.CostEstimate(flops=4 * pixels * channels * width * 28, bytes_accessed=50_000_000, transcendentals=0),
-    )(dz, xsub, ids, wat, wpt, wpl, gain, counts, pooled, pooln, pools, dap, stat, back)
+    )(dz, xsub, ids, wat, wpt, wpl, gain, counts, pooled, pooln, pools, dap, stat, back, proj)
 
 
 def extended(cells, sides, width):
@@ -1313,15 +1393,12 @@
         (row_index // 2 * (2 * rows_here), jnp.int32(margin)),
         (2 * rows_here + 2 * margin, grid_cols),
     )
-    grad_input, atrous, point, grad_pool, pool_sums = backward_call(
+    grad_input, atrous, point, grad_pool, pool_sums, grad_proj = backward_call(
         rows, cols, image_count, dz, xsub.reshape(2, 8, 4, pixels // 4, -1), id_columns(pair_window), w_atrous, w_point, w_pool,
-        norm_gain, count_table, pooled, pool_normed, pool_slope, dap, stats, back,
+        norm_gain, count_table, pooled, pool_normed, pool_slope, dap, stats, back, proj_term.reshape(rows, -1, branch_width),
     )
     grad_atrous = atrous.astype(F32).reshape(3, 9, channels // rows, branch_width)
 
-    proj_share = proj_term.shape[0] // rows
-    grad_proj = lax.psum(proj_term, ("rows", "cols"))
-    grad_proj = lax.dynamic_slice_in_dim(grad_proj, row_index * proj_share, proj_share, 0).astype(F32)
     grad_gain = jnp.concatenate([stats[4:8], pool_sums[1:2], stats[9:10]], axis=0)
     grad_shift = jnp.concatenate([stats[0:4], pool_sums[0:1], stats[8:9]], axis=0)
     grad_features = grad_input.reshape(rows_here, cols_here, channels)

time: 297 us -> 266 us (0.90)
  Pallas kernels: 260 us -> 245 us
  between operations: 14.2 us -> 0.72 us
    pallas_call x1, Pallas kernels: 122 us -> 101 us  [forward_call(): pl.pallas_call(functools.partial(forward_kernel, rows, cols, float(image_...]
    pallas_call x1, Pallas kernels: 138 us -> 143 us  [backward_call(): pl.pallas_call(functools.partial(backward_kernel, rows, cols, float(image...]
  transfers between devices with their start and end apart: 1 -> 0, of which waited for: 0 -> 0; matrix products, arithmetic and copies ran while one was open for 4% -> 0% of each run, Pallas kernels for 47% -> 0%
where the time goes in v4:
time: 266 us; the launch traced here: 264 us
  Pallas kernels  245 us (92%)
  local copies, waits for them, and re-layouts  9.58 us (4%)
  other arithmetic  9.42 us (4%)
    pallas_call x1, Pallas kernels, backward_call(): pl.pallas_call(functools.partial(backward_kernel, rows, cols, float(image...  143 us
    pallas_call x1, Pallas kernels, forward_call(): pl.pallas_call(functools.partial(forward_kernel, rows, cols, float(image_...  101 us
    reshape x1, other arithmetic, quick_shards(): atrous.astype(F32).reshape(3, 9, channels // rows, branch_width)  5.99 us

profile of v4, /device:TPU:0, one launch (start us, length us, event | category | flops | bytes accessed | tf_op | source)
XLA Modules:
  0.0 264.3 jit_solution(3474785365887044171)
XLA Ops:
  0.7 0.8 fusion
  1.5 0.1 copy.29
  1.6 0.2 copy.30
  1.8 0.7 pad.14.ids_ref
  2.5 0.8 fusion.1
  3.4 0.1 copy.26
  3.5 0.2 copy.31
  3.7 0.7 pad.13.ids_ref
  4.4 1.0 eq.15
  5.4 0.4 convert_reduce_fusion
  5.8 0.7 broadcast_in_dim.2.counts_ref
  6.5 101.3 %shard_map.170 = (bf16[576,256]{1,0:T(8,128)(2,1)}, bf16[4,4,144,256]{3,2,1,0:T(8,128)(2,1)}, bf16[1280,256]{1,0:T(8,128)(2,1)}, f32[16,256]{1,0:T(8,128)}, bf16...) custom-call(bf16[576,2048]{1,0:T(8,128)(2,1)} %bitcast.19, ...), custom_call_target="tpu_custom_call" | custom-call | flops 16911433728 | bytes 40000000 | tf_op jit(solution)/shard_map/pallas_call | solution.py:472
  107.8 143.4 %shard_map.171 = (bf16[576,2048]{1,0:T(8,128)(2,1)}, bf16[27,256,256]{2,1,0:T(8,128)(2,1)}, bf16[256,256]{1,0:T(8,128)(2,1)}, f32[256,256]{1,0:T(8,128)}, f32[8,256]{1,0:T(8,128)}, /*index=5*/f32[160,256]{1,0:T(8,128)}) custom-call(bf16[4,4,144,256]{3,2,1,0:T(8,128)(2,1)} %get-tuple-element.24.dz_ref, bf16[2,8,4,144,128]{4,3,2,1,0:T(8,128)(2,1)} %bitcast.21, ...), custom_call_target="tpu_custom_call" | custom-call | flops 33822867456 | bytes 50000000 | tf_op jit(solution)/shard_map/pallas_call | solution.py:1068
  251.2 0.8 fusion.4
  251.9 0.8 fusion.2
  252.7 0.8 fusion.3
  253.5 0.6 pad_maximum_fusion
  254.1 0.0 copy-start.4
  254.1 0.0 copy-start.1
  254.1 0.0 copy-start
  254.1 6.0 %convert.1 = f32[3,9,256,256]{3,2,1,0:T(8,128)} convert(bf16[3,9,256,256]{3,2,1,0:T(8,128)(2,1)} %bitcast.14) | non-fusion elementwise | flops 1769472 | bytes 10616832 | tf_op jit(solution)/shard_map/reshape | solution.py:1400
  260.1 0.0 copy-start.2
  260.1 0.0 copy-start.3
  260.1 0.0 copy-done.4
  260.1 0.7 convert_element_type.44
  260.8 0.0 copy-done.1
  260.8 0.7 copy.37
  261.6 0.0 copy-done
  261.6 1.4 copy.38
  263.0 0.0 copy-done.2
  263.0 0.7 copy.39
  263.7 0.0 copy-done.3
  263.7 0.7 copy.40
  (5 shorter events, 0.1 us)
Async XLA Ops:
  254.1 6.0 %copy-start.4 = (bf16[256,256]{1,0:T(8,128)(2,1)S(1)}, bf16[256,256]{1,0:T(8,128)(2,1)}, u32[]{:S(2)}) copy-start(bf16[256,256]{1,0:T(8,128)(2,1)} %get-tuple-element.33) | copy-start | bytes 393220
  254.1 6.7 %copy-start.1 = (bf16[576,256]{1,0:T(8,128)(2,1)S(1)}, bf16[576,256]{1,0:T(8,128)(2,1)}, u32[]{:S(2)}) copy-start(bf16[576,256]{1,0:T(8,128)(2,1)} %get-tuple-element.23) | copy-start | bytes 884740
  254.1 7.4 %copy-start = (bf16[576,2048]{1,0:T(8,128)(2,1)S(1)}, bf16[576,2048]{1,0:T(8,128)(2,1)}, u32[]{:S(2)}) copy-start(bf16[576,2048]{1,0:T(8,128)(2,1)} %get-tuple-element.32) | copy-start | bytes 7077892
  260.1 2.9 %copy-start.2 = (f32[256,256]{1,0:T(8,128)S(1)}, f32[256,256]{1,0:T(8,128)}, u32[]{:S(2)}) copy-start(f32[256,256]{1,0:T(8,128)} %get-tuple-element.58) | copy-start | bytes 786436
  260.1 3.6 %copy-start.3 = (f32[160,256]{1,0:T(8,128)S(1)}, f32[160,256]{1,0:T(8,128)}, u32[]{:S(2)}) copy-start(f32[160,256]{1,0:T(8,128)} %get-tuple-element.59) | copy-start | bytes 491524

commit v5 on v4

--- a/solution.py
+++ b/solution.py
@@ -37,14 +37,15 @@
     return lax.dot_general(left, right, (((1,), (1,)), ((), ())), preferred_element_type=F32)
 
 
-def greet_all(rows, cols, r, c):
+def greet(rows, cols, r, c):
     barrier = pltpu.get_barrier_semaphore()
-    for dr in range(rows):
-        for dc in range(cols):
-            if dr or dc:
-                other = (lax.rem(r + dr, rows), lax.rem(c + dc, cols))
-                pl.semaphore_signal(barrier, inc=1, device_id=other, device_id_type=MESH)
-    pl.semaphore_wait(barrier, rows * cols - 1)
+    near = r + 1 - 2 * lax.rem(r, 2)
+    others = [(lax.rem(r + step, rows), c) for step in range(1, rows)]
+    for step in range(1, cols):
+        others += [(r, lax.rem(c + step, cols)), (near, lax.rem(c + step, cols))]
+    for other in others:
+        pl.semaphore_signal(barrier, inc=1, device_id=other, device_id_type=MESH)
+    pl.semaphore_wait(barrier, len(others))
 
 
 class Exchange:
@@ -96,7 +97,7 @@
     rows, cols, image_count, total_pixels,
     raw_ref, order_ref, back_ref, ids_ref, wat_ref, wpt_ref, wpl_ref, wpj_ref, gain_ref, shift_ref, cot_ref,
     counts_ref, out_ref, dz_ref, pj_ref, stat_ref, pooled_ref, pooln_ref, pools_ref, dap_ref, xsub_ref,
-    x_ref, idrep, wbuf, wplbuf, parts, sums_by_row, edge_out, edge_in, rim_out, rim_in, zn, slope, joined, zf, dzf, active, isum, cbuf, rbuf, pr_buf, pc_buf, pz_buf,
+    x_ref, idrep, wbuf, wplbuf, parts, sums_by_row, edge_out, edge_in, rim_out, rim_in, zn, slope, joined, zf, dzf, active, upstream, isum, cbuf, rbuf, pr_buf, pc_buf, pz_buf,
     wsem, wplsem, esend, erecv, hsend, hrecv, csend, crecv, rsend, rrecv, psend, precv, pcsend, pcrecv, pzsend, pzrecv,
     xsend, xrecv,
 ):
@@ -121,7 +122,7 @@
     pool_weight.start()
     for block in range(idrep.shape[0]):
         idrep[block] = jnp.broadcast_to(ids_ref[:, block : block + 1], idrep.shape[1:])
-    greet_all(rows, cols, r, c)
+    greet(rows, cols, r, c)
 
     @pl.loop(0, x_ref.shape[1] // 256)
     def _(n):
@@ -181,31 +182,36 @@
 
     def conv(position, m):
         lines = parts[m - 1]
-        for i in range(3):
-            @pl.loop(0, blocks + 2 * m)
-            def _(block):
+
+        @pl.loop(0, blocks + 2 * m)
+        def _(block):
+            for i in range(3):
                 lines[i, block] = jnp.zeros(lines.shape[2:], F32)
 
-            @pl.loop(0, 3)
-            def _(j):
-                n = position * 9 + 3 * i + j
-                slot = lax.rem(n, SLOTS)
-                ahead = n + SLOTS - 1
-
-                @pl.when(ahead < taps)
-                def _():
-                    weight_copy(ahead).start()
-
-                weight_copy(n).wait()
-                product = jnp.dot(x_ref[...], wbuf[slot], preferred_element_type=F32)
-                for a in range(blocks):
-                    same = idrep[REACH + a, own : own + rb] == idrep[REACH + a - (j - 1) * m, own : own + rb]
-                    part = product[a * rb : (a + 1) * rb]
-                    lines[i, a + (2 - j) * m] += jnp.where(wide(same.astype(F32), width) > 0.0, part, 0.0)
-
+        @pl.loop(0, 9)
+        def _(tap):
+            i, j = tap // 3, lax.rem(tap, 3)
+            n = position * 9 + tap
+            slot = lax.rem(n, SLOTS)
+            ahead = n + SLOTS - 1
+
+            @pl.when(ahead < taps)
+            def _():
+                weight_copy(ahead).start()
+
+            weight_copy(n).wait()
+            product = jnp.dot(x_ref[...], wbuf[slot], preferred_element_type=F32)
+            for a in range(blocks):
+                same = idrep[REACH + a, own : own + rb] == idrep[REACH + a - (j - 1) * m, own : own + rb]
+                part = product[a * rb : (a + 1) * rb]
+                lines[i, a + (2 - j) * m] += jnp.where(wide(same.astype(F32), width) > 0.0, part, 0.0)
+
+        @pl.loop(0, 3)
+        def _(i):
             for a in range(m):
                 edge_out[m - 1][0, i, a] = lines[i, a].astype(BF16)
                 edge_out[m - 1][1, i, a] = lines[i, m + blocks + a].astype(BF16)
+
         for sends, _, copy in side_copies(m):
             pl.when(sends)(copy.start)
 
@@ -327,14 +333,18 @@
 
     started = []
 
-    def all_sum(step, value):
+    def all_sum(step, value, meanwhile=(None, None)):
         across = Exchange(cols, c, lambda other: (r, other), cbuf.at[step], csend.at[step], crecv.at[step])
         cbuf[step, c] = value
         across.start()
+        if meanwhile[0]:
+            meanwhile[0]()
         across.arrive()
         down = Exchange(rows, r, lambda other: (other, c), rbuf.at[step], rsend.at[step], rrecv.at[step])
         rbuf[step, r] = across.total()
         down.start()
+        if meanwhile[1]:
+            meanwhile[1]()
         down.arrive()
         started.extend((across, down))
         return down.total()
@@ -370,12 +380,15 @@
     for a in range(blocks):
         value = zf[a * rb : (a + 1) * rb]
         first, second = first + row_sum(value), second + row_sum(value * value)
-    moments = all_sum(1, jnp.concatenate([first, second] + [zero] * 6, axis=0))
+
+    def put_upstream():
+        upstream[...] = jnp.dot(order_ref[...], cot_ref[...], preferred_element_type=F32)
+
+    moments = all_sum(1, jnp.concatenate([first, second] + [zero] * 6, axis=0), (None, put_upstream))
     send_members((3, 5), (1,))
     final_avg = moments[0:1] / total_pixels
     final_inverse = lax.rsqrt(moments[1:2] / total_pixels - final_avg * final_avg + epsilon)
     shift_last, gain_last = zero, zero
-    upstream = jnp.dot(order_ref[...], cot_ref[...], preferred_element_type=F32)
     for a in range(blocks):
         piece = slice(a * rb, (a + 1) * rb)
         normed = (zf[piece] - final_avg) * final_inverse
@@ -385,8 +398,11 @@
         zf[piece] = normed
         dzf[piece] = grad
         shift_last, gain_last = shift_last + row_sum(grad), gain_last + row_sum(grad * normed)
-    out_ref[...] = jnp.dot(back_ref[...], active[...], preferred_element_type=F32).astype(BF16)
-    sums = all_sum(2, jnp.concatenate([shift_last, gain_last] + [zero] * 6, axis=0))
+
+    def put_output():
+        out_ref[...] = jnp.dot(back_ref[...], active[...], preferred_element_type=F32).astype(BF16)
+
+    sums = all_sum(2, jnp.concatenate([shift_last, gain_last] + [zero] * 6, axis=0), (None, put_output))
     send_members((6, 7), (1,))
     shift_last, gain_last = sums[0:1], sums[1:2]
     gain = gain_ref[5:6]
@@ -409,11 +425,19 @@
             shift_sum, gain_sum = shift_sum + row_sum(part), gain_sum + row_sum(part * zn[k, a])
         shifts.append(shift_sum)
         gains.append(gain_sum)
-    grad_pixel = contract_lanes(grad_final, wpj_ref[4 * width : 5 * width])
-    upper = grad_pixel.astype(BF16)
-    lower = (grad_pixel - upper.astype(F32)).astype(BF16)
-    dap_ref[...] = (contract_rows(one_hot, upper) + contract_rows(one_hot, lower))[:images]
-    sums = all_sum(3, jnp.concatenate(shifts + gains, axis=0))
+
+    def put_images():
+        grad_pixel = contract_lanes(grad_final, wpj_ref[4 * width : 5 * width])
+        upper = grad_pixel.astype(BF16)
+        lower = (grad_pixel - upper.astype(F32)).astype(BF16)
+        dap_ref[...] = (contract_rows(one_hot, upper) + contract_rows(one_hot, lower))[:images]
+
+    def put_projection():
+        for k in range(5):
+            piece = slice(k * width, (k + 1) * width)
+            pj_ref[piece] = contract_rows(joined[:, piece], grad_final).astype(BF16)
+
+    sums = all_sum(3, jnp.concatenate(shifts + gains, axis=0), (put_images, put_projection))
     for k in range(4):
         gain = gain_ref[k : k + 1]
         from_shift = gain * sums[k : k + 1] / total_pixels
@@ -425,9 +449,6 @@
                 inverse[k : k + 1] * (slope[k, a] * gain - from_shift - zn[k, a] * from_gain)
             ).astype(BF16)
 
-    for k in range(5):
-        piece = slice(k * width, (k + 1) * width)
-        pj_ref[piece] = contract_rows(joined[:, piece], grad_final).astype(BF16)
     stat_ref[...] = jnp.concatenate([sums, shift_last, gain_last, pool_inverse] + [zero] * 5, axis=0)
 
     pool_rows.leave(share_of)
@@ -499,6 +520,7 @@
             pltpu.VMEM((pixels, width), F32),
             pltpu.VMEM((pixels, width), F32),
             pltpu.VMEM((pixels, width), BF16),
+            pltpu.VMEM((pixels, width), F32),
             pltpu.VMEM((images, channels), F32),
             pltpu.VMEM((4, cols, 8, width), F32),
             pltpu.VMEM((4, rows, 8, width), F32),
@@ -577,7 +599,7 @@
         for copy in weight_copies(n):
             copy.start()
 
-    greet_all(rows, cols, r, c)
+    greet(rows, cols, r, c)
 
     def has_rim(dev_y):
         return (dev_y == 1) & (z >= 1) | (dev_y == 0) & (z <= levels - 2)
@@ -912,15 +934,20 @@
     def feature_grad(m, lines):
         for line in lines:
             n = 1 + (m - 1) * 3 + line
-            for place, (_, tap) in enumerate(groups[n]):
-                i, j = tap // 3, tap % 3
-                shift = (j - 1) * m
+            first, step = groups[n][0][1], groups[n][1][1] - groups[n][0][1]
+
+            @pl.loop(0, len(groups[n]))
+            def _(place):
+                tap = first + step * place
+                shift = (lax.rem(tap, 3) - 1) * m
                 for a in range(blocks):
                     block = c * blocks + a
                     source = lax.rem(block - shift + across, across)
-                    gown[a * rb : (a + 1) * rb, place * width : (place + 1) * width] = masked(
-                        shifted[i, source, pl.ds(pl.multiple_of(y * rb, 16), rb)], colmask[REACH + shift, block]
+                    gown[a * rb : (a + 1) * rb, pl.ds(pl.multiple_of(place * width, width), width)] = masked(
+                        shifted[tap // 3, source, pl.ds(pl.multiple_of(y * rb, 16), rb)],
+                        colmask[REACH + shift, block],
                     )
+
             add_products(n, len(groups[n]) * width)
 
     for m in (1, 2, 3):

time: 266 us -> 263 us (0.989)
  Pallas kernels: 245 us -> 242 us
where the time goes in v5:
time: 263 us; the launch traced here: 262 us
  Pallas kernels  242 us (92%)
  local copies, waits for them, and re-layouts  9.58 us (4%)
  other arithmetic  9.42 us (4%)
    pallas_call x1, Pallas kernels, backward_call(): pl.pallas_call(functools.partial(backward_kernel, rows, cols, float(image...  142 us
    pallas_call x1, Pallas kernels, forward_call(): pl.pallas_call(functools.partial(forward_kernel, rows, cols, float(image_...  99.7 us
    reshape x1, other arithmetic, quick_shards(): atrous.astype(F32).reshape(3, 9, channels // rows, branch_width)  5.99 us

profile of v5, /device:TPU:0, one launch (start us, length us, event | category | flops | bytes accessed | tf_op | source)
XLA Modules:
  0.0 261.6 jit_solution(12122478955161087162)
XLA Ops:
  0.7 0.8 fusion
  1.5 0.1 copy.29
  1.6 0.2 copy.30
  1.8 0.7 pad.14.ids_ref
  2.5 0.8 fusion.1
  3.4 0.1 copy.26
  3.5 0.2 copy.31
  3.7 0.7 pad.13.ids_ref
  4.4 1.0 eq.15
  5.4 0.4 convert_reduce_fusion
  5.8 0.7 broadcast_in_dim.2.counts_ref
  6.5 99.7 %shard_map.170 = (bf16[576,256]{1,0:T(8,128)(2,1)}, bf16[4,4,144,256]{3,2,1,0:T(8,128)(2,1)}, bf16[1280,256]{1,0:T(8,128)(2,1)}, f32[16,256]{1,0:T(8,128)}, bf16...) custom-call(bf16[576,2048]{1,0:T(8,128)(2,1)} %bitcast.19, ...), custom_call_target="tpu_custom_call" | custom-call | flops 16911433728 | bytes 40000000 | tf_op jit(solution)/shard_map/pallas_call | solution.py:493
  106.3 142.2 %shard_map.171 = (bf16[576,2048]{1,0:T(8,128)(2,1)}, bf16[27,256,256]{2,1,0:T(8,128)(2,1)}, bf16[256,256]{1,0:T(8,128)(2,1)}, f32[256,256]{1,0:T(8,128)}, f32[8,256]{1,0:T(8,128)}, /*index=5*/f32[160,256]{1,0:T(8,128)}) custom-call(bf16[4,4,144,256]{3,2,1,0:T(8,128)(2,1)} %get-tuple-element.24.dz_ref, bf16[2,8,4,144,128]{4,3,2,1,0:T(8,128)(2,1)} %bitcast.21, ...), custom_call_target="tpu_custom_call" | custom-call | flops 33822867456 | bytes 50000000 | tf_op jit(solution)/shard_map/pallas_call | solution.py:1095
  248.4 0.8 fusion.4
  249.2 0.8 fusion.2
  250.0 0.8 fusion.3
  250.8 0.6 pad_maximum_fusion
  251.4 0.0 copy-start.4
  251.4 0.0 copy-start.1
  251.4 0.0 copy-start
  251.4 6.0 %convert.1 = f32[3,9,256,256]{3,2,1,0:T(8,128)} convert(bf16[3,9,256,256]{3,2,1,0:T(8,128)(2,1)} %bitcast.14) | non-fusion elementwise | flops 1769472 | bytes 10616832 | tf_op jit(solution)/shard_map/reshape | solution.py:1427
  257.4 0.0 copy-start.2
  257.4 0.0 copy-start.3
  257.4 0.0 copy-done.4
  257.4 0.7 convert_element_type.44
  258.1 0.0 copy-done.1
  258.1 0.7 copy.37
  258.8 0.0 copy-done
  258.8 1.4 copy.38
  260.2 0.0 copy-done.2
  260.2 0.7 copy.39
  260.9 0.0 copy-done.3
  260.9 0.7 copy.40
  (5 shorter events, 0.1 us)
Async XLA Ops:
  251.4 6.0 %copy-start.4 = (bf16[256,256]{1,0:T(8,128)(2,1)S(1)}, bf16[256,256]{1,0:T(8,128)(2,1)}, u32[]{:S(2)}) copy-start(bf16[256,256]{1,0:T(8,128)(2,1)} %get-tuple-element.33) | copy-start | bytes 393220
  251.4 6.7 %copy-start.1 = (bf16[576,256]{1,0:T(8,128)(2,1)S(1)}, bf16[576,256]{1,0:T(8,128)(2,1)}, u32[]{:S(2)}) copy-start(bf16[576,256]{1,0:T(8,128)(2,1)} %get-tuple-element.23) | copy-start | bytes 884740
  251.4 7.4 %copy-start = (bf16[576,2048]{1,0:T(8,128)(2,1)S(1)}, bf16[576,2048]{1,0:T(8,128)(2,1)}, u32[]{:S(2)}) copy-start(bf16[576,2048]{1,0:T(8,128)(2,1)} %get-tuple-element.32) | copy-start | bytes 7077892
  257.4 2.9 %copy-start.2 = (f32[256,256]{1,0:T(8,128)S(1)}, f32[256,256]{1,0:T(8,128)}, u32[]{:S(2)}) copy-start(f32[256,256]{1,0:T(8,128)} %get-tuple-element.58) | copy-start | bytes 786436
  257.4 3.6 %copy-start.3 = (f32[160,256]{1,0:T(8,128)S(1)}, f32[160,256]{1,0:T(8,128)}, u32[]{:S(2)}) copy-start(f32[160,256]{1,0:T(8,128)} %get-tuple-element.59) | copy-start | bytes 491524

commit v6 on v5

--- a/solution.py
+++ b/solution.py
@@ -363,7 +363,7 @@
         firsts.append(first)
         seconds.append(second)
     moments = all_sum(0, jnp.concatenate(firsts + seconds, axis=0))
-    send_members((2, 4), (1,))
+    send_members((6, 7), (1,))
     average = moments[0:4] / total_pixels
     inverse = lax.rsqrt(moments[4:8] / total_pixels - average * average + epsilon)
     for k in range(4):
@@ -385,7 +385,6 @@
         upstream[...] = jnp.dot(order_ref[...], cot_ref[...], preferred_element_type=F32)
 
     moments = all_sum(1, jnp.concatenate([first, second] + [zero] * 6, axis=0), (None, put_upstream))
-    send_members((3, 5), (1,))
     final_avg = moments[0:1] / total_pixels
     final_inverse = lax.rsqrt(moments[1:2] / total_pixels - final_avg * final_avg + epsilon)
     shift_last, gain_last = zero, zero
@@ -403,7 +402,7 @@
         out_ref[...] = jnp.dot(back_ref[...], active[...], preferred_element_type=F32).astype(BF16)
 
     sums = all_sum(2, jnp.concatenate([shift_last, gain_last] + [zero] * 6, axis=0), (None, put_output))
-    send_members((6, 7), (1,))
+    send_members((2, 4, 3, 5), (1,))
     shift_last, gain_last = sums[0:1], sums[1:2]
     gain = gain_ref[5:6]
     for a in range(blocks):

time: 263 us -> 264 us (level)
  no operation moved by 1% of the time
where the time goes in v6:
time: 264 us; the launch traced here: 263 us
  Pallas kernels  243 us (92%)
  local copies, waits for them, and re-layouts  9.58 us (4%)
  other arithmetic  9.42 us (4%)
    pallas_call x1, Pallas kernels, backward_call(): pl.pallas_call(functools.partial(backward_kernel, rows, cols, float(image...  142 us
    pallas_call x1, Pallas kernels, forward_call(): pl.pallas_call(functools.partial(forward_kernel, rows, cols, float(image_...  101 us
    reshape x1, other arithmetic, quick_shards(): atrous.astype(F32).reshape(3, 9, channels // rows, branch_width)  5.99 us

profile of v6, /device:TPU:0, one launch (start us, length us, event | category | flops | bytes accessed | tf_op | source)
XLA Modules:
  0.0 263.1 jit_solution(13719811251663532885)
XLA Ops:
  0.7 0.8 fusion
  1.5 0.1 copy.29
  1.6 0.2 copy.30
  1.8 0.7 pad.14.ids_ref
  2.5 0.8 fusion.1
  3.4 0.1 copy.26
  3.5 0.2 copy.31
  3.7 0.7 pad.13.ids_ref
  4.4 1.0 eq.15
  5.4 0.4 convert_reduce_fusion
  5.8 0.7 broadcast_in_dim.2.counts_ref
  6.5 101.3 %shard_map.170 = (bf16[576,256]{1,0:T(8,128)(2,1)}, bf16[4,4,144,256]{3,2,1,0:T(8,128)(2,1)}, bf16[1280,256]{1,0:T(8,128)(2,1)}, f32[16,256]{1,0:T(8,128)}, bf16...) custom-call(bf16[576,2048]{1,0:T(8,128)(2,1)} %bitcast.19, ...), custom_call_target="tpu_custom_call" | custom-call | flops 16911433728 | bytes 40000000 | tf_op jit(solution)/shard_map/pallas_call | solution.py:492
  107.9 142.0 %shard_map.171 = (bf16[576,2048]{1,0:T(8,128)(2,1)}, bf16[27,256,256]{2,1,0:T(8,128)(2,1)}, bf16[256,256]{1,0:T(8,128)(2,1)}, f32[256,256]{1,0:T(8,128)}, f32[8,256]{1,0:T(8,128)}, /*index=5*/f32[160,256]{1,0:T(8,128)}) custom-call(bf16[4,4,144,256]{3,2,1,0:T(8,128)(2,1)} %get-tuple-element.24.dz_ref, bf16[2,8,4,144,128]{4,3,2,1,0:T(8,128)(2,1)} %bitcast.21, ...), custom_call_target="tpu_custom_call" | custom-call | flops 33822867456 | bytes 50000000 | tf_op jit(solution)/shard_map/pallas_call | solution.py:1094
  249.9 0.8 fusion.4
  250.7 0.8 fusion.2
  251.5 0.8 fusion.3
  252.2 0.6 pad_maximum_fusion
  252.9 0.0 copy-start.4
  252.9 0.0 copy-start.1
  252.9 0.0 copy-start
  252.9 6.0 %convert.1 = f32[3,9,256,256]{3,2,1,0:T(8,128)} convert(bf16[3,9,256,256]{3,2,1,0:T(8,128)(2,1)} %bitcast.14) | non-fusion elementwise | flops 1769472 | bytes 10616832 | tf_op jit(solution)/shard_map/reshape | solution.py:1426
  258.9 0.0 copy-start.2
  258.9 0.0 copy-start.3
  258.9 0.0 copy-done.4
  258.9 0.7 convert_element_type.44
  259.6 0.0 copy-done.1
  259.6 0.7 copy.37
  260.3 0.0 copy-done
  260.3 1.4 copy.38
  261.7 0.0 copy-done.2
  261.7 0.7 copy.39
  262.4 0.0 copy-done.3
  262.4 0.7 copy.40
  (5 shorter events, 0.1 us)
Async XLA Ops:
  252.9 6.0 %copy-start.4 = (bf16[256,256]{1,0:T(8,128)(2,1)S(1)}, bf16[256,256]{1,0:T(8,128)(2,1)}, u32[]{:S(2)}) copy-start(bf16[256,256]{1,0:T(8,128)(2,1)} %get-tuple-element.33) | copy-start | bytes 393220
  252.9 6.7 %copy-start.1 = (bf16[576,256]{1,0:T(8,128)(2,1)S(1)}, bf16[576,256]{1,0:T(8,128)(2,1)}, u32[]{:S(2)}) copy-start(bf16[576,256]{1,0:T(8,128)(2,1)} %get-tuple-element.23) | copy-start | bytes 884740
  252.9 7.4 %copy-start = (bf16[576,2048]{1,0:T(8,128)(2,1)S(1)}, bf16[576,2048]{1,0:T(8,128)(2,1)}, u32[]{:S(2)}) copy-start(bf16[576,2048]{1,0:T(8,128)(2,1)} %get-tuple-element.32) | copy-start | bytes 7077892
  258.9 2.9 %copy-start.2 = (f32[256,256]{1,0:T(8,128)S(1)}, f32[256,256]{1,0:T(8,128)}, u32[]{:S(2)}) copy-start(f32[256,256]{1,0:T(8,128)} %get-tuple-element.58) | copy-start | bytes 786436
  258.9 3.6 %copy-start.3 = (f32[160,256]{1,0:T(8,128)S(1)}, f32[160,256]{1,0:T(8,128)}, u32[]{:S(2)}) copy-start(f32[160,256]{1,0:T(8,128)} %get-tuple-element.59) | copy-start | bytes 491524
